TPU v7x, 512 devices: a whole 4x8x8 slice. The times are simulated.
512 devices in a mesh: dp: 32 (over x_hi, y, core), eigen: 16 (over x_lo, z).
Axes of the slice: x: 4 (x_hi: 2, x_lo: 2; x = x_hi * 2 + x_lo), y: 8, z: 8, core: 2. Of those that a mesh axis runs over, the one named last changes fastest.
Arguments:
- inputs: bfloat16 [128, 512, 8192], P('dp', None, 'eigen'), may hold values from -6 to 6
- output_gradients: bfloat16 [128, 512, 8192], P('dp', None, 'eigen'), may hold values from -0.5745243 to 0.5745243
- adapter_down_factor: bfloat16 [64, 8192], P(None, 'eigen'), may hold values from -0.0625 to 0.0625
- output_eigen_basis: bfloat16 [8192, 8192], P('dp', 'eigen'), may hold values from -0.0625 to 0.0625
- adapter_eigen_basis: bfloat16 [64, 64], replicated, may hold values from -0.75 to 0.75
Outputs:
- corrected: float32 [64, 8192], P(None, 'eigen')
All inputs are finite; a program needn't handle non-finite values.
Results may differ from a plain program's by a relative error of at most 0.0019.
Values may be sent and summed in bfloat16 or wider, within the bound.
No kernel may reach another device: no remote copies, remote signals or barrier semaphores. Data moves between devices by JAX's collectives and lax.ppermute only.
A program may use at most 64 MiB of HBM per device.

v0:
```python
import jax
import jax.numpy as jnp
from jax import lax
from jax.sharding import PartitionSpec as P


def rotate_adapter(corrected_eigenvalues, rotation_matrix):
    return jnp.dot(
        rotation_matrix.T,
        corrected_eigenvalues.astype(jnp.bfloat16),
        preferred_element_type=jnp.float32,
    ).astype(jnp.bfloat16)


def shards(inputs, output_gradients, adapter_down_factor, output_eigen_basis, adapter_eigen_basis):
    sample_count, token_total, feature_width = inputs.shape
    adapter_rank = adapter_down_factor.shape[0]
    partial_projected = jnp.einsum(
        "is,ajs->iaj", adapter_down_factor, inputs, preferred_element_type=jnp.float32
    )
    partial_projected = partial_projected.reshape(adapter_rank, sample_count * token_total)
    summed_entries = lax.psum(partial_projected, "eigen")
    rotated_gradients = rotate_adapter(summed_entries, adapter_eigen_basis)
    rotated_gradients = rotated_gradients.reshape(adapter_rank, sample_count, token_total)
    weight_gradients = jnp.einsum(
        "ntf,rnt->fnr", output_gradients, rotated_gradients, preferred_element_type=jnp.float32
    )
    weight_gradients = weight_gradients.reshape(feature_width, sample_count * adapter_rank).astype(
        jnp.bfloat16
    )
    eigen_direction_count = output_eigen_basis.shape[1]
    all_grads = lax.all_gather(weight_gradients, "eigen", axis=0, tiled=True)
    coefficient_values = lax.dot_general(
        all_grads,
        lax.all_gather(output_eigen_basis, "dp", axis=0, tiled=True),
        (((0,), (0,)), ((), ())),
        preferred_element_type=jnp.float32,
    )
    squared_entries = jnp.sum(
        (coefficient_values * coefficient_values).reshape(
            sample_count, adapter_rank, eigen_direction_count
        ),
        axis=0,
    )
    summed_squares = lax.psum(squared_entries, "dp")
    return summed_squares / (sample_count * lax.axis_size("dp"))


def solution(mesh):
    return jax.shard_map(
        shards,
        mesh=mesh,
        in_specs=(
            P("dp", None, "eigen"),
            P("dp", None, "eigen"),
            P(None, "eigen"),
            P("dp", "eigen"),
            P(),
        ),
        out_specs=P(None, "eigen"),
        check_vma=False,
    )
```

profile of v0, /device:TPU:1, one launch (start us, length us, event | category | flops | bytes accessed | tf_op | source)
XLA Modules:
  0.0 533.2 jit_solution(18319266017086847220)
XLA Ops:
  6.5 0.0 copy-start
  6.5 0.0 copy-start.1
  6.5 0.0 all-gather.3.cloned.1.call-start
  6.5 1.6 copy-done
  8.1 1.6 convolution_bitcast_fusion
  9.8 62.3 %all-reduce.4 = bf16[64,2048]{1,0:T(8,128)(2,1)S(1)} all-reduce(f32[64,2048]{1,0:T(8,128)S(1)} %bitcast.21), channel_id=1, replica_groups=mesh['dp'=32,'eigen'=16] {'eigen'}, use_global_device_ids=true, to_apply=%region_0.0 | all-reduce | flops 131072 | bytes 786432 | tf_op jit(solution)/shard_map/psum | solution.py:22
  72.1 0.0 copy-done.1
  72.1 0.3 convolution_convert_fusion
  72.4 2.8 convolution_convert_fusion.1
  75.1 0.0 all-gather.3.cloned.1.call-update
  75.2 0.0 all-gather.5.cloned.1.call-start
  75.2 0.7 all-gather.5.cloned.1.call-update
  75.9 0.0 all-reduce.3.cloned.1.call-start
  76.0 79.7 %all-gather.3.cloned.1.call-done = bf16[8192,256]{0,1:T(8,128)(2,1)} async-done(((bf16[512,256]{0,1:T(8,128)(2,1)}), bf16[8192,256]{0,1:T(8,128)(2,1)}) %all-gather.3.cloned.1.call-update) | async-done | bytes 4194320 | tf_op jit(solution)/shard_map/all_gather | solution.py:32
  155.7 117.6 %all-gather.5.cloned.1.call-done = bf16[8192,512]{1,0:T(8,128)(2,1)} async-done(((bf16[256,512]{1,0:T(8,128)(2,1)}), bf16[8192,512]{1,0:T(8,128)(2,1)}) %all-gather.5.cloned.1.call-update) | async-done | bytes 8388624 | tf_op jit(solution)/shard_map/all_gather | solution.py:35
  273.3 7.0 %convolution_multiply_fusion = f32[256,512]{1,0:T(8,128)S(1)} fusion(bf16[8192,256]{0,1:T(8,128)(2,1)} %all-gather.3.cloned.1.call-done, bf16[8192,512]{1,0:T(8,128)(2,1)} %all-gather.5.cloned.1.call-done), kind=kOutput, calls=%fused_computation.1 | convolution fusion | flops 2147614720 | bytes 13107200 | tf_op jit(solution)/shard_map/dot_general | solution.py:33
  280.2 0.7 reduce_sum.9
  280.9 0.0 all-reduce.3.cloned.1.call-update
  281.0 244.1 %all-reduce.3.cloned.1.call-done = f32[64,512]{1,0:T(8,128)} async-done(((f32[64,512]{1,0:T(8,128)}), f32[64,512]{1,0:T(8,128)}) %all-reduce.3.cloned.1.call-update) | async-done | bytes 131088 | tf_op jit(solution)/shard_map/psum | solution.py:45
  525.1 1.6 broadcast_multiply_fusion
  (1 shorter events, 0.0 us)
Async XLA Ops:
  6.5 1.6 copy-start
  6.5 65.6 %copy-start.1 = (bf16[64,64]{1,0:T(8,128)(2,1)S(1)}, bf16[64,64]{1,0:T(8,128)(2,1)}, u32[]{:S(2)}) copy-start(bf16[64,64]{1,0:T(8,128)(2,1)} %param.9) | copy-start | bytes 24580
  6.5 149.2 %all-gather.3.cloned.1.call-start = ((), (), s32[]{:S(2)}) async-start(), calls=%async_computation | async-start | bytes 4456448 | tf_op jit(solution)/shard_map/all_gather | solution.py:32
  75.2 198.1 %all-gather.5.cloned.1.call-start = ((), (), s32[]{:S(2)}) async-start(), calls=%async_computation.1 | async-start | bytes 8650752 | tf_op jit(solution)/shard_map/all_gather | solution.py:35
  75.9 449.2 %all-reduce.3.cloned.1.call-start = ((), (), s32[]{:S(2)}) async-start(), calls=%async_computation.2 | async-start | bytes 262144 | tf_op jit(solution)/shard_map/psum | solution.py:45
Sparse Core Ops, SparseCore 0:
  75.3 80.3 all-gather.2
  159.1 114.1 all-gather.4
  281.1 243.9 all-reduce.2
where the time goes:
time: 534 us; the launch traced here: 533 us
  waiting for transfers between devices  442 us (83%)
  blocking collectives  62.3 us (12%)
  between operations  13.1 us (2%)
  matrix products  11.6 us (2%)
    psum x1, waiting for transfers between devices, shards(): summed_squares = lax.psum(squared_entries, 'dp')  244 us
    all_gather x1, waiting for transfers between devices, shards(): lax.all_gather(output_eigen_basis, 'dp', axis=0, tiled=True)  118 us
    all_gather x1, waiting for transfers between devices, shards(): all_grads = lax.all_gather(weight_gradients, 'eigen', axis=0, tiled=True)  79.7 us
    psum x1, blocking collectives, shards(): summed_entries = lax.psum(partial_projected, 'eigen')  62.3 us
  transfers between devices with their start and end apart: 3, of which 3 were waited for; matrix products, arithmetic and copies ran while one was open for 0% of the time, Pallas kernels for 0%

commit v1 on v0

v1 whole, which is shorter than its diff:
```python
import functools

import jax
import jax.numpy as jnp
from jax import lax
from jax.experimental import pallas as pl
from jax.experimental.pallas import tpu as pltpu
from jax.sharding import Mesh, PartitionSpec as P

DP = ("x_hi", "y", "core")
EIGEN = ("x_lo", "z")
SIZES = (2, 8, 2, 2, 8)
F32, BF16 = jnp.float32, jnp.bfloat16
VMEM_LIMIT = 48 * 1024 * 1024


def params(**kw):
    return pltpu.CompilerParams(vmem_limit_bytes=VMEM_LIMIT, **kw)


def project_kernel(a_ref, x_ref, o_ref):
    got = lax.dot_general(
        a_ref[...], x_ref[0], (((1,), (1,)), ((), ())), preferred_element_type=F32
    )
    for c in range(o_ref.shape[0]):
        o_ref[c] = got[:, c * 128 : (c + 1) * 128]


def project(inputs, down):
    count, tokens, width = inputs.shape
    rank = down.shape[0]
    per = tokens // 128
    return pl.pallas_call(
        project_kernel,
        grid=(count,),
        in_specs=[
            pl.BlockSpec((rank, width), lambda n: (0, 0)),
            pl.BlockSpec((1, tokens, width), lambda n: (n, 0, 0)),
        ],
        out_specs=pl.BlockSpec((per, rank, 128), lambda n: (n, 0, 0)),
        out_shape=jax.ShapeDtypeStruct((count * per, rank, 128), F32),
        compiler_params=params(),
        cost_estimate=pl.CostEstimate(
            flops=2 * count * tokens * width * rank, bytes_accessed=3 << 20, transcendentals=0
        ),
    )(down, inputs)


def rotate_kernel(p_ref, e_ref, o_ref):
    total = jnp.sum(p_ref[...], axis=0).astype(BF16)
    rot = lax.dot_general(
        e_ref[...], total, (((0,), (0,)), ((), ())), preferred_element_type=F32
    ).astype(BF16)
    for c in range(o_ref.shape[0]):
        o_ref[c] = rot


def rotate(parts, basis):
    return pl.pallas_call(
        rotate_kernel,
        out_shape=jax.ShapeDtypeStruct(parts.shape, BF16),
        compiler_params=params(),
    )(parts, basis)


def grad_kernel(ids_ref, rot_ref, dy_ref, keep_ref, send_ref):
    rot = jnp.concatenate([rot_ref[c] for c in range(rot_ref.shape[0])], axis=1)
    grad = jnp.dot(rot, dy_ref[0], preferred_element_type=F32).astype(BF16)
    half = grad.shape[1] // 2
    low, high = grad[:, :half], grad[:, half:]
    first = ids_ref[1] == 0
    keep_ref[...] = jnp.where(first, low, high)
    send_ref[...] = jnp.where(first, high, low)


def gradients(ids, rot, dy):
    count, tokens, width = dy.shape
    rank = rot.shape[1]
    per = tokens // 128
    out = jax.ShapeDtypeStruct((count * rank, width // 2), BF16)
    return pl.pallas_call(
        grad_kernel,
        grid_spec=pltpu.PrefetchScalarGridSpec(
            num_scalar_prefetch=1,
            grid=(count,),
            in_specs=[
                pl.BlockSpec((per, rank, 128), lambda n, ids: (n, 0, 0)),
                pl.BlockSpec((1, tokens, width), lambda n, ids: (n, 0, 0)),
            ],
            out_specs=[
                pl.BlockSpec((rank, width // 2), lambda n, ids: (n, 0)),
                pl.BlockSpec((rank, width // 2), lambda n, ids: (n, 0)),
            ],
        ),
        out_shape=[out, out],
        compiler_params=params(),
        cost_estimate=pl.CostEstimate(
            flops=2 * count * tokens * width * rank, bytes_accessed=3 << 20, transcendentals=0
        ),
    )(ids, rot, dy)


def coef_kernel(offsets, ids_ref, q_ref, *refs):
    pieces, (away_ref, keep_ref) = refs[:-2], refs[-2:]
    z, core = ids_ref[0], ids_ref[1]
    own = pl.ds(pl.multiple_of(core * 256, 256), 256)
    other = pl.ds(pl.multiple_of((1 - core) * 256, 256), 256)
    blocks = [lax.rem(z + off + 8, 8) for off in offsets]
    for rows, h in ((own, 0), (other, 1)):
        for cols, out in ((other, away_ref), (own, keep_ref)):
            total = None
            for piece, b in zip(pieces, blocks):
                term = jnp.dot(piece[h], q_ref[b, 0, :, cols], preferred_element_type=F32)
                total = term if total is None else total + term
            out[rows, :] = total


def coefficients(ids, which, basis, pieces, offsets):
    out = jax.ShapeDtypeStruct((512, 256), F32)
    whole = pl.BlockSpec((2, 256, 256), lambda i, ids: (0, 0, 0))
    return pl.pallas_call(
        functools.partial(coef_kernel, offsets),
        grid_spec=pltpu.PrefetchScalarGridSpec(
            num_scalar_prefetch=1,
            grid=(1,),
            in_specs=[pl.BlockSpec((8, 1, 256, 512), lambda i, ids: (0, ids[which], 0, 0))]
            + [whole] * len(pieces),
            out_specs=[pl.BlockSpec((512, 256), lambda i, ids: (0, 0))] * 2,
        ),
        out_shape=[out, out],
        compiler_params=params(),
        cost_estimate=pl.CostEstimate(flops=1 << 30, bytes_accessed=5 << 20, transcendentals=0),
    )(ids, basis, *pieces)


def square_kernel(a_ref, b_ref, c_ref, o_ref):
    coef = (a_ref[...] + b_ref[...]) + c_ref[...]
    sq = coef * coef
    rank = o_ref.shape[0]
    total = sq[:rank]
    for n in range(1, sq.shape[0] // rank):
        total = total + sq[n * rank : (n + 1) * rank]
    o_ref[...] = total


def swap(x, axis, stride=1):
    size = dict(zip(DP + EIGEN, SIZES))[axis]
    return lax.ppermute(x, axis, [(i, i ^ stride) for i in range(size)])


def shift(x, step):
    return lax.ppermute(x, "z", [(i, (i + step) % 8) for i in range(8)])


def shards(inputs, out_grads, down, out_basis, adapter_basis):
    z, core = lax.axis_index("z"), lax.axis_index("core")
    x_hi, x_lo = lax.axis_index("x_hi"), lax.axis_index("x_lo")
    mine = lax.bitwise_xor(x_hi, x_lo)
    ids = jnp.stack([z, core, mine, 1 - mine]).astype(jnp.int32)

    basis_a = lax.ppermute(out_basis, ("x_hi", "x_lo"), [(0, 0), (1, 2), (2, 1), (3, 3)])
    basis_b = lax.ppermute(out_basis, ("x_hi", "x_lo"), [(1, 0), (0, 2), (3, 1), (2, 3)])
    basis = lax.all_gather(jnp.stack([basis_a, basis_b]), "y", axis=0)

    parts = project(inputs, down)
    parts = lax.all_to_all(parts, EIGEN, 0, 0)
    rot = lax.all_to_all(rotate(parts, adapter_basis), EIGEN, 0, 0)

    keep, send = gradients(ids, rot, out_grads)
    piece = jnp.stack([keep, swap(send, "core")])
    pieces, offsets = [piece], [0]
    up = down_ = piece
    for s in range(1, 5):
        up = shift(up, 1)
        pieces.append(up)
        offsets.append(-s)
        if s < 4:
            down_ = shift(down_, -1)
            pieces.append(down_)
            offsets.append(s)

    away, keep = coefficients(ids, 3, basis, pieces, offsets)
    theirs = swap(keep + swap(away, "core"), "x_lo")
    away, keep = coefficients(ids, 2, basis, pieces, offsets)
    ours = swap(away, "core")
    total = pl.pallas_call(
        square_kernel,
        out_shape=jax.ShapeDtypeStruct((64, 256), F32),
        compiler_params=params(),
    )(keep, ours, theirs)

    total = total + swap(total, "x_hi")
    for stride in (1, 2, 4):
        total = total + swap(total, "y", stride)
    total = total * (1.0 / 128)
    other = swap(total, "core")
    first = core == 0
    return jnp.concatenate(
        [jnp.where(first, total, other), jnp.where(first, other, total)], axis=1
    )


def solution(mesh):
    fine = Mesh(mesh.devices.reshape(SIZES), DP + EIGEN)
    return jax.shard_map(
        shards,
        mesh=fine,
        in_specs=(
            P(DP, None, EIGEN),
            P(DP, None, EIGEN),
            P(None, EIGEN),
            P(DP, EIGEN),
            P(),
        ),
        out_specs=P(None, EIGEN),
        check_vma=False,
    )
```

time: 534 us -> 184 us (0.34)
  waiting for transfers between devices: 442 us -> 49 us
  starting transfers between devices: 0.08 us -> 78.9 us
  blocking collectives: 62.3 us -> 26.8 us
  matrix products: 11.6 us -> 0 us
  Pallas kernels: 0 us -> 10.3 us
    psum x1 -> x0, waiting for transfers between devices: 244 us -> none  [shards(): summed_squares = lax.psum(squared_entries, 'dp')]
    all_gather x2 -> x1, waiting for transfers between devices: 197 us -> 0.01 us  [shards(): basis = lax.all_gather(jnp.stack([basis_a, basis_b]), 'y', axis=0)]
    ppermute x0 -> x18, starting transfers between devices: none -> 72.3 us  [the longest x9 43.3 us: swap(): return lax.ppermute(x, axis, [(i, i ^ stride) for i in range(size)])]
    psum x1 -> x0, blocking collectives: 62.3 us -> none  [shards(): summed_entries = lax.psum(partial_projected, 'eigen')]
    ppermute x0 -> x18, waiting for transfers between devices: none -> 41.3 us  [the longest x9 21.4 us: swap(): return lax.ppermute(x, axis, [(i, i ^ stride) for i in range(size)])]
    all_to_all x0 -> x1, blocking collectives: none -> 26.8 us  [shards(): parts = lax.all_to_all(parts, EIGEN, 0, 0)]
    dot_general x4 -> x0, matrix products: 11.6 us -> none  [the longest x1 6.98 us: shards(): lax.dot_general(all_grads, lax.all_gather(output_eigen_basis, 'dp', axis=...]
    pallas_call x0 -> x6, Pallas kernels: none -> 10.3 us  [the longest x2 6.76 us: coefficients(): pl.pallas_call(functools.partial(coef_kernel, offsets), grid_spec=pltpu.P...]
  transfers between devices with their start and end apart: 3 -> 20, of which waited for: 3 -> 13; matrix products, arithmetic and copies ran while one was open for 0% -> 0% of each run, Pallas kernels for 0% -> 4%
where the time goes in v1:
time: 184 us; the launch traced here: 183 us
  starting transfers between devices  78.9 us (43%)
  waiting for transfers between devices  49 us (27%)
  blocking collectives  26.8 us (15%)
  between operations  13.7 us (7%)
  Pallas kernels  10.3 us (6%)
  local copies, waits for them, and re-layouts  2.43 us (1%)
    ppermute x9, starting transfers between devices, swap(): return lax.ppermute(x, axis, [(i, i ^ stride) for i in range(size)])  43.3 us
    all_to_all x1, blocking collectives, shards(): parts = lax.all_to_all(parts, EIGEN, 0, 0)  26.8 us
    ppermute x7, starting transfers between devices, shift(): return lax.ppermute(x, 'z', [(i, (i + step) % 8) for i in range(8)])  21.4 us
    ppermute x9, waiting for transfers between devices, swap(): return lax.ppermute(x, axis, [(i, i ^ stride) for i in range(size)])  21.4 us
    ppermute x7, waiting for transfers between devices, shift(): return lax.ppermute(x, 'z', [(i, (i + step) % 8) for i in range(8)])  16.3 us
    all_to_all x1, waiting for transfers between devices, shards(): rot = lax.all_to_all(rotate(parts, adapter_basis), EIGEN, 0, 0)  7.67 us
    pallas_call x2, Pallas kernels, coefficients(): pl.pallas_call(functools.partial(coef_kernel, offsets), grid_spec=pltpu.P...  6.76 us
    all_to_all x1, starting transfers between devices, shards(): rot = lax.all_to_all(rotate(parts, adapter_basis), EIGEN, 0, 0)  6.59 us
  transfers between devices with their start and end apart: 20, of which 13 were waited for; matrix products, arithmetic and copies ran while one was open for 0% of the time, Pallas kernels for 4%

profile of v1, /device:TPU:1, one launch (start us, length us, event | category | flops | bytes accessed | tf_op | source)
XLA Modules:
  0.0 182.9 jit_solution(3411890023519664463)
XLA Ops:
  8.1 6.0 %collective-permute-start.1 = (bf16[256,512]{1,0:T(8,128)(2,1)}, bf16[256,512]{1,0:T(8,128)(2,1)S(1)}, u32[]{:S(2)}, u32[]{:S(2)}) collective-permute-start(bf16[256,512]{1,0:T(8,128)(2,1)} %param.8), channel_id=1, source_target_pairs={{8,0},{0,256},{264,8},{256,264},{9,1},{1,257},{265,9},{257,265},{1... | collective-permute-start | bytes 786440 | tf_op jit(solution)/shard_map/ppermute | solution.py:162
  14.2 3.6 %collective-permute-done.1 = bf16[256,512]{1,0:T(8,128)(2,1)S(1)} collective-permute-done((bf16[256,512]{1,0:T(8,128)(2,1)}, bf16[256,512]{1,0:T(8,128)(2,1)S(1)}, u32[]{:S(2)}, u32[]{:S(2)}) %collective-permute-start.1) | collective-permute-done | bytes 262176 | tf_op jit(solution)/shard_map/ppermute | solution.py:162
  22.3 26.8 %all_to_all.10.p_ref = f32[16,64,128]{2,1,0:T(8,128)S(1)} all-to-all(f32[16,64,128]{2,1,0:T(8,128)S(1)} %shard_map.55), channel_id=1, replica_groups=mesh['x_hi'=2,'y'=8,'core'=2,'x_lo'=2,'z'=8] {'x_lo','z'}, dimensions={0} | all-to-all | bytes 1048576 | tf_op jit(solution)/shard_map/all_to_all | solution.py:166
  50.0 6.6 %all-to-all-start.1 = ((bf16[16,64,128]{2,1,0:T(8,128)(2,1)}), bf16[16,64,128]{2,1,0:T(8,128)(2,1)S(1)}, u32[]{:S(2)}, u32[]{:S(2)}) async-start(bf16[16,64,128]{2,1,0:T(8,128)(2,1)} %shard_map.56), calls=%async_computation.1 | async-start | bytes 524288 | tf_op jit(solution)/shard_map/all_to_all | solution.py:167
  56.7 7.7 %all-to-all-done.1.rot_ref = bf16[16,64,128]{2,1,0:T(8,128)(2,1)S(1)} async-done(((bf16[16,64,128]{2,1,0:T(8,128)(2,1)}), bf16[16,64,128]{2,1,0:T(8,128)(2,1)S(1)}, u32[]{:S(2)}, u32[]{:S(2)}) %all-to-all-start.1) | async-done | bytes 262176 | tf_op jit(solution)/shard_map/all_to_all | solution.py:167
  65.8 5.5 %collective-permute-start.2 = (bf16[256,256]{1,0:T(8,128)(2,1)S(1)}, bf16[256,256]{1,0:T(8,128)(2,1)S(1)}, u32[]{:S(2)}, u32[]{:S(2)}) collective-permute-start(bf16[256,256]{1,0:T(8,128)(2,1)S(1)} %get-tuple-element.12), channel_id=1, source_target_pairs={{0,16},{16,0},{1,17},{17,1},{2,18},{18,2},{3,19},{19,3},{4,20},{20... | collective-permute-start | bytes 393224 | tf_op jit(solution)/shard_map/ppermute | solution.py:148
  72.3 3.5 %collective-permute-start.3 = (bf16[2,256,256]{2,1,0:T(8,128)(2,1)S(1)}, bf16[2,256,256]{2,1,0:T(8,128)(2,1)S(1)}, u32[]{:S(2)}, u32[]{:S(2)}) collective-permute-start(bf16[2,256,256]{2,1,0:T(8,128)(2,1)S(1)} %pad_maximum_fusion.1.refs_0_), channel_id=1, source_target_pairs={{0,1},{1,2},{2,3},{3,4},{4,5},{5,6},{6,7},{7,0},{8,9},{9,10},{10,1... | collective-permute-start | bytes 786440 | tf_op jit(solution)/shard_map/ppermute | solution.py:152
  75.8 3.0 %collective-permute-start.4 = (bf16[2,256,256]{2,1,0:T(8,128)(2,1)S(1)}, bf16[2,256,256]{2,1,0:T(8,128)(2,1)S(1)}, u32[]{:S(2)}, u32[]{:S(2)}) collective-permute-start(bf16[2,256,256]{2,1,0:T(8,128)(2,1)S(1)} %pad_maximum_fusion.1.refs_0_), channel_id=1, source_target_pairs={{0,7},{1,0},{2,1},{3,2},{4,3},{5,4},{6,5},{7,6},{8,15},{9,8},{10,9... | collective-permute-start | bytes 786440 | tf_op jit(solution)/shard_map/ppermute | solution.py:152
  78.8 4.2 %collective-permute-done.3.refs_1_ = bf16[2,256,256]{2,1,0:T(8,128)(2,1)S(1)} collective-permute-done((bf16[2,256,256]{2,1,0:T(8,128)(2,1)S(1)}, bf16[2,256,256]{2,1,0:T(8,128)(2,1)S(1)}, u32[]{:S(2)}, u32[]{:S(2)}) %collective-permute-start.3) | collective-permute-done | bytes 262176 | tf_op jit(solution)/shard_map/ppermute | solution.py:152
  83.0 2.3 %collective-permute-start.5 = (bf16[2,256,256]{2,1,0:T(8,128)(2,1)S(1)}, bf16[2,256,256]{2,1,0:T(8,128)(2,1)S(1)}, u32[]{:S(2)}, u32[]{:S(2)}) collective-permute-start(bf16[2,256,256]{2,1,0:T(8,128)(2,1)S(1)} %collective-permute-done.3.refs_1_), channel_id=1, source_target_pairs={{0,1},{1,2},{2,3},{3,4},{4,5},{5,6},{6,7},{7,0},{8,9},{9,10},{10,1... | collective-permute-start | bytes 786440 | tf_op jit(solution)/shard_map/ppermute | solution.py:152
  85.3 4.2 %collective-permute-start.6 = (bf16[2,256,256]{2,1,0:T(8,128)(2,1)S(1)}, bf16[2,256,256]{2,1,0:T(8,128)(2,1)S(1)}, u32[]{:S(2)}, u32[]{:S(2)}) collective-permute-start(bf16[2,256,256]{2,1,0:T(8,128)(2,1)S(1)} %collective-permute-done.4.refs_2_), channel_id=1, source_target_pairs={{0,7},{1,0},{2,1},{3,2},{4,3},{5,4},{6,5},{7,6},{8,15},{9,8},{10,9... | collective-permute-start | bytes 786440 | tf_op jit(solution)/shard_map/ppermute | solution.py:152
  89.5 3.3 %collective-permute-done.5.refs_3_ = bf16[2,256,256]{2,1,0:T(8,128)(2,1)S(1)} collective-permute-done((bf16[2,256,256]{2,1,0:T(8,128)(2,1)S(1)}, bf16[2,256,256]{2,1,0:T(8,128)(2,1)S(1)}, u32[]{:S(2)}, u32[]{:S(2)}) %collective-permute-start.5) | collective-permute-done | bytes 262176 | tf_op jit(solution)/shard_map/ppermute | solution.py:152
  92.8 1.9 %collective-permute-start.7 = (bf16[2,256,256]{2,1,0:T(8,128)(2,1)S(1)}, bf16[2,256,256]{2,1,0:T(8,128)(2,1)S(1)}, u32[]{:S(2)}, u32[]{:S(2)}) collective-permute-start(bf16[2,256,256]{2,1,0:T(8,128)(2,1)S(1)} %collective-permute-done.5.refs_3_), channel_id=1, source_target_pairs={{0,1},{1,2},{2,3},{3,4},{4,5},{5,6},{6,7},{7,0},{8,9},{9,10},{10,1... | collective-permute-start | bytes 786440 | tf_op jit(solution)/shard_map/ppermute | solution.py:152
  94.7 4.6 %collective-permute-start.8 = (bf16[2,256,256]{2,1,0:T(8,128)(2,1)S(1)}, bf16[2,256,256]{2,1,0:T(8,128)(2,1)S(1)}, u32[]{:S(2)}, u32[]{:S(2)}) collective-permute-start(bf16[2,256,256]{2,1,0:T(8,128)(2,1)S(1)} %collective-permute-done.6.refs_4_), channel_id=1, source_target_pairs={{0,7},{1,0},{2,1},{3,2},{4,3},{5,4},{6,5},{7,6},{8,15},{9,8},{10,9... | collective-permute-start | bytes 786440 | tf_op jit(solution)/shard_map/ppermute | solution.py:152
  99.3 2.4 %collective-permute-done.7.refs_5_ = bf16[2,256,256]{2,1,0:T(8,128)(2,1)S(1)} collective-permute-done((bf16[2,256,256]{2,1,0:T(8,128)(2,1)S(1)}, bf16[2,256,256]{2,1,0:T(8,128)(2,1)S(1)}, u32[]{:S(2)}, u32[]{:S(2)}) %collective-permute-start.7) | collective-permute-done | bytes 262176 | tf_op jit(solution)/shard_map/ppermute | solution.py:152
  101.7 1.9 %collective-permute-start.9 = (bf16[2,256,256]{2,1,0:T(8,128)(2,1)S(1)}, bf16[2,256,256]{2,1,0:T(8,128)(2,1)S(1)}, u32[]{:S(2)}, u32[]{:S(2)}) collective-permute-start(bf16[2,256,256]{2,1,0:T(8,128)(2,1)S(1)} %collective-permute-done.7.refs_5_), channel_id=1, source_target_pairs={{0,1},{1,2},{2,3},{3,4},{4,5},{5,6},{6,7},{7,0},{8,9},{9,10},{10,1... | collective-permute-start | bytes 786440 | tf_op jit(solution)/shard_map/ppermute | solution.py:152
  103.6 6.4 %collective-permute-done.9.refs_7_ = bf16[2,256,256]{2,1,0:T(8,128)(2,1)S(1)} collective-permute-done((bf16[2,256,256]{2,1,0:T(8,128)(2,1)S(1)}, bf16[2,256,256]{2,1,0:T(8,128)(2,1)S(1)}, u32[]{:S(2)}, u32[]{:S(2)}) %collective-permute-start.9) | collective-permute-done | bytes 262176 | tf_op jit(solution)/shard_map/ppermute | solution.py:152
  110.0 3.4 %shard_map.59 = (f32[512,256]{1,0:T(8,128)S(1)}, f32[512,256]{1,0:T(8,128)S(1)}) custom-call(s32[4]{0:T(128)S(1)} %pad_add_fusion.ids_ref, bf16[8,2,256,512]{3,2,1,0:T(8,128)(2,1)} %bitcast.10, bf16[2,256,256]{2,1,0:T(8,128)(2,1)S(1)} %pad_maximum_fusion.1.refs_0_, bf16[2,256,256]{2,1,0:T(8,128)(2,1)S(1)} %collective-permute-done.3.refs_1_, ...), custom_call_target="tpu_custom_call" | custom-call | flops 1073741824 | bytes 5242880 | tf_op jit(solution)/shard_map/pallas_call | solution.py:121
  113.4 6.0 %collective-permute-start.11 = (f32[512,256]{1,0:T(8,128)S(1)}, f32[512,256]{1,0:T(8,128)S(1)}, u32[]{:S(2)}, u32[]{:S(2)}) collective-permute-start(f32[512,256]{1,0:T(8,128)S(1)} %get-tuple-element.16), channel_id=1, source_target_pairs={{0,16},{16,0},{1,17},{17,1},{2,18},{18,2},{3,19},{19,3},{4,20},{20... | collective-permute-start | bytes 1572872 | tf_op jit(solution)/shard_map/ppermute | solution.py:148
  119.4 3.4 %shard_map.58 = (f32[512,256]{1,0:T(8,128)S(1)}, f32[512,256]{1,0:T(8,128)S(1)}) custom-call(s32[4]{0:T(128)S(1)} %pad_add_fusion.ids_ref, bf16[8,2,256,512]{3,2,1,0:T(8,128)(2,1)} %bitcast.11, bf16[2,256,256]{2,1,0:T(8,128)(2,1)S(1)} %pad_maximum_fusion.1.refs_0_, bf16[2,256,256]{2,1,0:T(8,128)(2,1)S(1)} %collective-permute-done.3.refs_1_, ...), custom_call_target="tpu_custom_call" | custom-call | flops 1073741824 | bytes 5242880 | tf_op jit(solution)/shard_map/pallas_call | solution.py:121
  122.8 1.9 %collective-permute-start.10 = (f32[512,256]{1,0:T(8,128)S(1)}, f32[512,256]{1,0:T(8,128)S(1)}, u32[]{:S(2)}, u32[]{:S(2)}) collective-permute-start(f32[512,256]{1,0:T(8,128)S(1)} %get-tuple-element.14), channel_id=1, source_target_pairs={{0,16},{16,0},{1,17},{17,1},{2,18},{18,2},{3,19},{19,3},{4,20},{20... | collective-permute-start | bytes 1572872 | tf_op jit(solution)/shard_map/ppermute | solution.py:148
  124.8 2.8 %collective-permute-start.12 = (f32[512,256]{1,0:T(8,128)S(1)}, f32[512,256]{1,0:T(8,128)S(1)}, u32[]{:S(2)}, u32[]{:S(2)}) collective-permute-start(f32[512,256]{1,0:T(8,128)S(1)} %add.15), channel_id=1, source_target_pairs={{0,8},{8,0},{1,9},{9,1},{2,10},{10,2},{3,11},{11,3},{4,12},{12,4},... | collective-permute-start | bytes 1572872 | tf_op jit(solution)/shard_map/ppermute | solution.py:148
  127.7 12.0 %collective-permute-done.12.c_ref = f32[512,256]{1,0:T(8,128)S(1)} collective-permute-done((f32[512,256]{1,0:T(8,128)S(1)}, f32[512,256]{1,0:T(8,128)S(1)}, u32[]{:S(2)}, u32[]{:S(2)}) %collective-permute-start.12) | collective-permute-done | bytes 524320 | tf_op jit(solution)/shard_map/ppermute | solution.py:148
  139.8 4.8 %collective-permute-start.13 = (f32[64,256]{1,0:T(8,128)S(1)}, f32[64,256]{1,0:T(8,128)S(1)}, u32[]{:S(2)}, u32[]{:S(2)}) collective-permute-start(f32[64,256]{1,0:T(8,128)S(1)} %shard_map.60), channel_id=1, source_target_pairs={{0,256},{256,0},{1,257},{257,1},{2,258},{258,2},{3,259},{259,3},{4... | collective-permute-start | bytes 196616 | tf_op jit(solution)/shard_map/ppermute | solution.py:148
  144.6 1.7 collective-permute-done.13
  146.3 2.8 %collective-permute-start.14 = (f32[64,256]{1,0:T(8,128)S(1)}, f32[64,256]{1,0:T(8,128)S(1)}, u32[]{:S(2)}, u32[]{:S(2)}) collective-permute-start(f32[64,256]{1,0:T(8,128)S(1)} %add.16), channel_id=1, source_target_pairs={{0,32},{32,0},{64,96},{96,64},{128,160},{160,128},{192,224},{224,1... | collective-permute-start | bytes 196616 | tf_op jit(solution)/shard_map/ppermute | solution.py:148
  149.1 2.2 %collective-permute-done.14 = f32[64,256]{1,0:T(8,128)S(1)} collective-permute-done((f32[64,256]{1,0:T(8,128)S(1)}, f32[64,256]{1,0:T(8,128)S(1)}, u32[]{:S(2)}, u32[]{:S(2)}) %collective-permute-start.14) | collective-permute-done | bytes 65568 | tf_op jit(solution)/shard_map/ppermute | solution.py:148
  151.3 4.1 %collective-permute-start.15 = (f32[64,256]{1,0:T(8,128)S(1)}, f32[64,256]{1,0:T(8,128)S(1)}, u32[]{:S(2)}, u32[]{:S(2)}) collective-permute-start(f32[64,256]{1,0:T(8,128)S(1)} %add.17), channel_id=1, source_target_pairs={{0,64},{32,96},{64,0},{96,32},{128,192},{160,224},{192,128},{224,1... | collective-permute-start | bytes 196616 | tf_op jit(solution)/shard_map/ppermute | solution.py:148
  155.4 1.8 %collective-permute-done.15 = f32[64,256]{1,0:T(8,128)S(1)} collective-permute-done((f32[64,256]{1,0:T(8,128)S(1)}, f32[64,256]{1,0:T(8,128)S(1)}, u32[]{:S(2)}, u32[]{:S(2)}) %collective-permute-start.15) | collective-permute-done | bytes 65568 | tf_op jit(solution)/shard_map/ppermute | solution.py:148
  157.3 7.9 %collective-permute-start.16 = (f32[64,256]{1,0:T(8,128)S(1)}, f32[64,256]{1,0:T(8,128)S(1)}, u32[]{:S(2)}, u32[]{:S(2)}) collective-permute-start(f32[64,256]{1,0:T(8,128)S(1)} %add.18), channel_id=1, source_target_pairs={{0,128},{32,160},{64,192},{96,224},{128,0},{160,32},{192,64},{224,... | collective-permute-start | bytes 196616 | tf_op jit(solution)/shard_map/ppermute | solution.py:148
  165.1 1.7 collective-permute-done.16
  166.9 7.6 %collective-permute-start.17 = (f32[64,256]{1,0:T(8,128)S(1)}, f32[64,256]{1,0:T(8,128)S(1)}, u32[]{:S(2)}, u32[]{:S(2)}) collective-permute-start(f32[64,256]{1,0:T(8,128)S(1)} %add_multiply_fusion), channel_id=1, source_target_pairs={{0,16},{16,0},{1,17},{17,1},{2,18},{18,2},{3,19},{19,3},{4,20},{20... | collective-permute-start | bytes 196616 | tf_op jit(solution)/shard_map/ppermute | solution.py:148
  (34 shorter events, 11.2 us)
Async XLA Ops:
  6.5 103.5 %all-gather.3.cloned.1.call-start = ((), (), s32[]{:S(2)}) async-start(), calls=%async_computation.2 | async-start | bytes 4718592 | tf_op jit(solution)/shard_map/all_gather | solution.py:163
  6.5 7.7 %collective-permute-start = (bf16[256,512]{1,0:T(8,128)(2,1)}, bf16[256,512]{1,0:T(8,128)(2,1)S(1)}, u32[]{:S(2)}, u32[]{:S(2)}) collective-permute-start(bf16[256,512]{1,0:T(8,128)(2,1)} %param.8), channel_id=1, source_target_pairs={{0,0},{8,256},{256,8},{264,264},{1,1},{9,257},{257,9},{265,265},{2... | collective-permute-start | bytes 786440 | tf_op jit(solution)/shard_map/ppermute | solution.py:161
  8.1 9.7 %collective-permute-start.1 = (bf16[256,512]{1,0:T(8,128)(2,1)}, bf16[256,512]{1,0:T(8,128)(2,1)S(1)}, u32[]{:S(2)}, u32[]{:S(2)}) collective-permute-start(bf16[256,512]{1,0:T(8,128)(2,1)} %param.8), channel_id=1, source_target_pairs={{8,0},{0,256},{264,8},{256,264},{9,1},{1,257},{265,9},{257,265},{1... | collective-permute-start | bytes 786440 | tf_op jit(solution)/shard_map/ppermute | solution.py:162
  18.7 30.4 %copy-start.3 = (bf16[64,64]{1,0:T(8,128)(2,1)S(1)}, bf16[64,64]{1,0:T(8,128)(2,1)}, u32[]{:S(2)}) copy-start(bf16[64,64]{1,0:T(8,128)(2,1)} %e_ref.1) | copy-start | bytes 24580
  18.7 1.6 copy-start.1
  20.3 0.8 copy-start.2
  21.2 43.2 %copy-start = (bf16[4,512,512]{2,1,0:T(8,128)(2,1)S(1)}, bf16[4,512,512]{2,1,0:T(8,128)(2,1)}, u32[]{:S(2)}) copy-start(bf16[4,512,512]{2,1,0:T(8,128)(2,1)} %dy_ref.1) | copy-start | bytes 6291460
  50.0 14.4 %all-to-all-start.1 = ((bf16[16,64,128]{2,1,0:T(8,128)(2,1)}), bf16[16,64,128]{2,1,0:T(8,128)(2,1)S(1)}, u32[]{:S(2)}, u32[]{:S(2)}) async-start(bf16[16,64,128]{2,1,0:T(8,128)(2,1)} %shard_map.56), calls=%async_computation.1 | async-start | bytes 524288 | tf_op jit(solution)/shard_map/all_to_all | solution.py:167
  65.8 6.4 %collective-permute-start.2 = (bf16[256,256]{1,0:T(8,128)(2,1)S(1)}, bf16[256,256]{1,0:T(8,128)(2,1)S(1)}, u32[]{:S(2)}, u32[]{:S(2)}) collective-permute-start(bf16[256,256]{1,0:T(8,128)(2,1)S(1)} %get-tuple-element.12), channel_id=1, source_target_pairs={{0,16},{16,0},{1,17},{17,1},{2,18},{18,2},{3,19},{19,3},{4,20},{20... | collective-permute-start | bytes 393224 | tf_op jit(solution)/shard_map/ppermute | solution.py:148
  72.3 10.7 %collective-permute-start.3 = (bf16[2,256,256]{2,1,0:T(8,128)(2,1)S(1)}, bf16[2,256,256]{2,1,0:T(8,128)(2,1)S(1)}, u32[]{:S(2)}, u32[]{:S(2)}) collective-permute-start(bf16[2,256,256]{2,1,0:T(8,128)(2,1)S(1)} %pad_maximum_fusion.1.refs_0_), channel_id=1, source_target_pairs={{0,1},{1,2},{2,3},{3,4},{4,5},{5,6},{6,7},{7,0},{8,9},{9,10},{10,1... | collective-permute-start | bytes 786440 | tf_op jit(solution)/shard_map/ppermute | solution.py:152
  75.8 9.5 %collective-permute-start.4 = (bf16[2,256,256]{2,1,0:T(8,128)(2,1)S(1)}, bf16[2,256,256]{2,1,0:T(8,128)(2,1)S(1)}, u32[]{:S(2)}, u32[]{:S(2)}) collective-permute-start(bf16[2,256,256]{2,1,0:T(8,128)(2,1)S(1)} %pad_maximum_fusion.1.refs_0_), channel_id=1, source_target_pairs={{0,7},{1,0},{2,1},{3,2},{4,3},{5,4},{6,5},{7,6},{8,15},{9,8},{10,9... | collective-permute-start | bytes 786440 | tf_op jit(solution)/shard_map/ppermute | solution.py:152
  83.0 9.8 %collective-permute-start.5 = (bf16[2,256,256]{2,1,0:T(8,128)(2,1)S(1)}, bf16[2,256,256]{2,1,0:T(8,128)(2,1)S(1)}, u32[]{:S(2)}, u32[]{:S(2)}) collective-permute-start(bf16[2,256,256]{2,1,0:T(8,128)(2,1)S(1)} %collective-permute-done.3.refs_1_), channel_id=1, source_target_pairs={{0,1},{1,2},{2,3},{3,4},{4,5},{5,6},{6,7},{7,0},{8,9},{9,10},{10,1... | collective-permute-start | bytes 786440 | tf_op jit(solution)/shard_map/ppermute | solution.py:152
  85.3 9.4 %collective-permute-start.6 = (bf16[2,256,256]{2,1,0:T(8,128)(2,1)S(1)}, bf16[2,256,256]{2,1,0:T(8,128)(2,1)S(1)}, u32[]{:S(2)}, u32[]{:S(2)}) collective-permute-start(bf16[2,256,256]{2,1,0:T(8,128)(2,1)S(1)} %collective-permute-done.4.refs_2_), channel_id=1, source_target_pairs={{0,7},{1,0},{2,1},{3,2},{4,3},{5,4},{6,5},{7,6},{8,15},{9,8},{10,9... | collective-permute-start | bytes 786440 | tf_op jit(solution)/shard_map/ppermute | solution.py:152
  92.8 8.9 %collective-permute-start.7 = (bf16[2,256,256]{2,1,0:T(8,128)(2,1)S(1)}, bf16[2,256,256]{2,1,0:T(8,128)(2,1)S(1)}, u32[]{:S(2)}, u32[]{:S(2)}) collective-permute-start(bf16[2,256,256]{2,1,0:T(8,128)(2,1)S(1)} %collective-permute-done.5.refs_3_), channel_id=1, source_target_pairs={{0,1},{1,2},{2,3},{3,4},{4,5},{5,6},{6,7},{7,0},{8,9},{9,10},{10,1... | collective-permute-start | bytes 786440 | tf_op jit(solution)/shard_map/ppermute | solution.py:152
  94.7 8.9 %collective-permute-start.8 = (bf16[2,256,256]{2,1,0:T(8,128)(2,1)S(1)}, bf16[2,256,256]{2,1,0:T(8,128)(2,1)S(1)}, u32[]{:S(2)}, u32[]{:S(2)}) collective-permute-start(bf16[2,256,256]{2,1,0:T(8,128)(2,1)S(1)} %collective-permute-done.6.refs_4_), channel_id=1, source_target_pairs={{0,7},{1,0},{2,1},{3,2},{4,3},{5,4},{6,5},{7,6},{8,15},{9,8},{10,9... | collective-permute-start | bytes 786440 | tf_op jit(solution)/shard_map/ppermute | solution.py:152
  101.7 8.3 %collective-permute-start.9 = (bf16[2,256,256]{2,1,0:T(8,128)(2,1)S(1)}, bf16[2,256,256]{2,1,0:T(8,128)(2,1)S(1)}, u32[]{:S(2)}, u32[]{:S(2)}) collective-permute-start(bf16[2,256,256]{2,1,0:T(8,128)(2,1)S(1)} %collective-permute-done.7.refs_5_), channel_id=1, source_target_pairs={{0,1},{1,2},{2,3},{3,4},{4,5},{5,6},{6,7},{7,0},{8,9},{9,10},{10,1... | collective-permute-start | bytes 786440 | tf_op jit(solution)/shard_map/ppermute | solution.py:152
  113.4 11.3 %collective-permute-start.11 = (f32[512,256]{1,0:T(8,128)S(1)}, f32[512,256]{1,0:T(8,128)S(1)}, u32[]{:S(2)}, u32[]{:S(2)}) collective-permute-start(f32[512,256]{1,0:T(8,128)S(1)} %get-tuple-element.16), channel_id=1, source_target_pairs={{0,16},{16,0},{1,17},{17,1},{2,18},{18,2},{3,19},{19,3},{4,20},{20... | collective-permute-start | bytes 1572872 | tf_op jit(solution)/shard_map/ppermute | solution.py:148
  122.8 4.9 %collective-permute-start.10 = (f32[512,256]{1,0:T(8,128)S(1)}, f32[512,256]{1,0:T(8,128)S(1)}, u32[]{:S(2)}, u32[]{:S(2)}) collective-permute-start(f32[512,256]{1,0:T(8,128)S(1)} %get-tuple-element.14), channel_id=1, source_target_pairs={{0,16},{16,0},{1,17},{17,1},{2,18},{18,2},{3,19},{19,3},{4,20},{20... | collective-permute-start | bytes 1572872 | tf_op jit(solution)/shard_map/ppermute | solution.py:148
  124.8 14.9 %collective-permute-start.12 = (f32[512,256]{1,0:T(8,128)S(1)}, f32[512,256]{1,0:T(8,128)S(1)}, u32[]{:S(2)}, u32[]{:S(2)}) collective-permute-start(f32[512,256]{1,0:T(8,128)S(1)} %add.15), channel_id=1, source_target_pairs={{0,8},{8,0},{1,9},{9,1},{2,10},{10,2},{3,11},{11,3},{4,12},{12,4},... | collective-permute-start | bytes 1572872 | tf_op jit(solution)/shard_map/ppermute | solution.py:148
  139.8 6.5 %collective-permute-start.13 = (f32[64,256]{1,0:T(8,128)S(1)}, f32[64,256]{1,0:T(8,128)S(1)}, u32[]{:S(2)}, u32[]{:S(2)}) collective-permute-start(f32[64,256]{1,0:T(8,128)S(1)} %shard_map.60), channel_id=1, source_target_pairs={{0,256},{256,0},{1,257},{257,1},{2,258},{258,2},{3,259},{259,3},{4... | collective-permute-start | bytes 196616 | tf_op jit(solution)/shard_map/ppermute | solution.py:148
  146.3 5.0 %collective-permute-start.14 = (f32[64,256]{1,0:T(8,128)S(1)}, f32[64,256]{1,0:T(8,128)S(1)}, u32[]{:S(2)}, u32[]{:S(2)}) collective-permute-start(f32[64,256]{1,0:T(8,128)S(1)} %add.16), channel_id=1, source_target_pairs={{0,32},{32,0},{64,96},{96,64},{128,160},{160,128},{192,224},{224,1... | collective-permute-start | bytes 196616 | tf_op jit(solution)/shard_map/ppermute | solution.py:148
  151.3 5.9 %collective-permute-start.15 = (f32[64,256]{1,0:T(8,128)S(1)}, f32[64,256]{1,0:T(8,128)S(1)}, u32[]{:S(2)}, u32[]{:S(2)}) collective-permute-start(f32[64,256]{1,0:T(8,128)S(1)} %add.17), channel_id=1, source_target_pairs={{0,64},{32,96},{64,0},{96,32},{128,192},{160,224},{192,128},{224,1... | collective-permute-start | bytes 196616 | tf_op jit(solution)/shard_map/ppermute | solution.py:148
  157.3 9.6 %collective-permute-start.16 = (f32[64,256]{1,0:T(8,128)S(1)}, f32[64,256]{1,0:T(8,128)S(1)}, u32[]{:S(2)}, u32[]{:S(2)}) collective-permute-start(f32[64,256]{1,0:T(8,128)S(1)} %add.18), channel_id=1, source_target_pairs={{0,128},{32,160},{64,192},{96,224},{128,0},{160,32},{192,64},{224,... | collective-permute-start | bytes 196616 | tf_op jit(solution)/shard_map/ppermute | solution.py:148
  166.9 8.5 %collective-permute-start.17 = (f32[64,256]{1,0:T(8,128)S(1)}, f32[64,256]{1,0:T(8,128)S(1)}, u32[]{:S(2)}, u32[]{:S(2)}) collective-permute-start(f32[64,256]{1,0:T(8,128)S(1)} %add_multiply_fusion), channel_id=1, source_target_pairs={{0,16},{16,0},{1,17},{17,1},{2,18},{18,2},{3,19},{19,3},{4,20},{20... | collective-permute-start | bytes 196616 | tf_op jit(solution)/shard_map/ppermute | solution.py:148
Sparse Core Ops, SparseCore 0:
  18.9 67.0 all-gather.2

commit v2 on v1

v2 whole, which is shorter than its diff:
```python
import functools

import jax
import jax.numpy as jnp
from jax import lax
from jax.experimental import pallas as pl
from jax.experimental.pallas import tpu as pltpu
from jax.sharding import Mesh, PartitionSpec as P

DP = ("x_hi", "y", "core")
EIGEN = ("x_lo", "z")
SIZES = (2, 8, 2, 2, 8)
F32, BF16 = jnp.float32, jnp.bfloat16
VMEM_LIMIT = 48 * 1024 * 1024


def params(**kw):
    return pltpu.CompilerParams(vmem_limit_bytes=VMEM_LIMIT, **kw)


WHOLE = pl.BlockSpec(memory_space=pltpu.VMEM)
SCALARS = pl.BlockSpec(memory_space=pltpu.SMEM)


def project_kernel(a_ref, x_ref, o_ref):
    per = o_ref.shape[0] // x_ref.shape[0]
    for n in range(x_ref.shape[0]):
        got = lax.dot_general(
            a_ref[...], x_ref[n], (((1,), (1,)), ((), ())), preferred_element_type=F32
        )
        for c in range(per):
            o_ref[n * per + c] = got[:, c * 128 : (c + 1) * 128].astype(o_ref.dtype)


def project(inputs, down):
    count, tokens, width = inputs.shape
    rank = down.shape[0]
    return pl.pallas_call(
        project_kernel,
        in_specs=[WHOLE, WHOLE],
        out_specs=WHOLE,
        out_shape=jax.ShapeDtypeStruct((count * tokens // 128, rank, 128), F32),
        compiler_params=params(),
        cost_estimate=pl.CostEstimate(
            flops=2 * count * tokens * width * rank, bytes_accessed=3 << 20, transcendentals=0
        ),
    )(down, inputs)


def rotate_kernel(p_ref, e_ref, o_ref):
    total = p_ref[0].astype(F32)
    for c in range(1, p_ref.shape[0]):
        total = total + p_ref[c].astype(F32)
    rot = lax.dot_general(
        e_ref[...], total.astype(BF16), (((0,), (0,)), ((), ())), preferred_element_type=F32
    ).astype(BF16)
    for c in range(o_ref.shape[0]):
        o_ref[c] = rot


def rotate(parts, basis):
    return pl.pallas_call(
        rotate_kernel,
        in_specs=[WHOLE, WHOLE],
        out_specs=WHOLE,
        out_shape=jax.ShapeDtypeStruct(parts.shape, BF16),
        compiler_params=params(),
    )(parts, basis)


def grad_kernel(ids_ref, rot_ref, dy_ref, keep_ref, send_ref):
    count, rank = dy_ref.shape[0], rot_ref.shape[1]
    per = rot_ref.shape[0] // count
    half = dy_ref.shape[2] // 2
    first = ids_ref[1] == 0
    for n in range(count):
        rot = jnp.concatenate([rot_ref[n * per + c] for c in range(per)], axis=1)
        grad = jnp.dot(rot, dy_ref[n], preferred_element_type=F32).astype(BF16)
        low, high = grad[:, :half], grad[:, half:]
        rows = slice(n * rank, (n + 1) * rank)
        keep_ref[rows, :] = jnp.where(first, low, high)
        send_ref[rows, :] = jnp.where(first, high, low)


def gradients(ids, rot, dy):
    count, tokens, width = dy.shape
    rank = rot.shape[1]
    out = jax.ShapeDtypeStruct((count * rank, width // 2), BF16)
    return pl.pallas_call(
        grad_kernel,
        in_specs=[SCALARS, WHOLE, WHOLE],
        out_specs=[WHOLE, WHOLE],
        out_shape=[out, out],
        compiler_params=params(),
        cost_estimate=pl.CostEstimate(
            flops=2 * count * tokens * width * rank, bytes_accessed=3 << 20, transcendentals=0
        ),
    )(ids, rot, dy)


def coef_kernel(offsets, which, ids_ref, q_ref, *refs):
    pieces, (away_ref, keep_ref) = refs[:-2], refs[-2:]
    z, core, mine = ids_ref[0], ids_ref[1], ids_ref[which]
    own = pl.ds(pl.multiple_of(core * 256, 256), 256)
    other = pl.ds(pl.multiple_of((1 - core) * 256, 256), 256)
    blocks = [lax.rem(z + off + 8, 8) for off in offsets]
    for rows, h in ((own, 0), (other, 1)):
        for cols, out in ((other, away_ref), (own, keep_ref)):
            total = None
            for piece, b in zip(pieces, blocks):
                term = jnp.dot(piece[h], q_ref[b, mine, :, cols], preferred_element_type=F32)
                total = term if total is None else total + term
            out[rows, :] = total


def coefficients(ids, which, basis, pieces, offsets):
    out = jax.ShapeDtypeStruct((512, 256), F32)
    return pl.pallas_call(
        functools.partial(coef_kernel, offsets, which),
        in_specs=[SCALARS] + [WHOLE] * (1 + len(pieces)),
        out_specs=[WHOLE, WHOLE],
        out_shape=[out, out],
        compiler_params=params(),
        cost_estimate=pl.CostEstimate(flops=1 << 30, bytes_accessed=5 << 20, transcendentals=0),
    )(ids, basis, *pieces)


def square_kernel(a_ref, b_ref, c_ref, o_ref):
    coef = (a_ref[...] + b_ref[...]) + c_ref[...].astype(F32)
    sq = coef * coef
    copies, rank, _ = o_ref.shape
    total = sq[:rank]
    for n in range(1, sq.shape[0] // rank):
        total = total + sq[n * rank : (n + 1) * rank]
    total = total.astype(BF16)
    for i in range(copies):
        o_ref[i] = total


def mean_kernel(p_ref, o_ref):
    total = p_ref[0].astype(F32)
    for i in range(1, p_ref.shape[0]):
        total = total + p_ref[i].astype(F32)
    o_ref[...] = total * (1.0 / 128)


def join_kernel(ids_ref, own_ref, other_ref, o_ref):
    first = ids_ref[1] == 0
    own, other = own_ref[...], other_ref[...]
    half = own.shape[1]
    o_ref[:, :half] = jnp.where(first, own, other)
    o_ref[:, half:] = jnp.where(first, other, own)


def swap(x, axis, stride=1):
    size = dict(zip(DP + EIGEN, SIZES))[axis]
    return lax.ppermute(x, axis, [(i, i ^ stride) for i in range(size)])


def shift(x, step):
    return lax.ppermute(x, "z", [(i, (i + step) % 8) for i in range(8)])


def shards(inputs, out_grads, down, out_basis, adapter_basis):
    z, core = lax.axis_index("z"), lax.axis_index("core")
    x_hi, x_lo = lax.axis_index("x_hi"), lax.axis_index("x_lo")
    mine = lax.bitwise_xor(x_hi, x_lo)
    ids = jnp.stack([z, core, mine, 1 - mine]).astype(jnp.int32)

    basis_a = lax.ppermute(out_basis, ("x_hi", "x_lo"), [(0, 0), (1, 2), (2, 1), (3, 3)])
    basis_b = lax.ppermute(out_basis, ("x_hi", "x_lo"), [(1, 0), (0, 2), (3, 1), (2, 3)])
    parts = project(inputs, down)
    parts, basis_a, basis_b = lax.optimization_barrier((parts, basis_a, basis_b))
    basis = lax.all_gather(jnp.stack([basis_a, basis_b]), "y", axis=0)

    parts = lax.all_to_all(parts, EIGEN, 0, 0)
    rot = lax.all_to_all(rotate(parts, adapter_basis), EIGEN, 0, 0)

    keep, send = gradients(ids, rot, out_grads)
    piece = jnp.stack([keep, swap(send, "core")])
    pieces, offsets = [piece], [0]
    up = down_ = piece
    for s in range(1, 5):
        if s == 4:
            up, basis = lax.optimization_barrier((up, basis))
        up = shift(up, 1)
        pieces.append(up)
        offsets.append(-s)
        if s < 4:
            down_ = shift(down_, -1)
            pieces.append(down_)
            offsets.append(s)

    away, keep = coefficients(ids, 3, basis, pieces, offsets)
    theirs = swap((keep + swap(away, "core")).astype(BF16), "x_lo")
    away, keep = coefficients(ids, 2, basis, pieces, offsets)
    ours = swap(away, "core")
    sums = pl.pallas_call(
        square_kernel,
        in_specs=[WHOLE] * 3,
        out_specs=WHOLE,
        out_shape=jax.ShapeDtypeStruct((16, 64, 256), BF16),
        compiler_params=params(),
    )(keep, ours, theirs)
    sums = lax.all_to_all(sums, ("x_hi", "y"), 0, 0)
    mean = pl.pallas_call(
        mean_kernel,
        in_specs=[WHOLE],
        out_specs=WHOLE,
        out_shape=jax.ShapeDtypeStruct((64, 256), F32),
        compiler_params=params(),
    )(sums)
    return pl.pallas_call(
        join_kernel,
        in_specs=[SCALARS, WHOLE, WHOLE],
        out_specs=WHOLE,
        out_shape=jax.ShapeDtypeStruct((64, 512), F32),
        compiler_params=params(),
    )(ids, mean, swap(mean, "core"))


def solution(mesh):
    fine = Mesh(mesh.devices.reshape(SIZES), DP + EIGEN)
    return jax.shard_map(
        shards,
        mesh=fine,
        in_specs=(
            P(DP, None, EIGEN),
            P(DP, None, EIGEN),
            P(None, EIGEN),
            P(DP, EIGEN),
            P(),
        ),
        out_specs=P(None, EIGEN),
        check_vma=False,
    )
```

time: 184 us -> 169 us (0.918)
  blocking collectives: 26.8 us -> 51 us
  starting transfers between devices: 78.9 us -> 56.6 us
  waiting for transfers between devices: 49 us -> 32.5 us
    all_to_all x0 -> x1, blocking collectives: none -> 24.2 us  [shards(): sums = lax.all_to_all(sums, ('x_hi', 'y'), 0, 0)]
    ppermute x9 -> x5, starting transfers between devices: 43.3 us -> 21.1 us  [swap(): return lax.ppermute(x, axis, [(i, i ^ stride) for i in range(size)])]
    ppermute x9 -> x5, waiting for transfers between devices: 21.4 us -> 8.03 us  [swap(): return lax.ppermute(x, axis, [(i, i ^ stride) for i in range(size)])]
    ppermute x1, waiting for transfers between devices: 3.64 us -> 0.45 us  [shards(): lax.ppermute(out_basis, ('x_hi', 'x_lo'), [(1, 0), (0, 2), (3, 1), (2, 3)])]
    pallas_call x6 -> x8, Pallas kernels: 10.3 us -> 11 us  [the longest x2 6.91 us: coefficients(): pl.pallas_call(functools.partial(coef_kernel, offsets, which), in_specs=[...]
  transfers between devices with their start and end apart: 20 -> 16, of which waited for: 13 -> 9; matrix products, arithmetic and copies ran while one was open for 0% -> 0% of each run, Pallas kernels for 4% -> 4%
where the time goes in v2:
time: 169 us; the launch traced here: 168 us
  starting transfers between devices  56.6 us (33%)
  blocking collectives  51 us (30%)
  waiting for transfers between devices  32.5 us (19%)
  between operations  13.6 us (8%)
  Pallas kernels  11 us (7%)
  local copies, waits for them, and re-layouts  2.43 us (1%)
    all_to_all x1, blocking collectives, shards(): parts = lax.all_to_all(parts, EIGEN, 0, 0)  26.8 us
    all_to_all x1, blocking collectives, shards(): sums = lax.all_to_all(sums, ('x_hi', 'y'), 0, 0)  24.2 us
    ppermute x7, starting transfers between devices, shift(): return lax.ppermute(x, 'z', [(i, (i + step) % 8) for i in range(8)])  21.4 us
    ppermute x5, starting transfers between devices, swap(): return lax.ppermute(x, axis, [(i, i ^ stride) for i in range(size)])  21.1 us
    ppermute x7, waiting for transfers between devices, shift(): return lax.ppermute(x, 'z', [(i, (i + step) % 8) for i in range(8)])  16.3 us
    ppermute x5, waiting for transfers between devices, swap(): return lax.ppermute(x, axis, [(i, i ^ stride) for i in range(size)])  8.03 us
    all_to_all x1, waiting for transfers between devices, shards(): rot = lax.all_to_all(rotate(parts, adapter_basis), EIGEN, 0, 0)  7.67 us
    pallas_call x2, Pallas kernels, coefficients(): pl.pallas_call(functools.partial(coef_kernel, offsets, which), in_specs=[...  6.91 us
  transfers between devices with their start and end apart: 16, of which 9 were waited for; matrix products, arithmetic and copies ran while one was open for 0% of the time, Pallas kernels for 4%

profile of v2, /device:TPU:1, one launch (start us, length us, event | category | flops | bytes accessed | tf_op | source)
XLA Modules:
  0.0 168.1 jit_solution(15914395767947410806)
XLA Ops:
  6.5 1.6 collective-permute-start
  8.1 6.0 %collective-permute-start.1 = (bf16[256,512]{1,0:T(8,128)(2,1)}, bf16[256,512]{1,0:T(8,128)(2,1)S(1)}, u32[]{:S(2)}, u32[]{:S(2)}) collective-permute-start(bf16[256,512]{1,0:T(8,128)(2,1)} %param.8), channel_id=1, source_target_pairs={{8,0},{0,256},{264,8},{256,264},{9,1},{1,257},{265,9},{257,265},{1... | collective-permute-start | bytes 786440 | tf_op jit(solution)/shard_map/ppermute | solution.py:171
  14.2 1.6 copy-done.1
  17.8 0.8 pad_maximum_fusion
  18.7 26.8 %all_to_all.15.p_ref = f32[16,64,128]{2,1,0:T(8,128)S(1)} all-to-all(f32[16,64,128]{2,1,0:T(8,128)S(1)} %shard_map.55), channel_id=1, replica_groups=mesh['x_hi'=2,'y'=8,'core'=2,'x_lo'=2,'z'=8] {'x_lo','z'}, dimensions={0} | all-to-all | bytes 1048576 | tf_op jit(solution)/shard_map/all_to_all | solution.py:176
  45.5 0.9 shard_map.56
  46.4 6.5 %all-to-all-start.1 = ((bf16[16,64,128]{2,1,0:T(8,128)(2,1)}), bf16[16,64,128]{2,1,0:T(8,128)(2,1)S(1)}, u32[]{:S(2)}, u32[]{:S(2)}) async-start(bf16[16,64,128]{2,1,0:T(8,128)(2,1)} %shard_map.56), calls=%async_computation.1 | async-start | bytes 524288 | tf_op jit(solution)/shard_map/all_to_all | solution.py:177
  52.9 7.7 %all-to-all-done.1.rot_ref = bf16[16,64,128]{2,1,0:T(8,128)(2,1)S(1)} async-done(((bf16[16,64,128]{2,1,0:T(8,128)(2,1)}), bf16[16,64,128]{2,1,0:T(8,128)(2,1)S(1)}, u32[]{:S(2)}, u32[]{:S(2)}) %all-to-all-start.1) | async-done | bytes 262176 | tf_op jit(solution)/shard_map/all_to_all | solution.py:177
  60.6 1.0 shard_map.57
  61.6 5.3 %collective-permute-start.2 = (bf16[256,256]{1,0:T(8,128)(2,1)S(1)}, bf16[256,256]{1,0:T(8,128)(2,1)S(1)}, u32[]{:S(2)}, u32[]{:S(2)}) collective-permute-start(bf16[256,256]{1,0:T(8,128)(2,1)S(1)} %get-tuple-element.18), channel_id=1, source_target_pairs={{0,16},{16,0},{1,17},{17,1},{2,18},{18,2},{3,19},{19,3},{4,20},{20... | collective-permute-start | bytes 393224 | tf_op jit(solution)/shard_map/ppermute | solution.py:157
  67.0 1.0 collective-permute-done.2
  68.0 3.7 %collective-permute-start.3 = (bf16[2,256,256]{2,1,0:T(8,128)(2,1)S(1)}, bf16[2,256,256]{2,1,0:T(8,128)(2,1)S(1)}, u32[]{:S(2)}, u32[]{:S(2)}) collective-permute-start(bf16[2,256,256]{2,1,0:T(8,128)(2,1)S(1)} %pad_maximum_fusion.1.refs_0_), channel_id=1, source_target_pairs={{0,1},{1,2},{2,3},{3,4},{4,5},{5,6},{6,7},{7,0},{8,9},{9,10},{10,1... | collective-permute-start | bytes 786440 | tf_op jit(solution)/shard_map/ppermute | solution.py:161
  71.6 2.8 %collective-permute-start.6 = (bf16[2,256,256]{2,1,0:T(8,128)(2,1)S(1)}, bf16[2,256,256]{2,1,0:T(8,128)(2,1)S(1)}, u32[]{:S(2)}, u32[]{:S(2)}) collective-permute-start(bf16[2,256,256]{2,1,0:T(8,128)(2,1)S(1)} %pad_maximum_fusion.1.refs_0_), channel_id=1, source_target_pairs={{0,7},{1,0},{2,1},{3,2},{4,3},{5,4},{6,5},{7,6},{8,15},{9,8},{10,9... | collective-permute-start | bytes 786440 | tf_op jit(solution)/shard_map/ppermute | solution.py:161
  74.5 4.2 %collective-permute-done.3.refs_1_ = bf16[2,256,256]{2,1,0:T(8,128)(2,1)S(1)} collective-permute-done((bf16[2,256,256]{2,1,0:T(8,128)(2,1)S(1)}, bf16[2,256,256]{2,1,0:T(8,128)(2,1)S(1)}, u32[]{:S(2)}, u32[]{:S(2)}) %collective-permute-start.3) | collective-permute-done | bytes 262176 | tf_op jit(solution)/shard_map/ppermute | solution.py:161
  78.7 2.4 %collective-permute-start.4 = (bf16[2,256,256]{2,1,0:T(8,128)(2,1)S(1)}, bf16[2,256,256]{2,1,0:T(8,128)(2,1)S(1)}, u32[]{:S(2)}, u32[]{:S(2)}) collective-permute-start(bf16[2,256,256]{2,1,0:T(8,128)(2,1)S(1)} %collective-permute-done.3.refs_1_), channel_id=1, source_target_pairs={{0,1},{1,2},{2,3},{3,4},{4,5},{5,6},{6,7},{7,0},{8,9},{9,10},{10,1... | collective-permute-start | bytes 786440 | tf_op jit(solution)/shard_map/ppermute | solution.py:161
  81.2 4.1 %collective-permute-start.7 = (bf16[2,256,256]{2,1,0:T(8,128)(2,1)S(1)}, bf16[2,256,256]{2,1,0:T(8,128)(2,1)S(1)}, u32[]{:S(2)}, u32[]{:S(2)}) collective-permute-start(bf16[2,256,256]{2,1,0:T(8,128)(2,1)S(1)} %collective-permute-done.6.refs_2_), channel_id=1, source_target_pairs={{0,7},{1,0},{2,1},{3,2},{4,3},{5,4},{6,5},{7,6},{8,15},{9,8},{10,9... | collective-permute-start | bytes 786440 | tf_op jit(solution)/shard_map/ppermute | solution.py:161
  85.2 3.3 %collective-permute-done.4.refs_3_ = bf16[2,256,256]{2,1,0:T(8,128)(2,1)S(1)} collective-permute-done((bf16[2,256,256]{2,1,0:T(8,128)(2,1)S(1)}, bf16[2,256,256]{2,1,0:T(8,128)(2,1)S(1)}, u32[]{:S(2)}, u32[]{:S(2)}) %collective-permute-start.4) | collective-permute-done | bytes 262176 | tf_op jit(solution)/shard_map/ppermute | solution.py:161
  88.5 1.9 %collective-permute-start.5 = (bf16[2,256,256]{2,1,0:T(8,128)(2,1)S(1)}, bf16[2,256,256]{2,1,0:T(8,128)(2,1)S(1)}, u32[]{:S(2)}, u32[]{:S(2)}) collective-permute-start(bf16[2,256,256]{2,1,0:T(8,128)(2,1)S(1)} %collective-permute-done.4.refs_3_), channel_id=1, source_target_pairs={{0,1},{1,2},{2,3},{3,4},{4,5},{5,6},{6,7},{7,0},{8,9},{9,10},{10,1... | collective-permute-start | bytes 786440 | tf_op jit(solution)/shard_map/ppermute | solution.py:161
  90.5 4.6 %collective-permute-start.8 = (bf16[2,256,256]{2,1,0:T(8,128)(2,1)S(1)}, bf16[2,256,256]{2,1,0:T(8,128)(2,1)S(1)}, u32[]{:S(2)}, u32[]{:S(2)}) collective-permute-start(bf16[2,256,256]{2,1,0:T(8,128)(2,1)S(1)} %collective-permute-done.7.refs_4_), channel_id=1, source_target_pairs={{0,7},{1,0},{2,1},{3,2},{4,3},{5,4},{6,5},{7,6},{8,15},{9,8},{10,9... | collective-permute-start | bytes 786440 | tf_op jit(solution)/shard_map/ppermute | solution.py:161
  95.0 2.4 %collective-permute-done.5.refs_5_ = bf16[2,256,256]{2,1,0:T(8,128)(2,1)S(1)} collective-permute-done((bf16[2,256,256]{2,1,0:T(8,128)(2,1)S(1)}, bf16[2,256,256]{2,1,0:T(8,128)(2,1)S(1)}, u32[]{:S(2)}, u32[]{:S(2)}) %collective-permute-start.5) | collective-permute-done | bytes 262176 | tf_op jit(solution)/shard_map/ppermute | solution.py:161
  97.4 1.9 %collective-permute-start.9 = (bf16[2,256,256]{2,1,0:T(8,128)(2,1)S(1)}, bf16[2,256,256]{2,1,0:T(8,128)(2,1)S(1)}, u32[]{:S(2)}, u32[]{:S(2)}) collective-permute-start(bf16[2,256,256]{2,1,0:T(8,128)(2,1)S(1)} %collective-permute-done.5.refs_5_), channel_id=1, source_target_pairs={{0,1},{1,2},{2,3},{3,4},{4,5},{5,6},{6,7},{7,0},{8,9},{9,10},{10,1... | collective-permute-start | bytes 786440 | tf_op jit(solution)/shard_map/ppermute | solution.py:161
  99.3 6.4 %collective-permute-done.9.refs_7_ = bf16[2,256,256]{2,1,0:T(8,128)(2,1)S(1)} collective-permute-done((bf16[2,256,256]{2,1,0:T(8,128)(2,1)S(1)}, bf16[2,256,256]{2,1,0:T(8,128)(2,1)S(1)}, u32[]{:S(2)}, u32[]{:S(2)}) %collective-permute-start.9) | collective-permute-done | bytes 262176 | tf_op jit(solution)/shard_map/ppermute | solution.py:161
  105.7 3.5 %shard_map.59 = (f32[512,256]{1,0:T(8,128)S(1)}, f32[512,256]{1,0:T(8,128)S(1)}) custom-call(s32[4]{0:T(128)S(1)} %pad_add_fusion.ids_ref, bf16[8,2,256,512]{3,2,1,0:T(8,128)(2,1)} %bitcast.10, bf16[2,256,256]{2,1,0:T(8,128)(2,1)S(1)} %pad_maximum_fusion.1.refs_0_, bf16[2,256,256]{2,1,0:T(8,128)(2,1)S(1)} %collective-permute-done.3.refs_1_, ...), custom_call_target="tpu_custom_call" | custom-call | flops 1073741824 | bytes 5242880 | tf_op jit(solution)/shard_map/pallas_call | solution.py:118
  109.2 6.0 %collective-permute-start.11 = (f32[512,256]{1,0:T(8,128)S(1)}, f32[512,256]{1,0:T(8,128)S(1)}, u32[]{:S(2)}, u32[]{:S(2)}) collective-permute-start(f32[512,256]{1,0:T(8,128)S(1)} %get-tuple-element.26), channel_id=1, source_target_pairs={{0,16},{16,0},{1,17},{17,1},{2,18},{18,2},{3,19},{19,3},{4,20},{20... | collective-permute-start | bytes 1572872 | tf_op jit(solution)/shard_map/ppermute | solution.py:157
  115.2 3.5 %shard_map.58 = (f32[512,256]{1,0:T(8,128)S(1)}, f32[512,256]{1,0:T(8,128)S(1)}) custom-call(s32[4]{0:T(128)S(1)} %pad_add_fusion.ids_ref, bf16[8,2,256,512]{3,2,1,0:T(8,128)(2,1)} %bitcast.11, bf16[2,256,256]{2,1,0:T(8,128)(2,1)S(1)} %pad_maximum_fusion.1.refs_0_, bf16[2,256,256]{2,1,0:T(8,128)(2,1)S(1)} %collective-permute-done.3.refs_1_, ...), custom_call_target="tpu_custom_call" | custom-call | flops 1073741824 | bytes 5242880 | tf_op jit(solution)/shard_map/pallas_call | solution.py:118
  118.7 1.9 %collective-permute-start.10 = (f32[512,256]{1,0:T(8,128)S(1)}, f32[512,256]{1,0:T(8,128)S(1)}, u32[]{:S(2)}, u32[]{:S(2)}) collective-permute-start(f32[512,256]{1,0:T(8,128)S(1)} %get-tuple-element.24), channel_id=1, source_target_pairs={{0,16},{16,0},{1,17},{17,1},{2,18},{18,2},{3,19},{19,3},{4,20},{20... | collective-permute-start | bytes 1572872 | tf_op jit(solution)/shard_map/ppermute | solution.py:157
  120.7 3.1 %collective-permute-start.12 = (bf16[512,256]{1,0:T(8,128)(2,1)S(1)}, bf16[512,256]{1,0:T(8,128)(2,1)S(1)}, u32[]{:S(2)}, u32[]{:S(2)}) collective-permute-start(bf16[512,256]{1,0:T(8,128)(2,1)S(1)} %add_convert_fusion), channel_id=1, source_target_pairs={{0,8},{8,0},{1,9},{9,1},{2,10},{10,2},{3,11},{11,3},{4,12},{12,4},... | collective-permute-start | bytes 786440 | tf_op jit(solution)/shard_map/ppermute | solution.py:157
  123.8 6.2 %collective-permute-done.12.c_ref = bf16[512,256]{1,0:T(8,128)(2,1)S(1)} collective-permute-done((bf16[512,256]{1,0:T(8,128)(2,1)S(1)}, bf16[512,256]{1,0:T(8,128)(2,1)S(1)}, u32[]{:S(2)}, u32[]{:S(2)}) %collective-permute-start.12) | collective-permute-done | bytes 262176 | tf_op jit(solution)/shard_map/ppermute | solution.py:157
  130.1 24.2 %all_to_all.16.p_ref = bf16[16,64,256]{2,1,0:T(8,128)(2,1)S(1)} all-to-all(bf16[16,64,256]{2,1,0:T(8,128)(2,1)S(1)} %shard_map.60), channel_id=1, replica_groups=mesh['x_hi'=2,'y'=8,'core'=2,'x_lo'=2,'z'=8] {'x_hi','y'}, dimensions={0} | all-to-all | bytes 1048576 | tf_op jit(solution)/shard_map/all_to_all | solution.py:205
  154.4 4.8 %collective-permute-start.13 = (f32[64,256]{1,0:T(8,128)S(1)}, f32[64,256]{1,0:T(8,128)S(1)}, u32[]{:S(2)}, u32[]{:S(2)}) collective-permute-start(f32[64,256]{1,0:T(8,128)S(1)} %shard_map.61.own_ref), channel_id=1, source_target_pairs={{0,16},{16,0},{1,17},{17,1},{2,18},{18,2},{3,19},{19,3},{4,20},{20... | collective-permute-start | bytes 196616 | tf_op jit(solution)/shard_map/ppermute | solution.py:157
  159.2 0.9 collective-permute-done.13.other_ref
  160.1 1.2 shard_map.62
  (23 shorter events, 2.5 us)
Async XLA Ops:
  6.5 90.9 %all-gather.3.cloned.1.call-start = ((), (), s32[]{:S(2)}) async-start(), calls=%async_computation.3 | async-start | bytes 4718592 | tf_op jit(solution)/shard_map/all_gather | solution.py:174
  6.5 10.8 %collective-permute-start = (bf16[256,512]{1,0:T(8,128)(2,1)}, bf16[256,512]{1,0:T(8,128)(2,1)S(1)}, u32[]{:S(2)}, u32[]{:S(2)}) collective-permute-start(bf16[256,512]{1,0:T(8,128)(2,1)} %param.8), channel_id=1, source_target_pairs={{0,0},{8,256},{256,8},{264,264},{1,1},{9,257},{257,9},{265,265},{2... | collective-permute-start | bytes 786440 | tf_op jit(solution)/shard_map/ppermute | solution.py:170
  8.1 9.7 %collective-permute-start.1 = (bf16[256,512]{1,0:T(8,128)(2,1)}, bf16[256,512]{1,0:T(8,128)(2,1)S(1)}, u32[]{:S(2)}, u32[]{:S(2)}) collective-permute-start(bf16[256,512]{1,0:T(8,128)(2,1)} %param.8), channel_id=1, source_target_pairs={{8,0},{0,256},{264,8},{256,264},{9,1},{1,257},{265,9},{257,265},{1... | collective-permute-start | bytes 786440 | tf_op jit(solution)/shard_map/ppermute | solution.py:171
  14.2 1.6 copy-start.1
  15.8 0.8 copy-start.2
  16.6 28.9 %copy-start.3 = (bf16[64,64]{1,0:T(8,128)(2,1)S(1)}, bf16[64,64]{1,0:T(8,128)(2,1)}, u32[]{:S(2)}) copy-start(bf16[64,64]{1,0:T(8,128)(2,1)} %e_ref.1) | copy-start | bytes 24580
  17.4 43.3 %copy-start = (bf16[4,512,512]{2,1,0:T(8,128)(2,1)S(1)}, bf16[4,512,512]{2,1,0:T(8,128)(2,1)}, u32[]{:S(2)}) copy-start(bf16[4,512,512]{2,1,0:T(8,128)(2,1)} %dy_ref.1) | copy-start | bytes 6291460
  46.4 14.2 %all-to-all-start.1 = ((bf16[16,64,128]{2,1,0:T(8,128)(2,1)}), bf16[16,64,128]{2,1,0:T(8,128)(2,1)S(1)}, u32[]{:S(2)}, u32[]{:S(2)}) async-start(bf16[16,64,128]{2,1,0:T(8,128)(2,1)} %shard_map.56), calls=%async_computation.1 | async-start | bytes 524288 | tf_op jit(solution)/shard_map/all_to_all | solution.py:177
  61.6 6.3 %collective-permute-start.2 = (bf16[256,256]{1,0:T(8,128)(2,1)S(1)}, bf16[256,256]{1,0:T(8,128)(2,1)S(1)}, u32[]{:S(2)}, u32[]{:S(2)}) collective-permute-start(bf16[256,256]{1,0:T(8,128)(2,1)S(1)} %get-tuple-element.18), channel_id=1, source_target_pairs={{0,16},{16,0},{1,17},{17,1},{2,18},{18,2},{3,19},{19,3},{4,20},{20... | collective-permute-start | bytes 393224 | tf_op jit(solution)/shard_map/ppermute | solution.py:157
  68.0 10.7 %collective-permute-start.3 = (bf16[2,256,256]{2,1,0:T(8,128)(2,1)S(1)}, bf16[2,256,256]{2,1,0:T(8,128)(2,1)S(1)}, u32[]{:S(2)}, u32[]{:S(2)}) collective-permute-start(bf16[2,256,256]{2,1,0:T(8,128)(2,1)S(1)} %pad_maximum_fusion.1.refs_0_), channel_id=1, source_target_pairs={{0,1},{1,2},{2,3},{3,4},{4,5},{5,6},{6,7},{7,0},{8,9},{9,10},{10,1... | collective-permute-start | bytes 786440 | tf_op jit(solution)/shard_map/ppermute | solution.py:161
  71.6 9.5 %collective-permute-start.6 = (bf16[2,256,256]{2,1,0:T(8,128)(2,1)S(1)}, bf16[2,256,256]{2,1,0:T(8,128)(2,1)S(1)}, u32[]{:S(2)}, u32[]{:S(2)}) collective-permute-start(bf16[2,256,256]{2,1,0:T(8,128)(2,1)S(1)} %pad_maximum_fusion.1.refs_0_), channel_id=1, source_target_pairs={{0,7},{1,0},{2,1},{3,2},{4,3},{5,4},{6,5},{7,6},{8,15},{9,8},{10,9... | collective-permute-start | bytes 786440 | tf_op jit(solution)/shard_map/ppermute | solution.py:161
  78.7 9.8 %collective-permute-start.4 = (bf16[2,256,256]{2,1,0:T(8,128)(2,1)S(1)}, bf16[2,256,256]{2,1,0:T(8,128)(2,1)S(1)}, u32[]{:S(2)}, u32[]{:S(2)}) collective-permute-start(bf16[2,256,256]{2,1,0:T(8,128)(2,1)S(1)} %collective-permute-done.3.refs_1_), channel_id=1, source_target_pairs={{0,1},{1,2},{2,3},{3,4},{4,5},{5,6},{6,7},{7,0},{8,9},{9,10},{10,1... | collective-permute-start | bytes 786440 | tf_op jit(solution)/shard_map/ppermute | solution.py:161
  81.2 9.3 %collective-permute-start.7 = (bf16[2,256,256]{2,1,0:T(8,128)(2,1)S(1)}, bf16[2,256,256]{2,1,0:T(8,128)(2,1)S(1)}, u32[]{:S(2)}, u32[]{:S(2)}) collective-permute-start(bf16[2,256,256]{2,1,0:T(8,128)(2,1)S(1)} %collective-permute-done.6.refs_2_), channel_id=1, source_target_pairs={{0,7},{1,0},{2,1},{3,2},{4,3},{5,4},{6,5},{7,6},{8,15},{9,8},{10,9... | collective-permute-start | bytes 786440 | tf_op jit(solution)/shard_map/ppermute | solution.py:161
  88.5 8.9 %collective-permute-start.5 = (bf16[2,256,256]{2,1,0:T(8,128)(2,1)S(1)}, bf16[2,256,256]{2,1,0:T(8,128)(2,1)S(1)}, u32[]{:S(2)}, u32[]{:S(2)}) collective-permute-start(bf16[2,256,256]{2,1,0:T(8,128)(2,1)S(1)} %collective-permute-done.4.refs_3_), channel_id=1, source_target_pairs={{0,1},{1,2},{2,3},{3,4},{4,5},{5,6},{6,7},{7,0},{8,9},{9,10},{10,1... | collective-permute-start | bytes 786440 | tf_op jit(solution)/shard_map/ppermute | solution.py:161
  90.5 8.9 %collective-permute-start.8 = (bf16[2,256,256]{2,1,0:T(8,128)(2,1)S(1)}, bf16[2,256,256]{2,1,0:T(8,128)(2,1)S(1)}, u32[]{:S(2)}, u32[]{:S(2)}) collective-permute-start(bf16[2,256,256]{2,1,0:T(8,128)(2,1)S(1)} %collective-permute-done.7.refs_4_), channel_id=1, source_target_pairs={{0,7},{1,0},{2,1},{3,2},{4,3},{5,4},{6,5},{7,6},{8,15},{9,8},{10,9... | collective-permute-start | bytes 786440 | tf_op jit(solution)/shard_map/ppermute | solution.py:161
  97.4 8.3 %collective-permute-start.9 = (bf16[2,256,256]{2,1,0:T(8,128)(2,1)S(1)}, bf16[2,256,256]{2,1,0:T(8,128)(2,1)S(1)}, u32[]{:S(2)}, u32[]{:S(2)}) collective-permute-start(bf16[2,256,256]{2,1,0:T(8,128)(2,1)S(1)} %collective-permute-done.5.refs_5_), channel_id=1, source_target_pairs={{0,1},{1,2},{2,3},{3,4},{4,5},{5,6},{6,7},{7,0},{8,9},{9,10},{10,1... | collective-permute-start | bytes 786440 | tf_op jit(solution)/shard_map/ppermute | solution.py:161
  109.2 11.4 %collective-permute-start.11 = (f32[512,256]{1,0:T(8,128)S(1)}, f32[512,256]{1,0:T(8,128)S(1)}, u32[]{:S(2)}, u32[]{:S(2)}) collective-permute-start(f32[512,256]{1,0:T(8,128)S(1)} %get-tuple-element.26), channel_id=1, source_target_pairs={{0,16},{16,0},{1,17},{17,1},{2,18},{18,2},{3,19},{19,3},{4,20},{20... | collective-permute-start | bytes 1572872 | tf_op jit(solution)/shard_map/ppermute | solution.py:157
  118.7 5.1 %collective-permute-start.10 = (f32[512,256]{1,0:T(8,128)S(1)}, f32[512,256]{1,0:T(8,128)S(1)}, u32[]{:S(2)}, u32[]{:S(2)}) collective-permute-start(f32[512,256]{1,0:T(8,128)S(1)} %get-tuple-element.24), channel_id=1, source_target_pairs={{0,16},{16,0},{1,17},{17,1},{2,18},{18,2},{3,19},{19,3},{4,20},{20... | collective-permute-start | bytes 1572872 | tf_op jit(solution)/shard_map/ppermute | solution.py:157
  120.7 9.3 %collective-permute-start.12 = (bf16[512,256]{1,0:T(8,128)(2,1)S(1)}, bf16[512,256]{1,0:T(8,128)(2,1)S(1)}, u32[]{:S(2)}, u32[]{:S(2)}) collective-permute-start(bf16[512,256]{1,0:T(8,128)(2,1)S(1)} %add_convert_fusion), channel_id=1, source_target_pairs={{0,8},{8,0},{1,9},{9,1},{2,10},{10,2},{3,11},{11,3},{4,12},{12,4},... | collective-permute-start | bytes 786440 | tf_op jit(solution)/shard_map/ppermute | solution.py:157
  154.4 5.7 %collective-permute-start.13 = (f32[64,256]{1,0:T(8,128)S(1)}, f32[64,256]{1,0:T(8,128)S(1)}, u32[]{:S(2)}, u32[]{:S(2)}) collective-permute-start(f32[64,256]{1,0:T(8,128)S(1)} %shard_map.61.own_ref), channel_id=1, source_target_pairs={{0,16},{16,0},{1,17},{17,1},{2,18},{18,2},{3,19},{19,3},{4,20},{20... | collective-permute-start | bytes 196616 | tf_op jit(solution)/shard_map/ppermute | solution.py:157
Sparse Core Ops, SparseCore 0:
  18.8 67.0 all-gather.2

commit v3 on v2

v3 whole, which is shorter than its diff:
```python
import functools

import jax
import jax.numpy as jnp
from jax import lax
from jax.experimental import pallas as pl
from jax.experimental.pallas import tpu as pltpu
from jax.sharding import Mesh, PartitionSpec as P

DP = ("x_hi", "y", "core")
EIGEN = ("x_lo", "z")
SIZES = (2, 8, 2, 2, 8)
F32, BF16 = jnp.float32, jnp.bfloat16
PARTIAL = BF16
VMEM_LIMIT = 16 * 1024 * 1024


def params(**kw):
    return pltpu.CompilerParams(vmem_limit_bytes=VMEM_LIMIT, **kw)


WHOLE = pl.BlockSpec(memory_space=pltpu.VMEM)
SCALARS = pl.BlockSpec(memory_space=pltpu.SMEM)


HBM = pl.BlockSpec(memory_space=pltpu.HBM)


def project_kernel(a_ref, x_ref, o_ref, a_buf, x_buf, sems):
    count = x_ref.shape[0]
    per = o_ref.shape[0] // count
    down = pltpu.make_async_copy(a_ref, a_buf, sems.at[count])
    down.start()
    copies = [pltpu.make_async_copy(x_ref.at[n], x_buf.at[n], sems.at[n]) for n in range(count)]
    for copy in copies:
        copy.start()
    down.wait()
    for n in range(count):
        copies[n].wait()
        got = lax.dot_general(
            a_buf[...], x_buf[n], (((1,), (1,)), ((), ())), preferred_element_type=F32
        )
        for c in range(per):
            o_ref[n * per + c] = got[:, c * 128 : (c + 1) * 128].astype(o_ref.dtype)


def project(inputs, down):
    count, tokens, width = inputs.shape
    rank = down.shape[0]
    return pl.pallas_call(
        project_kernel,
        in_specs=[HBM, HBM],
        out_specs=WHOLE,
        out_shape=jax.ShapeDtypeStruct((count * tokens // 128, rank, 128), PARTIAL),
        scratch_shapes=[
            pltpu.VMEM(down.shape, BF16),
            pltpu.VMEM(inputs.shape, BF16),
            pltpu.SemaphoreType.DMA((count + 1,)),
        ],
        compiler_params=pltpu.CompilerParams(vmem_limit_bytes=60 * 1024 * 1024),
        cost_estimate=pl.CostEstimate(
            flops=2 * count * tokens * width * rank, bytes_accessed=3 << 20, transcendentals=0
        ),
    )(down, inputs)


def rotate_kernel(p_ref, e_ref, o_ref):
    total = p_ref[0].astype(F32)
    for c in range(1, p_ref.shape[0]):
        total = total + p_ref[c].astype(F32)
    rot = lax.dot_general(
        e_ref[...], total.astype(BF16), (((0,), (0,)), ((), ())), preferred_element_type=F32
    ).astype(BF16)
    for c in range(o_ref.shape[0]):
        o_ref[c] = rot


def rotate(parts, basis):
    return pl.pallas_call(
        rotate_kernel,
        in_specs=[WHOLE, WHOLE],
        out_specs=WHOLE,
        out_shape=jax.ShapeDtypeStruct(parts.shape, BF16),
        compiler_params=params(),
    )(parts, basis)


def grad_kernel(ids_ref, rot_ref, dy_ref, keep_ref, send_ref):
    count, rank = dy_ref.shape[0], rot_ref.shape[1]
    per = rot_ref.shape[0] // count
    half = dy_ref.shape[2] // 2
    first = ids_ref[1] == 0
    for n in range(count):
        rot = jnp.concatenate([rot_ref[n * per + c] for c in range(per)], axis=1)
        grad = jnp.dot(rot, dy_ref[n], preferred_element_type=F32).astype(BF16)
        low, high = grad[:, :half], grad[:, half:]
        rows = slice(n * rank, (n + 1) * rank)
        keep_ref[rows, :] = jnp.where(first, low, high)
        send_ref[rows, :] = jnp.where(first, high, low)


def gradients(ids, rot, dy):
    count, tokens, width = dy.shape
    rank = rot.shape[1]
    out = jax.ShapeDtypeStruct((count * rank, width // 2), BF16)
    return pl.pallas_call(
        grad_kernel,
        in_specs=[SCALARS, WHOLE, WHOLE],
        out_specs=[WHOLE, WHOLE],
        out_shape=[out, out],
        compiler_params=params(),
        cost_estimate=pl.CostEstimate(
            flops=2 * count * tokens * width * rank, bytes_accessed=3 << 20, transcendentals=0
        ),
    )(ids, rot, dy)


def coef_parts(ids_ref, q_ref, pieces, offsets, dests):
    z, x_hi, x_lo = ids_ref[0], ids_ref[1], ids_ref[2]
    blocks = [lax.rem(z + off + 8, 8) for off in offsets]
    for i, (other_hi, other_lo) in enumerate(dests):
        j = 1 - x_lo if other_lo else x_lo
        half = 1 - x_hi if other_hi else x_hi
        cols = pl.ds(pl.multiple_of(half * 256, 256), 256)
        for h in range(2):
            rows = pl.ds(pl.multiple_of((1 - x_lo if h else x_lo) * 256, 256), 256)
            total = None
            for piece, b in zip(pieces, blocks):
                term = jnp.dot(piece[h], q_ref[b, j, :, cols], preferred_element_type=F32)
                total = term if total is None else total + term
            yield i, rows, total


DESTS = ((1, 0), (0, 1), (1, 1), (0, 0))
COEF = (512, 256)


def early_kernel(offsets, ids_ref, q_ref, *refs):
    pieces, out = refs[:-1], refs[-1]
    for i, rows, total in coef_parts(ids_ref, q_ref, pieces, offsets, DESTS):
        out[i, rows, :] = total


def late_kernel(offset, first, count, ids_ref, q_ref, piece_ref, sum_ref, *outs):
    dests = DESTS[first : first + count]
    for i, rows, total in coef_parts(ids_ref, q_ref, [piece_ref], [offset], dests):
        outs[i][rows, :] = (sum_ref[first + i, rows, :] + total).astype(outs[i].dtype)


def early(ids, basis, pieces, offsets):
    return pl.pallas_call(
        functools.partial(early_kernel, offsets),
        in_specs=[SCALARS] + [WHOLE] * (1 + len(pieces)),
        out_specs=WHOLE,
        out_shape=jax.ShapeDtypeStruct((4,) + COEF, F32),
        compiler_params=params(),
        cost_estimate=pl.CostEstimate(flops=2 << 30, bytes_accessed=8 << 20, transcendentals=0),
    )(ids, basis, *pieces)


def late(ids, basis, piece, offset, sums, first, count, dtype):
    return pl.pallas_call(
        functools.partial(late_kernel, offset, first, count),
        in_specs=[SCALARS] + [WHOLE] * 3,
        out_specs=[WHOLE] * count,
        out_shape=[jax.ShapeDtypeStruct(COEF, dtype)] * count,
        compiler_params=params(),
        cost_estimate=pl.CostEstimate(flops=1 << 28, bytes_accessed=2 << 20, transcendentals=0),
    )(ids, basis, piece, sums)


def square_kernel(a_ref, b_ref, c_ref, d_ref, o_ref):
    coef = (a_ref[...] + b_ref[...].astype(F32)) + (c_ref[...].astype(F32) + d_ref[...].astype(F32))
    sq = coef * coef
    rank = o_ref.shape[1]
    total = sq[:rank]
    for n in range(1, sq.shape[0] // rank):
        total = total + sq[n * rank : (n + 1) * rank]
    total = total.astype(BF16)
    for i in range(o_ref.shape[0]):
        o_ref[i] = total


def mean_kernel(p_ref, o_ref):
    total = p_ref[0].astype(F32)
    for i in range(1, p_ref.shape[0]):
        total = total + p_ref[i].astype(F32)
    o_ref[...] = total * (1.0 / 128)


def join_kernel(ids_ref, own_ref, core_ref, hi_ref, both_ref, o_ref):
    first = ids_ref[1] == 0
    own, other = own_ref[...] + core_ref[...], hi_ref[...] + both_ref[...]
    half = own.shape[1]
    o_ref[:, :half] = jnp.where(first, own, other)
    o_ref[:, half:] = jnp.where(first, other, own)


def swap(x, axis, stride=1):
    size = dict(zip(DP + EIGEN, SIZES))[axis]
    return lax.ppermute(x, axis, [(i, i ^ stride) for i in range(size)])


def shift(x, step):
    return lax.ppermute(x, "z", [(i, (i + step) % 8) for i in range(8)])


TURN = [(0, 0), (1, 2), (2, 1), (3, 3)]
CROSS = [(2, 0), (0, 1), (3, 2), (1, 3)]


def shards(inputs, out_grads, down, out_basis, adapter_basis):
    z = lax.axis_index("z")
    x_hi, x_lo = lax.axis_index("x_hi"), lax.axis_index("x_lo")
    ids = jnp.stack([z, x_hi, x_lo]).astype(jnp.int32)

    turned = lax.ppermute(out_basis, ("core", "x_lo"), TURN)
    parts = project(inputs, down)
    parts = lax.all_to_all(parts, EIGEN, 0, 0)
    parts, turned = lax.optimization_barrier((parts, turned))
    basis = lax.all_gather(turned, ("y", "core"), axis=0).reshape(8, 2, *out_basis.shape)
    rot = lax.all_to_all(rotate(parts, adapter_basis), EIGEN, 0, 0)

    keep, send = gradients(ids, rot, out_grads)
    send = lax.ppermute(send, ("x_hi", "x_lo"), CROSS)
    keep = lax.ppermute(keep, ("x_hi", "x_lo"), TURN)
    piece = jnp.stack([keep, send])
    pieces, offsets = [piece], [0]
    up = down_ = piece
    for s in range(1, 4):
        up, down_ = shift(up, 1), shift(down_, -1)
        pieces += [up, down_]
        offsets += [-s, s]
    last = shift(up, 1)

    sums = early(ids, basis, pieces, offsets)
    (far,) = late(ids, basis, last, 4, sums, 0, 1, BF16)
    beside, across = late(ids, basis, last, 4, sums, 1, 2, BF16)
    (keep,) = late(ids, basis, last, 4, sums, 3, 1, F32)
    far = swap(far, "x_hi")
    beside = swap(beside, "x_lo")
    across = lax.ppermute(across, ("x_hi", "x_lo"), [(0, 3), (1, 2), (2, 1), (3, 0)])
    sums = pl.pallas_call(
        square_kernel,
        in_specs=[WHOLE] * 4,
        out_specs=WHOLE,
        out_shape=jax.ShapeDtypeStruct((8, 64, 256), BF16),
        compiler_params=params(),
    )(keep, far, beside, across)
    sums = lax.all_to_all(sums, "y", 0, 0)
    mean = pl.pallas_call(
        mean_kernel,
        in_specs=[WHOLE],
        out_specs=WHOLE,
        out_shape=jax.ShapeDtypeStruct((64, 256), F32),
        compiler_params=params(),
    )(sums)
    both = lax.ppermute(mean, ("x_hi", "core"), [(0, 3), (1, 2), (2, 1), (3, 0)])
    return pl.pallas_call(
        join_kernel,
        in_specs=[SCALARS] + [WHOLE] * 4,
        out_specs=WHOLE,
        out_shape=jax.ShapeDtypeStruct((64, 512), F32),
        compiler_params=params(),
    )(ids, mean, swap(mean, "core"), swap(mean, "x_hi"), both)


def solution(mesh):
    fine = Mesh(mesh.devices.reshape(SIZES), DP + EIGEN)
    return jax.shard_map(
        shards,
        mesh=fine,
        in_specs=(
            P(DP, None, EIGEN),
            P(DP, None, EIGEN),
            P(None, EIGEN),
            P(DP, EIGEN),
            P(),
        ),
        out_specs=P(None, EIGEN),
        check_vma=False,
    )
```

time: 169 us -> 158 us (0.935)
  blocking collectives: 51 us -> 15.8 us
  starting transfers between devices: 56.6 us -> 78.8 us
  waiting for transfers between devices: 32.5 us -> 34.4 us
    all_to_all x2 -> x1, blocking collectives: 51 us -> 15.8 us  [shards(): sums = lax.all_to_all(sums, 'y', 0, 0)]
    ppermute x2 -> x5, waiting for transfers between devices: 0.46 us -> 13.5 us  [the longest x1 6.22 us: shards(): turned = lax.ppermute(out_basis, ('core', 'x_lo'), TURN)]
    all_to_all x0 -> x1, starting transfers between devices: none -> 11.9 us  [shards(): parts = lax.all_to_all(parts, EIGEN, 0, 0)]
    ppermute x2 -> x5, starting transfers between devices: 7.64 us -> 16.7 us  [the longest x1 5.28 us: shards(): send = lax.ppermute(send, ('x_hi', 'x_lo'), CROSS)]
    ppermute x7, waiting for transfers between devices: 16.3 us -> 8.98 us  [shift(): return lax.ppermute(x, 'z', [(i, (i + step) % 8) for i in range(8)])]
    ppermute x5 -> x4, waiting for transfers between devices: 8.03 us -> 4.2 us  [swap(): return lax.ppermute(x, axis, [(i, i ^ stride) for i in range(size)])]
    ppermute x5 -> x4, starting transfers between devices: 21.1 us -> 23.6 us  [swap(): return lax.ppermute(x, axis, [(i, i ^ stride) for i in range(size)])]
    pallas_call x5 -> x7, Pallas kernels: 8.99 us -> 9.54 us  [the longest x1 3.11 us: project(): pl.pallas_call(project_kernel, in_specs=[HBM, HBM], out_specs=WHOLE, out_...]
  transfers between devices with their start and end apart: 16 -> 19, of which waited for: 9 -> 11; matrix products, arithmetic and copies ran while one was open for 0% -> 0% of each run, Pallas kernels for 4% -> 4%
where the time goes in v3:
time: 158 us; the launch traced here: 157 us
  starting transfers between devices  78.8 us (50%)
  waiting for transfers between devices  34.4 us (22%)
  blocking collectives  15.8 us (10%)
  between operations  13.7 us (9%)
  Pallas kernels  11.5 us (7%)
  local copies, waits for them, and re-layouts  2.89 us (2%)
    ppermute x4, starting transfers between devices, swap(): return lax.ppermute(x, axis, [(i, i ^ stride) for i in range(size)])  23.6 us
    ppermute x7, starting transfers between devices, shift(): return lax.ppermute(x, 'z', [(i, (i + step) % 8) for i in range(8)])  21.4 us
    all_to_all x1, blocking collectives, shards(): sums = lax.all_to_all(sums, 'y', 0, 0)  15.8 us
    all_to_all x1, starting transfers between devices, shards(): parts = lax.all_to_all(parts, EIGEN, 0, 0)  11.9 us
    ppermute x7, waiting for transfers between devices, shift(): return lax.ppermute(x, 'z', [(i, (i + step) % 8) for i in range(8)])  8.98 us
    all_to_all x1, waiting for transfers between devices, shards(): rot = lax.all_to_all(rotate(parts, adapter_basis), EIGEN, 0, 0)  7.71 us
    ppermute x1, waiting for transfers between devices, shards(): turned = lax.ppermute(out_basis, ('core', 'x_lo'), TURN)  6.22 us
    ppermute x1, starting transfers between devices, shards(): send = lax.ppermute(send, ('x_hi', 'x_lo'), CROSS)  5.28 us
  transfers between devices with their start and end apart: 19, of which 11 were waited for; matrix products, arithmetic and copies ran while one was open for 0% of the time, Pallas kernels for 4%

profile of v3, /device:TPU:1, one launch (start us, length us, event | category | flops | bytes accessed | tf_op | source)
XLA Modules:
  0.0 157.2 jit_solution(18270204634419346407)
XLA Ops:
  6.5 3.1 %shard_map.55 = bf16[16,64,128]{2,1,0:T(8,128)(2,1)} custom-call(bf16[64,512]{1,0:T(8,128)(2,1)} %a_ref.1, bf16[4,512,512]{2,1,0:T(8,128)(2,1)} %x_ref.1), custom_call_target="tpu_custom_call" | custom-call | flops 134217728 | bytes 3145728 | tf_op jit(solution)/shard_map/pallas_call | solution.py:50
  9.7 11.9 %all-to-all-start = ((bf16[16,64,128]{2,1,0:T(8,128)(2,1)}), bf16[16,64,128]{2,1,0:T(8,128)(2,1)S(1)}, u32[]{:S(2)}, u32[]{:S(2)}) async-start(bf16[16,64,128]{2,1,0:T(8,128)(2,1)} %shard_map.55), calls=%async_computation | async-start | bytes 524288 | tf_op jit(solution)/shard_map/all_to_all | solution.py:219
  21.6 4.4 %collective-permute-start = (bf16[256,512]{1,0:T(8,128)(2,1)S(1)}, bf16[256,512]{1,0:T(8,128)(2,1)S(1)}, u32[]{:S(2)}, u32[]{:S(2)}) collective-permute-start(bf16[256,512]{1,0:T(8,128)(2,1)S(1)} %copy-done.4), channel_id=1, source_target_pairs={{0,0},{8,16},{16,8},{24,24},{1,1},{9,17},{17,9},{25,25},{2,2},{10,... | collective-permute-start | bytes 786440 | tf_op jit(solution)/shard_map/ppermute | solution.py:217
  26.0 6.2 %collective-permute-done = bf16[256,512]{1,0:T(8,128)(2,1)S(1)} collective-permute-done((bf16[256,512]{1,0:T(8,128)(2,1)S(1)}, bf16[256,512]{1,0:T(8,128)(2,1)S(1)}, u32[]{:S(2)}, u32[]{:S(2)}) %collective-permute-start) | collective-permute-done | bytes 262176 | tf_op jit(solution)/shard_map/ppermute | solution.py:217
  33.9 5.2 %all-to-all-start.1 = ((bf16[16,64,128]{2,1,0:T(8,128)(2,1)}), bf16[16,64,128]{2,1,0:T(8,128)(2,1)S(1)}, u32[]{:S(2)}, u32[]{:S(2)}) async-start(bf16[16,64,128]{2,1,0:T(8,128)(2,1)} %shard_map.56), calls=%async_computation.1 | async-start | bytes 524288 | tf_op jit(solution)/shard_map/all_to_all | solution.py:222
  39.2 7.7 %all-to-all-done.1.rot_ref = bf16[16,64,128]{2,1,0:T(8,128)(2,1)S(1)} async-done(((bf16[16,64,128]{2,1,0:T(8,128)(2,1)}), bf16[16,64,128]{2,1,0:T(8,128)(2,1)S(1)}, u32[]{:S(2)}, u32[]{:S(2)}) %all-to-all-start.1) | async-done | bytes 262176 | tf_op jit(solution)/shard_map/all_to_all | solution.py:222
  46.9 1.0 shard_map.57
  48.6 5.3 %collective-permute-start.2 = (bf16[256,256]{1,0:T(8,128)(2,1)S(1)}, bf16[256,256]{1,0:T(8,128)(2,1)S(1)}, u32[]{:S(2)}, u32[]{:S(2)}) collective-permute-start(bf16[256,256]{1,0:T(8,128)(2,1)S(1)} %get-tuple-element.14), channel_id=1, source_target_pairs={{256,0},{0,8},{264,256},{8,264},{257,1},{1,9},{265,257},{9,265},{2... | collective-permute-start | bytes 393224 | tf_op jit(solution)/shard_map/ppermute | solution.py:225
  53.9 2.7 %collective-permute-done.2 = bf16[256,256]{1,0:T(8,128)(2,1)S(1)} collective-permute-done((bf16[256,256]{1,0:T(8,128)(2,1)S(1)}, bf16[256,256]{1,0:T(8,128)(2,1)S(1)}, u32[]{:S(2)}, u32[]{:S(2)}) %collective-permute-start.2) | collective-permute-done | bytes 131104 | tf_op jit(solution)/shard_map/ppermute | solution.py:225
  56.6 4.5 %collective-permute-start.3 = (bf16[2,256,256]{2,1,0:T(8,128)(2,1)S(1)}, bf16[2,256,256]{2,1,0:T(8,128)(2,1)S(1)}, u32[]{:S(2)}, u32[]{:S(2)}) collective-permute-start(bf16[2,256,256]{2,1,0:T(8,128)(2,1)S(1)} %pad_maximum_fusion.refs_0_), channel_id=1, source_target_pairs={{0,1},{1,2},{2,3},{3,4},{4,5},{5,6},{6,7},{7,0},{8,9},{9,10},{10,1... | collective-permute-start | bytes 786440 | tf_op jit(solution)/shard_map/ppermute | solution.py:205
  61.2 1.9 %collective-permute-start.7 = (bf16[2,256,256]{2,1,0:T(8,128)(2,1)S(1)}, bf16[2,256,256]{2,1,0:T(8,128)(2,1)S(1)}, u32[]{:S(2)}, u32[]{:S(2)}) collective-permute-start(bf16[2,256,256]{2,1,0:T(8,128)(2,1)S(1)} %pad_maximum_fusion.refs_0_), channel_id=1, source_target_pairs={{0,7},{1,0},{2,1},{3,2},{4,3},{5,4},{6,5},{7,6},{8,15},{9,8},{10,9... | collective-permute-start | bytes 786440 | tf_op jit(solution)/shard_map/ppermute | solution.py:205
  63.2 2.2 %collective-permute-done.3.refs_1_ = bf16[2,256,256]{2,1,0:T(8,128)(2,1)S(1)} collective-permute-done((bf16[2,256,256]{2,1,0:T(8,128)(2,1)S(1)}, bf16[2,256,256]{2,1,0:T(8,128)(2,1)S(1)}, u32[]{:S(2)}, u32[]{:S(2)}) %collective-permute-start.3) | collective-permute-done | bytes 262176 | tf_op jit(solution)/shard_map/ppermute | solution.py:205
  65.4 3.3 %collective-permute-start.4 = (bf16[2,256,256]{2,1,0:T(8,128)(2,1)S(1)}, bf16[2,256,256]{2,1,0:T(8,128)(2,1)S(1)}, u32[]{:S(2)}, u32[]{:S(2)}) collective-permute-start(bf16[2,256,256]{2,1,0:T(8,128)(2,1)S(1)} %collective-permute-done.3.refs_1_), channel_id=1, source_target_pairs={{0,1},{1,2},{2,3},{3,4},{4,5},{5,6},{6,7},{7,0},{8,9},{9,10},{10,1... | collective-permute-start | bytes 786440 | tf_op jit(solution)/shard_map/ppermute | solution.py:205
  68.7 3.2 %collective-permute-start.8 = (bf16[2,256,256]{2,1,0:T(8,128)(2,1)S(1)}, bf16[2,256,256]{2,1,0:T(8,128)(2,1)S(1)}, u32[]{:S(2)}, u32[]{:S(2)}) collective-permute-start(bf16[2,256,256]{2,1,0:T(8,128)(2,1)S(1)} %collective-permute-done.7.refs_2_), channel_id=1, source_target_pairs={{0,7},{1,0},{2,1},{3,2},{4,3},{5,4},{6,5},{7,6},{8,15},{9,8},{10,9... | collective-permute-start | bytes 786440 | tf_op jit(solution)/shard_map/ppermute | solution.py:205
  71.9 2.2 %collective-permute-done.4.refs_3_ = bf16[2,256,256]{2,1,0:T(8,128)(2,1)S(1)} collective-permute-done((bf16[2,256,256]{2,1,0:T(8,128)(2,1)S(1)}, bf16[2,256,256]{2,1,0:T(8,128)(2,1)S(1)}, u32[]{:S(2)}, u32[]{:S(2)}) %collective-permute-start.4) | collective-permute-done | bytes 262176 | tf_op jit(solution)/shard_map/ppermute | solution.py:205
  74.1 2.1 %collective-permute-start.5 = (bf16[2,256,256]{2,1,0:T(8,128)(2,1)S(1)}, bf16[2,256,256]{2,1,0:T(8,128)(2,1)S(1)}, u32[]{:S(2)}, u32[]{:S(2)}) collective-permute-start(bf16[2,256,256]{2,1,0:T(8,128)(2,1)S(1)} %collective-permute-done.4.refs_3_), channel_id=1, source_target_pairs={{0,1},{1,2},{2,3},{3,4},{4,5},{5,6},{6,7},{7,0},{8,9},{9,10},{10,1... | collective-permute-start | bytes 786440 | tf_op jit(solution)/shard_map/ppermute | solution.py:205
  76.2 4.4 %collective-permute-start.9 = (bf16[2,256,256]{2,1,0:T(8,128)(2,1)S(1)}, bf16[2,256,256]{2,1,0:T(8,128)(2,1)S(1)}, u32[]{:S(2)}, u32[]{:S(2)}) collective-permute-start(bf16[2,256,256]{2,1,0:T(8,128)(2,1)S(1)} %collective-permute-done.8.refs_4_), channel_id=1, source_target_pairs={{0,7},{1,0},{2,1},{3,2},{4,3},{5,4},{6,5},{7,6},{8,15},{9,8},{10,9... | collective-permute-start | bytes 786440 | tf_op jit(solution)/shard_map/ppermute | solution.py:205
  80.6 1.9 %collective-permute-done.5.refs_5_ = bf16[2,256,256]{2,1,0:T(8,128)(2,1)S(1)} collective-permute-done((bf16[2,256,256]{2,1,0:T(8,128)(2,1)S(1)}, bf16[2,256,256]{2,1,0:T(8,128)(2,1)S(1)}, u32[]{:S(2)}, u32[]{:S(2)}) %collective-permute-start.5) | collective-permute-done | bytes 262176 | tf_op jit(solution)/shard_map/ppermute | solution.py:205
  82.4 1.9 %collective-permute-start.6 = (bf16[2,256,256]{2,1,0:T(8,128)(2,1)S(1)}, bf16[2,256,256]{2,1,0:T(8,128)(2,1)S(1)}, u32[]{:S(2)}, u32[]{:S(2)}) collective-permute-start(bf16[2,256,256]{2,1,0:T(8,128)(2,1)S(1)} %collective-permute-done.5.refs_5_), channel_id=1, source_target_pairs={{0,1},{1,2},{2,3},{3,4},{4,5},{5,6},{6,7},{7,0},{8,9},{9,10},{10,1... | collective-permute-start | bytes 786440 | tf_op jit(solution)/shard_map/ppermute | solution.py:205
  84.4 2.2 %copy-done = bf16[4096,512]{1,0:T(8,128)(2,1)S(1)} copy-done((bf16[4096,512]{1,0:T(8,128)(2,1)S(1)}, bf16[4096,512]{1,0:T(8,128)(2,1)}, u32[]{:S(2)}) %copy-start) | copy-done | bytes 4194328
  86.6 2.6 %shard_map.58.sum_ref = f32[4,512,256]{2,1,0:T(8,128)S(1)} custom-call(s32[3]{0:T(128)S(1)} %pad_add_fusion.ids_ref, bf16[8,2,256,512]{3,2,1,0:T(8,128)(2,1)S(1)} %bitcast.6, bf16[2,256,256]{2,1,0:T(8,128)(2,1)S(1)} %pad_maximum_fusion.refs_0_, bf16[2,256,256]{2,1,0:T(8,128)(2,1)S(1)} %collective-permute-done.3.refs_1_, ...), custom_call_target="tpu_custom_call" | custom-call | flops 2147483648 | bytes 8388608 | tf_op jit(solution)/shard_map/pallas_call | solution.py:151
  89.2 2.7 %collective-permute-done.6.piece_ref = bf16[2,256,256]{2,1,0:T(8,128)(2,1)S(1)} collective-permute-done((bf16[2,256,256]{2,1,0:T(8,128)(2,1)S(1)}, bf16[2,256,256]{2,1,0:T(8,128)(2,1)S(1)}, u32[]{:S(2)}, u32[]{:S(2)}) %collective-permute-start.6) | collective-permute-done | bytes 262176 | tf_op jit(solution)/shard_map/ppermute | solution.py:205
  92.8 3.1 %collective-permute-start.11 = (bf16[512,256]{1,0:T(8,128)(2,1)S(1)}, bf16[512,256]{1,0:T(8,128)(2,1)S(1)}, u32[]{:S(2)}, u32[]{:S(2)}) collective-permute-start(bf16[512,256]{1,0:T(8,128)(2,1)S(1)} %get-tuple-element.15), channel_id=1, source_target_pairs={{0,8},{8,0},{1,9},{9,1},{2,10},{10,2},{3,11},{11,3},{4,12},{12,4},... | collective-permute-start | bytes 786440 | tf_op jit(solution)/shard_map/ppermute | solution.py:201
  95.9 2.8 %collective-permute-start.12 = (bf16[512,256]{1,0:T(8,128)(2,1)S(1)}, bf16[512,256]{1,0:T(8,128)(2,1)S(1)}, u32[]{:S(2)}, u32[]{:S(2)}) collective-permute-start(bf16[512,256]{1,0:T(8,128)(2,1)S(1)} %get-tuple-element.16), channel_id=1, source_target_pairs={{0,264},{8,256},{256,8},{264,0},{1,265},{9,257},{257,9},{265,1},{2... | collective-permute-start | bytes 786440 | tf_op jit(solution)/shard_map/ppermute | solution.py:242
  99.5 3.0 %collective-permute-start.10 = (bf16[512,256]{1,0:T(8,128)(2,1)S(1)}, bf16[512,256]{1,0:T(8,128)(2,1)S(1)}, u32[]{:S(2)}, u32[]{:S(2)}) collective-permute-start(bf16[512,256]{1,0:T(8,128)(2,1)S(1)} %shard_map.60), channel_id=1, source_target_pairs={{0,256},{256,0},{1,257},{257,1},{2,258},{258,2},{3,259},{259,3},{4... | collective-permute-start | bytes 786440 | tf_op jit(solution)/shard_map/ppermute | solution.py:201
  104.2 4.1 %collective-permute-done.10.b_ref = bf16[512,256]{1,0:T(8,128)(2,1)S(1)} collective-permute-done((bf16[512,256]{1,0:T(8,128)(2,1)S(1)}, bf16[512,256]{1,0:T(8,128)(2,1)S(1)}, u32[]{:S(2)}, u32[]{:S(2)}) %collective-permute-start.10) | collective-permute-done | bytes 262176 | tf_op jit(solution)/shard_map/ppermute | solution.py:201
  108.4 15.8 %all_to_all.15.p_ref = bf16[8,64,256]{2,1,0:T(8,128)(2,1)S(1)} all-to-all(bf16[8,64,256]{2,1,0:T(8,128)(2,1)S(1)} %shard_map.62), channel_id=1, replica_groups=mesh['x_hi'=2,'y'=8,'core'=2,'x_lo'=2,'z'=8] {'y'}, dimensions={0} | all-to-all | bytes 524288 | tf_op jit(solution)/shard_map/all_to_all | solution.py:250
  124.3 14.0 %collective-permute-start.13 = (f32[64,256]{1,0:T(8,128)S(1)}, f32[64,256]{1,0:T(8,128)S(1)}, u32[]{:S(2)}, u32[]{:S(2)}) collective-permute-start(f32[64,256]{1,0:T(8,128)S(1)} %shard_map.63.own_ref), channel_id=1, source_target_pairs={{0,16},{16,0},{1,17},{17,1},{2,18},{18,2},{3,19},{19,3},{4,20},{20... | collective-permute-start | bytes 196616 | tf_op jit(solution)/shard_map/ppermute | solution.py:201
  138.3 3.4 %collective-permute-start.14 = (f32[64,256]{1,0:T(8,128)S(1)}, f32[64,256]{1,0:T(8,128)S(1)}, u32[]{:S(2)}, u32[]{:S(2)}) collective-permute-start(f32[64,256]{1,0:T(8,128)S(1)} %shard_map.63.own_ref), channel_id=1, source_target_pairs={{0,256},{256,0},{1,257},{257,1},{2,258},{258,2},{3,259},{259,3},{4... | collective-permute-start | bytes 196616 | tf_op jit(solution)/shard_map/ppermute | solution.py:201
  141.8 3.6 %collective-permute-start.15 = (f32[64,256]{1,0:T(8,128)S(1)}, f32[64,256]{1,0:T(8,128)S(1)}, u32[]{:S(2)}, u32[]{:S(2)}) collective-permute-start(f32[64,256]{1,0:T(8,128)S(1)} %shard_map.63.own_ref), channel_id=1, source_target_pairs={{0,272},{16,256},{256,16},{272,0},{1,273},{17,257},{257,17},{273,1... | collective-permute-start | bytes 196616 | tf_op jit(solution)/shard_map/ppermute | solution.py:258
  145.5 3.7 %collective-permute-done.15.both_ref = f32[64,256]{1,0:T(8,128)S(1)} collective-permute-done((f32[64,256]{1,0:T(8,128)S(1)}, f32[64,256]{1,0:T(8,128)S(1)}, u32[]{:S(2)}, u32[]{:S(2)}) %collective-permute-start.15) | collective-permute-done | bytes 65568 | tf_op jit(solution)/shard_map/ppermute | solution.py:258
  149.2 1.2 shard_map.64
  (30 shorter events, 6.1 us)
Async XLA Ops:
  6.5 15.1 %copy-start.4 = (bf16[256,512]{1,0:T(8,128)(2,1)S(1)}, bf16[256,512]{1,0:T(8,128)(2,1)}, u32[]{:S(2)}) copy-start(bf16[256,512]{1,0:T(8,128)(2,1)} %param.8) | copy-start | bytes 786436
  6.5 26.4 %copy-start.2 = (bf16[64,64]{1,0:T(8,128)(2,1)S(1)}, bf16[64,64]{1,0:T(8,128)(2,1)}, u32[]{:S(2)}) copy-start(bf16[64,64]{1,0:T(8,128)(2,1)} %e_ref.1) | copy-start | bytes 24580
  6.5 40.3 %copy-start.1 = (bf16[4,512,512]{2,1,0:T(8,128)(2,1)S(1)}, bf16[4,512,512]{2,1,0:T(8,128)(2,1)}, u32[]{:S(2)}) copy-start(bf16[4,512,512]{2,1,0:T(8,128)(2,1)} %dy_ref.1) | copy-start | bytes 6291460
  9.7 22.6 %all-to-all-start = ((bf16[16,64,128]{2,1,0:T(8,128)(2,1)}), bf16[16,64,128]{2,1,0:T(8,128)(2,1)S(1)}, u32[]{:S(2)}, u32[]{:S(2)}) async-start(bf16[16,64,128]{2,1,0:T(8,128)(2,1)} %shard_map.55), calls=%async_computation | async-start | bytes 524288 | tf_op jit(solution)/shard_map/all_to_all | solution.py:219
  21.6 62.8 %all-gather.3.cloned.1.call-start = ((), (), s32[]{:S(2)}) async-start(), calls=%async_computation.3 | async-start | bytes 4456448 | tf_op jit(solution)/shard_map/all_gather | solution.py:221
  21.6 10.6 %collective-permute-start = (bf16[256,512]{1,0:T(8,128)(2,1)S(1)}, bf16[256,512]{1,0:T(8,128)(2,1)S(1)}, u32[]{:S(2)}, u32[]{:S(2)}) collective-permute-start(bf16[256,512]{1,0:T(8,128)(2,1)S(1)} %copy-done.4), channel_id=1, source_target_pairs={{0,0},{8,16},{16,8},{24,24},{1,1},{9,17},{17,9},{25,25},{2,2},{10,... | collective-permute-start | bytes 786440 | tf_op jit(solution)/shard_map/ppermute | solution.py:217
  32.2 0.7 copy-start.3
  33.9 13.0 %all-to-all-start.1 = ((bf16[16,64,128]{2,1,0:T(8,128)(2,1)}), bf16[16,64,128]{2,1,0:T(8,128)(2,1)S(1)}, u32[]{:S(2)}, u32[]{:S(2)}) async-start(bf16[16,64,128]{2,1,0:T(8,128)(2,1)} %shard_map.56), calls=%async_computation.1 | async-start | bytes 524288 | tf_op jit(solution)/shard_map/all_to_all | solution.py:222
  47.9 6.0 %collective-permute-start.1 = (bf16[256,256]{1,0:T(8,128)(2,1)S(1)}, bf16[256,256]{1,0:T(8,128)(2,1)S(1)}, u32[]{:S(2)}, u32[]{:S(2)}) collective-permute-start(bf16[256,256]{1,0:T(8,128)(2,1)S(1)} %get-tuple-element.13), channel_id=1, source_target_pairs={{0,0},{8,256},{256,8},{264,264},{1,1},{9,257},{257,9},{265,265},{2... | collective-permute-start | bytes 393224 | tf_op jit(solution)/shard_map/ppermute | solution.py:226
  48.6 8.0 %collective-permute-start.2 = (bf16[256,256]{1,0:T(8,128)(2,1)S(1)}, bf16[256,256]{1,0:T(8,128)(2,1)S(1)}, u32[]{:S(2)}, u32[]{:S(2)}) collective-permute-start(bf16[256,256]{1,0:T(8,128)(2,1)S(1)} %get-tuple-element.14), channel_id=1, source_target_pairs={{256,0},{0,8},{264,256},{8,264},{257,1},{1,9},{265,257},{9,265},{2... | collective-permute-start | bytes 393224 | tf_op jit(solution)/shard_map/ppermute | solution.py:225
  56.6 8.7 %collective-permute-start.3 = (bf16[2,256,256]{2,1,0:T(8,128)(2,1)S(1)}, bf16[2,256,256]{2,1,0:T(8,128)(2,1)S(1)}, u32[]{:S(2)}, u32[]{:S(2)}) collective-permute-start(bf16[2,256,256]{2,1,0:T(8,128)(2,1)S(1)} %pad_maximum_fusion.refs_0_), channel_id=1, source_target_pairs={{0,1},{1,2},{2,3},{3,4},{4,5},{5,6},{6,7},{7,0},{8,9},{9,10},{10,1... | collective-permute-start | bytes 786440 | tf_op jit(solution)/shard_map/ppermute | solution.py:205
  61.2 7.5 %collective-permute-start.7 = (bf16[2,256,256]{2,1,0:T(8,128)(2,1)S(1)}, bf16[2,256,256]{2,1,0:T(8,128)(2,1)S(1)}, u32[]{:S(2)}, u32[]{:S(2)}) collective-permute-start(bf16[2,256,256]{2,1,0:T(8,128)(2,1)S(1)} %pad_maximum_fusion.refs_0_), channel_id=1, source_target_pairs={{0,7},{1,0},{2,1},{3,2},{4,3},{5,4},{6,5},{7,6},{8,15},{9,8},{10,9... | collective-permute-start | bytes 786440 | tf_op jit(solution)/shard_map/ppermute | solution.py:205
  65.4 8.7 %collective-permute-start.4 = (bf16[2,256,256]{2,1,0:T(8,128)(2,1)S(1)}, bf16[2,256,256]{2,1,0:T(8,128)(2,1)S(1)}, u32[]{:S(2)}, u32[]{:S(2)}) collective-permute-start(bf16[2,256,256]{2,1,0:T(8,128)(2,1)S(1)} %collective-permute-done.3.refs_1_), channel_id=1, source_target_pairs={{0,1},{1,2},{2,3},{3,4},{4,5},{5,6},{6,7},{7,0},{8,9},{9,10},{10,1... | collective-permute-start | bytes 786440 | tf_op jit(solution)/shard_map/ppermute | solution.py:205
  68.7 7.5 %collective-permute-start.8 = (bf16[2,256,256]{2,1,0:T(8,128)(2,1)S(1)}, bf16[2,256,256]{2,1,0:T(8,128)(2,1)S(1)}, u32[]{:S(2)}, u32[]{:S(2)}) collective-permute-start(bf16[2,256,256]{2,1,0:T(8,128)(2,1)S(1)} %collective-permute-done.7.refs_2_), channel_id=1, source_target_pairs={{0,7},{1,0},{2,1},{3,2},{4,3},{5,4},{6,5},{7,6},{8,15},{9,8},{10,9... | collective-permute-start | bytes 786440 | tf_op jit(solution)/shard_map/ppermute | solution.py:205
  74.1 8.4 %collective-permute-start.5 = (bf16[2,256,256]{2,1,0:T(8,128)(2,1)S(1)}, bf16[2,256,256]{2,1,0:T(8,128)(2,1)S(1)}, u32[]{:S(2)}, u32[]{:S(2)}) collective-permute-start(bf16[2,256,256]{2,1,0:T(8,128)(2,1)S(1)} %collective-permute-done.4.refs_3_), channel_id=1, source_target_pairs={{0,1},{1,2},{2,3},{3,4},{4,5},{5,6},{6,7},{7,0},{8,9},{9,10},{10,1... | collective-permute-start | bytes 786440 | tf_op jit(solution)/shard_map/ppermute | solution.py:205
  76.2 8.1 %collective-permute-start.9 = (bf16[2,256,256]{2,1,0:T(8,128)(2,1)S(1)}, bf16[2,256,256]{2,1,0:T(8,128)(2,1)S(1)}, u32[]{:S(2)}, u32[]{:S(2)}) collective-permute-start(bf16[2,256,256]{2,1,0:T(8,128)(2,1)S(1)} %collective-permute-done.8.refs_4_), channel_id=1, source_target_pairs={{0,7},{1,0},{2,1},{3,2},{4,3},{5,4},{6,5},{7,6},{8,15},{9,8},{10,9... | collective-permute-start | bytes 786440 | tf_op jit(solution)/shard_map/ppermute | solution.py:205
  82.4 9.5 %collective-permute-start.6 = (bf16[2,256,256]{2,1,0:T(8,128)(2,1)S(1)}, bf16[2,256,256]{2,1,0:T(8,128)(2,1)S(1)}, u32[]{:S(2)}, u32[]{:S(2)}) collective-permute-start(bf16[2,256,256]{2,1,0:T(8,128)(2,1)S(1)} %collective-permute-done.5.refs_5_), channel_id=1, source_target_pairs={{0,1},{1,2},{2,3},{3,4},{4,5},{5,6},{6,7},{7,0},{8,9},{9,10},{10,1... | collective-permute-start | bytes 786440 | tf_op jit(solution)/shard_map/ppermute | solution.py:205
  84.4 2.2 %copy-start = (bf16[4096,512]{1,0:T(8,128)(2,1)S(1)}, bf16[4096,512]{1,0:T(8,128)(2,1)}, u32[]{:S(2)}) copy-start(bf16[4096,512]{1,0:T(8,128)(2,1)} %all-gather.3.cloned.1.call-done) | copy-start | bytes 12582916
  92.8 10.6 %collective-permute-start.11 = (bf16[512,256]{1,0:T(8,128)(2,1)S(1)}, bf16[512,256]{1,0:T(8,128)(2,1)S(1)}, u32[]{:S(2)}, u32[]{:S(2)}) collective-permute-start(bf16[512,256]{1,0:T(8,128)(2,1)S(1)} %get-tuple-element.15), channel_id=1, source_target_pairs={{0,8},{8,0},{1,9},{9,1},{2,10},{10,2},{3,11},{11,3},{4,12},{12,4},... | collective-permute-start | bytes 786440 | tf_op jit(solution)/shard_map/ppermute | solution.py:201
  95.9 8.3 %collective-permute-start.12 = (bf16[512,256]{1,0:T(8,128)(2,1)S(1)}, bf16[512,256]{1,0:T(8,128)(2,1)S(1)}, u32[]{:S(2)}, u32[]{:S(2)}) collective-permute-start(bf16[512,256]{1,0:T(8,128)(2,1)S(1)} %get-tuple-element.16), channel_id=1, source_target_pairs={{0,264},{8,256},{256,8},{264,0},{1,265},{9,257},{257,9},{265,1},{2... | collective-permute-start | bytes 786440 | tf_op jit(solution)/shard_map/ppermute | solution.py:242
  99.5 8.8 %collective-permute-start.10 = (bf16[512,256]{1,0:T(8,128)(2,1)S(1)}, bf16[512,256]{1,0:T(8,128)(2,1)S(1)}, u32[]{:S(2)}, u32[]{:S(2)}) collective-permute-start(bf16[512,256]{1,0:T(8,128)(2,1)S(1)} %shard_map.60), channel_id=1, source_target_pairs={{0,256},{256,0},{1,257},{257,1},{2,258},{258,2},{3,259},{259,3},{4... | collective-permute-start | bytes 786440 | tf_op jit(solution)/shard_map/ppermute | solution.py:201
  124.3 21.0 %collective-permute-start.13 = (f32[64,256]{1,0:T(8,128)S(1)}, f32[64,256]{1,0:T(8,128)S(1)}, u32[]{:S(2)}, u32[]{:S(2)}) collective-permute-start(f32[64,256]{1,0:T(8,128)S(1)} %shard_map.63.own_ref), channel_id=1, source_target_pairs={{0,16},{16,0},{1,17},{17,1},{2,18},{18,2},{3,19},{19,3},{4,20},{20... | collective-permute-start | bytes 196616 | tf_op jit(solution)/shard_map/ppermute | solution.py:201
  138.3 7.1 %collective-permute-start.14 = (f32[64,256]{1,0:T(8,128)S(1)}, f32[64,256]{1,0:T(8,128)S(1)}, u32[]{:S(2)}, u32[]{:S(2)}) collective-permute-start(f32[64,256]{1,0:T(8,128)S(1)} %shard_map.63.own_ref), channel_id=1, source_target_pairs={{0,256},{256,0},{1,257},{257,1},{2,258},{258,2},{3,259},{259,3},{4... | collective-permute-start | bytes 196616 | tf_op jit(solution)/shard_map/ppermute | solution.py:201
  141.8 7.4 %collective-permute-start.15 = (f32[64,256]{1,0:T(8,128)S(1)}, f32[64,256]{1,0:T(8,128)S(1)}, u32[]{:S(2)}, u32[]{:S(2)}) collective-permute-start(f32[64,256]{1,0:T(8,128)S(1)} %shard_map.63.own_ref), channel_id=1, source_target_pairs={{0,272},{16,256},{256,16},{272,0},{1,273},{17,257},{257,17},{273,1... | collective-permute-start | bytes 196616 | tf_op jit(solution)/shard_map/ppermute | solution.py:258
Sparse Core Ops, SparseCore 0:
  33.1 44.1 all-gather.2

commit v4 on v3

--- a/solution.py
+++ b/solution.py
@@ -141,10 +141,14 @@
         out[i, rows, :] = total
 
 
-def late_kernel(offset, first, count, ids_ref, q_ref, piece_ref, sum_ref, *outs):
-    dests = DESTS[first : first + count]
-    for i, rows, total in coef_parts(ids_ref, q_ref, [piece_ref], [offset], dests):
-        outs[i][rows, :] = (sum_ref[first + i, rows, :] + total).astype(outs[i].dtype)
+def late_kernel(offset, ids_ref, q_ref, piece_ref, sum_ref, away_ref, keep_ref):
+    for i, rows, total in coef_parts(ids_ref, q_ref, [piece_ref], [offset], DESTS):
+        total = sum_ref[i, rows, :] + total
+        if i == 3:
+            keep_ref[rows, :] = total
+        hi, lo = DESTS[i]
+        slot = (1 - ids_ref[1] if hi else ids_ref[1]) * 2 + (1 - ids_ref[2] if lo else ids_ref[2])
+        away_ref[slot, rows, :] = total.astype(BF16)
 
 
 def early(ids, basis, pieces, offsets):
@@ -158,19 +162,27 @@
     )(ids, basis, *pieces)
 
 
-def late(ids, basis, piece, offset, sums, first, count, dtype):
-    return pl.pallas_call(
-        functools.partial(late_kernel, offset, first, count),
+def late(ids, basis, piece, offset, sums):
+    return pl.pallas_call(
+        functools.partial(late_kernel, offset),
         in_specs=[SCALARS] + [WHOLE] * 3,
-        out_specs=[WHOLE] * count,
-        out_shape=[jax.ShapeDtypeStruct(COEF, dtype)] * count,
+        out_specs=[WHOLE] * 2,
+        out_shape=[
+            jax.ShapeDtypeStruct((4,) + COEF, BF16),
+            jax.ShapeDtypeStruct(COEF, F32),
+        ],
         compiler_params=params(),
         cost_estimate=pl.CostEstimate(flops=1 << 28, bytes_accessed=2 << 20, transcendentals=0),
     )(ids, basis, piece, sums)
 
 
-def square_kernel(a_ref, b_ref, c_ref, d_ref, o_ref):
-    coef = (a_ref[...] + b_ref[...].astype(F32)) + (c_ref[...].astype(F32) + d_ref[...].astype(F32))
+def square_kernel(ids_ref, keep_ref, p_ref, o_ref):
+    x_hi, x_lo = ids_ref[1], ids_ref[2]
+    far, beside = 2 * (1 - x_hi) + x_lo, 2 * x_hi + 1 - x_lo
+    across = 2 * (1 - x_hi) + 1 - x_lo
+    coef = keep_ref[...]
+    for slot in (far, beside, across):
+        coef = coef + p_ref[slot].astype(F32)
     sq = coef * coef
     rank = o_ref.shape[1]
     total = sq[:rank]
@@ -185,15 +197,15 @@
     total = p_ref[0].astype(F32)
     for i in range(1, p_ref.shape[0]):
         total = total + p_ref[i].astype(F32)
-    o_ref[...] = total * (1.0 / 128)
-
-
-def join_kernel(ids_ref, own_ref, core_ref, hi_ref, both_ref, o_ref):
-    first = ids_ref[1] == 0
-    own, other = own_ref[...] + core_ref[...], hi_ref[...] + both_ref[...]
-    half = own.shape[1]
-    o_ref[:, :half] = jnp.where(first, own, other)
-    o_ref[:, half:] = jnp.where(first, other, own)
+    total = total * (1.0 / 128)
+    for i in range(o_ref.shape[0]):
+        o_ref[i] = total
+
+
+def join_kernel(p_ref, o_ref):
+    half = p_ref.shape[2]
+    for h in range(2):
+        o_ref[:, h * half : (h + 1) * half] = p_ref[2 * h] + p_ref[2 * h + 1]
 
 
 def swap(x, axis, stride=1):
@@ -234,35 +246,31 @@
     last = shift(up, 1)
 
     sums = early(ids, basis, pieces, offsets)
-    (far,) = late(ids, basis, last, 4, sums, 0, 1, BF16)
-    beside, across = late(ids, basis, last, 4, sums, 1, 2, BF16)
-    (keep,) = late(ids, basis, last, 4, sums, 3, 1, F32)
-    far = swap(far, "x_hi")
-    beside = swap(beside, "x_lo")
-    across = lax.ppermute(across, ("x_hi", "x_lo"), [(0, 3), (1, 2), (2, 1), (3, 0)])
+    away, keep = late(ids, basis, last, 4, sums)
+    away = lax.all_to_all(away, ("x_hi", "x_lo"), 0, 0)
     sums = pl.pallas_call(
         square_kernel,
-        in_specs=[WHOLE] * 4,
+        in_specs=[SCALARS] + [WHOLE] * 2,
         out_specs=WHOLE,
         out_shape=jax.ShapeDtypeStruct((8, 64, 256), BF16),
         compiler_params=params(),
-    )(keep, far, beside, across)
+    )(ids, keep, away)
     sums = lax.all_to_all(sums, "y", 0, 0)
     mean = pl.pallas_call(
         mean_kernel,
         in_specs=[WHOLE],
         out_specs=WHOLE,
-        out_shape=jax.ShapeDtypeStruct((64, 256), F32),
+        out_shape=jax.ShapeDtypeStruct((4, 64, 256), F32),
         compiler_params=params(),
     )(sums)
-    both = lax.ppermute(mean, ("x_hi", "core"), [(0, 3), (1, 2), (2, 1), (3, 0)])
+    mean = lax.all_to_all(mean, ("x_hi", "core"), 0, 0)
     return pl.pallas_call(
         join_kernel,
-        in_specs=[SCALARS] + [WHOLE] * 4,
+        in_specs=[WHOLE],
         out_specs=WHOLE,
         out_shape=jax.ShapeDtypeStruct((64, 512), F32),
         compiler_params=params(),
-    )(ids, mean, swap(mean, "core"), swap(mean, "x_hi"), both)
+    )(mean)
 
 
 def solution(mesh):

time: 158 us -> 151 us (0.956)
  blocking collectives: 15.8 us -> 49.4 us
  starting transfers between devices: 78.8 us -> 48.8 us
  waiting for transfers between devices: 34.4 us -> 25.7 us
    all_to_all x0 -> x2, blocking collectives: none -> 33.4 us  [the longest x1 20.5 us: shards(): mean = lax.all_to_all(mean, ('x_hi', 'core'), 0, 0)]
    ppermute x6 -> x0, starting transfers between devices: 30 us -> none  [the longest x4 23.6 us: swap(): return lax.ppermute(x, axis, [(i, i ^ stride) for i in range(size)])]
    ppermute x6 -> x0, waiting for transfers between devices: 8.72 us -> none  [the longest x4 4.2 us: swap(): return lax.ppermute(x, axis, [(i, i ^ stride) for i in range(size)])]
    pallas_call x5 -> x3, Pallas kernels: 3.81 us -> 2.38 us  [the longest x1 1.02 us: late(): pl.pallas_call(functools.partial(late_kernel, offset), in_specs=[SCALARS]...]
  transfers between devices with their start and end apart: 19 -> 13, of which waited for: 11 -> 7; matrix products, arithmetic and copies ran while one was open for 0% -> 0% of each run, Pallas kernels for 4% -> 3%
where the time goes in v4:
time: 151 us
  blocking collectives  49.4 us (33%)
  starting transfers between devices  48.8 us (32%)
  waiting for transfers between devices  25.7 us (17%)
  between operations  13.6 us (9%)
  Pallas kernels  10.1 us (7%)
  local copies, waits for them, and re-layouts  2.9 us (2%)
    ppermute x7, starting transfers between devices, shift(): return lax.ppermute(x, 'z', [(i, (i + step) % 8) for i in range(8)])  21.4 us
    all_to_all x1, blocking collectives, shards(): mean = lax.all_to_all(mean, ('x_hi', 'core'), 0, 0)  20.5 us
    all_to_all x1, blocking collectives, shards(): sums = lax.all_to_all(sums, 'y', 0, 0)  15.9 us
    all_to_all x1, blocking collectives, shards(): away = lax.all_to_all(away, ('x_hi', 'x_lo'), 0, 0)  12.9 us
    all_to_all x1, starting transfers between devices, shards(): parts = lax.all_to_all(parts, EIGEN, 0, 0)  11.9 us
    ppermute x7, waiting for transfers between devices, shift(): return lax.ppermute(x, 'z', [(i, (i + step) % 8) for i in range(8)])  8.98 us
    all_to_all x1, waiting for transfers between devices, shards(): rot = lax.all_to_all(rotate(parts, adapter_basis), EIGEN, 0, 0)  7.71 us
    ppermute x1, waiting for transfers between devices, shards(): turned = lax.ppermute(out_basis, ('core', 'x_lo'), TURN)  6.22 us
  transfers between devices with their start and end apart: 13, of which 7 were waited for; matrix products, arithmetic and copies ran while one was open for 0% of the time, Pallas kernels for 3%

profile of v4, /device:TPU:1, one launch (start us, length us, event | category | flops | bytes accessed | tf_op | source)
XLA Modules:
  0.0 150.6 jit_solution(18234606010253338319)
XLA Ops:
  6.5 3.1 %shard_map.55 = bf16[16,64,128]{2,1,0:T(8,128)(2,1)} custom-call(bf16[64,512]{1,0:T(8,128)(2,1)} %a_ref.1, bf16[4,512,512]{2,1,0:T(8,128)(2,1)} %x_ref.1), custom_call_target="tpu_custom_call" | custom-call | flops 134217728 | bytes 3145728 | tf_op jit(solution)/shard_map/pallas_call | solution.py:50
  9.7 11.9 %all-to-all-start = ((bf16[16,64,128]{2,1,0:T(8,128)(2,1)}), bf16[16,64,128]{2,1,0:T(8,128)(2,1)S(1)}, u32[]{:S(2)}, u32[]{:S(2)}) async-start(bf16[16,64,128]{2,1,0:T(8,128)(2,1)} %shard_map.55), calls=%async_computation | async-start | bytes 524288 | tf_op jit(solution)/shard_map/all_to_all | solution.py:231
  21.6 4.4 %collective-permute-start = (bf16[256,512]{1,0:T(8,128)(2,1)S(1)}, bf16[256,512]{1,0:T(8,128)(2,1)S(1)}, u32[]{:S(2)}, u32[]{:S(2)}) collective-permute-start(bf16[256,512]{1,0:T(8,128)(2,1)S(1)} %copy-done.4), channel_id=1, source_target_pairs={{0,0},{8,16},{16,8},{24,24},{1,1},{9,17},{17,9},{25,25},{2,2},{10,... | collective-permute-start | bytes 786440 | tf_op jit(solution)/shard_map/ppermute | solution.py:229
  26.0 6.2 %collective-permute-done = bf16[256,512]{1,0:T(8,128)(2,1)S(1)} collective-permute-done((bf16[256,512]{1,0:T(8,128)(2,1)S(1)}, bf16[256,512]{1,0:T(8,128)(2,1)S(1)}, u32[]{:S(2)}, u32[]{:S(2)}) %collective-permute-start) | collective-permute-done | bytes 262176 | tf_op jit(solution)/shard_map/ppermute | solution.py:229
  32.3 0.7 copy-done.3
  33.0 0.9 shard_map.56
  33.9 5.2 %all-to-all-start.1 = ((bf16[16,64,128]{2,1,0:T(8,128)(2,1)}), bf16[16,64,128]{2,1,0:T(8,128)(2,1)S(1)}, u32[]{:S(2)}, u32[]{:S(2)}) async-start(bf16[16,64,128]{2,1,0:T(8,128)(2,1)} %shard_map.56), calls=%async_computation.1 | async-start | bytes 524288 | tf_op jit(solution)/shard_map/all_to_all | solution.py:234
  39.1 0.1 pad_add_fusion.ids_ref
  39.2 7.7 %all-to-all-done.1.rot_ref = bf16[16,64,128]{2,1,0:T(8,128)(2,1)S(1)} async-done(((bf16[16,64,128]{2,1,0:T(8,128)(2,1)}), bf16[16,64,128]{2,1,0:T(8,128)(2,1)S(1)}, u32[]{:S(2)}, u32[]{:S(2)}) %all-to-all-start.1) | async-done | bytes 262176 | tf_op jit(solution)/shard_map/all_to_all | solution.py:234
  46.9 1.0 shard_map.57
  47.9 0.7 collective-permute-start.1
  48.6 5.3 %collective-permute-start.2 = (bf16[256,256]{1,0:T(8,128)(2,1)S(1)}, bf16[256,256]{1,0:T(8,128)(2,1)S(1)}, u32[]{:S(2)}, u32[]{:S(2)}) collective-permute-start(bf16[256,256]{1,0:T(8,128)(2,1)S(1)} %get-tuple-element.14), channel_id=1, source_target_pairs={{256,0},{0,8},{264,256},{8,264},{257,1},{1,9},{265,257},{9,265},{2... | collective-permute-start | bytes 393224 | tf_op jit(solution)/shard_map/ppermute | solution.py:237
  53.9 2.7 %collective-permute-done.2 = bf16[256,256]{1,0:T(8,128)(2,1)S(1)} collective-permute-done((bf16[256,256]{1,0:T(8,128)(2,1)S(1)}, bf16[256,256]{1,0:T(8,128)(2,1)S(1)}, u32[]{:S(2)}, u32[]{:S(2)}) %collective-permute-start.2) | collective-permute-done | bytes 131104 | tf_op jit(solution)/shard_map/ppermute | solution.py:237
  56.7 4.5 %collective-permute-start.3 = (bf16[2,256,256]{2,1,0:T(8,128)(2,1)S(1)}, bf16[2,256,256]{2,1,0:T(8,128)(2,1)S(1)}, u32[]{:S(2)}, u32[]{:S(2)}) collective-permute-start(bf16[2,256,256]{2,1,0:T(8,128)(2,1)S(1)} %pad_maximum_fusion.refs_0_), channel_id=1, source_target_pairs={{0,1},{1,2},{2,3},{3,4},{4,5},{5,6},{6,7},{7,0},{8,9},{9,10},{10,1... | collective-permute-start | bytes 786440 | tf_op jit(solution)/shard_map/ppermute | solution.py:217
  61.2 1.9 %collective-permute-start.7 = (bf16[2,256,256]{2,1,0:T(8,128)(2,1)S(1)}, bf16[2,256,256]{2,1,0:T(8,128)(2,1)S(1)}, u32[]{:S(2)}, u32[]{:S(2)}) collective-permute-start(bf16[2,256,256]{2,1,0:T(8,128)(2,1)S(1)} %pad_maximum_fusion.refs_0_), channel_id=1, source_target_pairs={{0,7},{1,0},{2,1},{3,2},{4,3},{5,4},{6,5},{7,6},{8,15},{9,8},{10,9... | collective-permute-start | bytes 786440 | tf_op jit(solution)/shard_map/ppermute | solution.py:217
  63.2 2.2 %collective-permute-done.3.refs_1_ = bf16[2,256,256]{2,1,0:T(8,128)(2,1)S(1)} collective-permute-done((bf16[2,256,256]{2,1,0:T(8,128)(2,1)S(1)}, bf16[2,256,256]{2,1,0:T(8,128)(2,1)S(1)}, u32[]{:S(2)}, u32[]{:S(2)}) %collective-permute-start.3) | collective-permute-done | bytes 262176 | tf_op jit(solution)/shard_map/ppermute | solution.py:217
  65.4 3.3 %collective-permute-start.4 = (bf16[2,256,256]{2,1,0:T(8,128)(2,1)S(1)}, bf16[2,256,256]{2,1,0:T(8,128)(2,1)S(1)}, u32[]{:S(2)}, u32[]{:S(2)}) collective-permute-start(bf16[2,256,256]{2,1,0:T(8,128)(2,1)S(1)} %collective-permute-done.3.refs_1_), channel_id=1, source_target_pairs={{0,1},{1,2},{2,3},{3,4},{4,5},{5,6},{6,7},{7,0},{8,9},{9,10},{10,1... | collective-permute-start | bytes 786440 | tf_op jit(solution)/shard_map/ppermute | solution.py:217
  68.7 3.2 %collective-permute-start.8 = (bf16[2,256,256]{2,1,0:T(8,128)(2,1)S(1)}, bf16[2,256,256]{2,1,0:T(8,128)(2,1)S(1)}, u32[]{:S(2)}, u32[]{:S(2)}) collective-permute-start(bf16[2,256,256]{2,1,0:T(8,128)(2,1)S(1)} %collective-permute-done.7.refs_2_), channel_id=1, source_target_pairs={{0,7},{1,0},{2,1},{3,2},{4,3},{5,4},{6,5},{7,6},{8,15},{9,8},{10,9... | collective-permute-start | bytes 786440 | tf_op jit(solution)/shard_map/ppermute | solution.py:217
  71.9 2.2 %collective-permute-done.4.refs_3_ = bf16[2,256,256]{2,1,0:T(8,128)(2,1)S(1)} collective-permute-done((bf16[2,256,256]{2,1,0:T(8,128)(2,1)S(1)}, bf16[2,256,256]{2,1,0:T(8,128)(2,1)S(1)}, u32[]{:S(2)}, u32[]{:S(2)}) %collective-permute-start.4) | collective-permute-done | bytes 262176 | tf_op jit(solution)/shard_map/ppermute | solution.py:217
  74.1 2.1 %collective-permute-start.5 = (bf16[2,256,256]{2,1,0:T(8,128)(2,1)S(1)}, bf16[2,256,256]{2,1,0:T(8,128)(2,1)S(1)}, u32[]{:S(2)}, u32[]{:S(2)}) collective-permute-start(bf16[2,256,256]{2,1,0:T(8,128)(2,1)S(1)} %collective-permute-done.4.refs_3_), channel_id=1, source_target_pairs={{0,1},{1,2},{2,3},{3,4},{4,5},{5,6},{6,7},{7,0},{8,9},{9,10},{10,1... | collective-permute-start | bytes 786440 | tf_op jit(solution)/shard_map/ppermute | solution.py:217
  76.2 4.4 %collective-permute-start.9 = (bf16[2,256,256]{2,1,0:T(8,128)(2,1)S(1)}, bf16[2,256,256]{2,1,0:T(8,128)(2,1)S(1)}, u32[]{:S(2)}, u32[]{:S(2)}) collective-permute-start(bf16[2,256,256]{2,1,0:T(8,128)(2,1)S(1)} %collective-permute-done.8.refs_4_), channel_id=1, source_target_pairs={{0,7},{1,0},{2,1},{3,2},{4,3},{5,4},{6,5},{7,6},{8,15},{9,8},{10,9... | collective-permute-start | bytes 786440 | tf_op jit(solution)/shard_map/ppermute | solution.py:217
  80.6 1.8 %collective-permute-done.5.refs_5_ = bf16[2,256,256]{2,1,0:T(8,128)(2,1)S(1)} collective-permute-done((bf16[2,256,256]{2,1,0:T(8,128)(2,1)S(1)}, bf16[2,256,256]{2,1,0:T(8,128)(2,1)S(1)}, u32[]{:S(2)}, u32[]{:S(2)}) %collective-permute-start.5) | collective-permute-done | bytes 262176 | tf_op jit(solution)/shard_map/ppermute | solution.py:217
  82.5 1.9 %collective-permute-start.6 = (bf16[2,256,256]{2,1,0:T(8,128)(2,1)S(1)}, bf16[2,256,256]{2,1,0:T(8,128)(2,1)S(1)}, u32[]{:S(2)}, u32[]{:S(2)}) collective-permute-start(bf16[2,256,256]{2,1,0:T(8,128)(2,1)S(1)} %collective-permute-done.5.refs_5_), channel_id=1, source_target_pairs={{0,1},{1,2},{2,3},{3,4},{4,5},{5,6},{6,7},{7,0},{8,9},{9,10},{10,1... | collective-permute-start | bytes 786440 | tf_op jit(solution)/shard_map/ppermute | solution.py:217
  84.4 2.2 %copy-done = bf16[4096,512]{1,0:T(8,128)(2,1)S(1)} copy-done((bf16[4096,512]{1,0:T(8,128)(2,1)S(1)}, bf16[4096,512]{1,0:T(8,128)(2,1)}, u32[]{:S(2)}) %copy-start) | copy-done | bytes 4194328
  86.6 2.6 %shard_map.58.sum_ref = f32[4,512,256]{2,1,0:T(8,128)S(1)} custom-call(s32[3]{0:T(128)S(1)} %pad_add_fusion.ids_ref, bf16[8,2,256,512]{3,2,1,0:T(8,128)(2,1)S(1)} %bitcast.6, bf16[2,256,256]{2,1,0:T(8,128)(2,1)S(1)} %pad_maximum_fusion.refs_0_, bf16[2,256,256]{2,1,0:T(8,128)(2,1)S(1)} %collective-permute-done.3.refs_1_, ...), custom_call_target="tpu_custom_call" | custom-call | flops 2147483648 | bytes 8388608 | tf_op jit(solution)/shard_map/pallas_call | solution.py:155
  89.2 2.7 %collective-permute-done.6.piece_ref = bf16[2,256,256]{2,1,0:T(8,128)(2,1)S(1)} collective-permute-done((bf16[2,256,256]{2,1,0:T(8,128)(2,1)S(1)}, bf16[2,256,256]{2,1,0:T(8,128)(2,1)S(1)}, u32[]{:S(2)}, u32[]{:S(2)}) %collective-permute-start.6) | collective-permute-done | bytes 262176 | tf_op jit(solution)/shard_map/ppermute | solution.py:217
  91.9 1.0 shard_map.59
  93.0 12.9 %all_to_all.25.p_ref = bf16[4,512,256]{2,1,0:T(8,128)(2,1)S(1)} all-to-all(bf16[4,512,256]{2,1,0:T(8,128)(2,1)S(1)} %get-tuple-element.16), channel_id=1, replica_groups=mesh['x_hi'=2,'y'=8,'core'=2,'x_lo'=2,'z'=8] {'x_hi','x_lo'}, dimensions={0} | all-to-all | bytes 2097152 | tf_op jit(solution)/shard_map/all_to_all | solution.py:250
  105.8 0.7 shard_map.60
  106.5 15.9 %all_to_all.26.p_ref = bf16[8,64,256]{2,1,0:T(8,128)(2,1)S(1)} all-to-all(bf16[8,64,256]{2,1,0:T(8,128)(2,1)S(1)} %shard_map.60), channel_id=1, replica_groups=mesh['x_hi'=2,'y'=8,'core'=2,'x_lo'=2,'z'=8] {'y'}, dimensions={0} | all-to-all | bytes 524288 | tf_op jit(solution)/shard_map/all_to_all | solution.py:258
  122.5 20.5 %all_to_all.27.p_ref = f32[4,64,256]{2,1,0:T(8,128)S(1)} all-to-all(f32[4,64,256]{2,1,0:T(8,128)S(1)} %shard_map.61), channel_id=1, replica_groups=mesh['x_hi'=2,'y'=8,'core'=2,'x_lo'=2,'z'=8] {'x_hi','core'}, dimensions={0} | all-to-all | bytes 524288 | tf_op jit(solution)/shard_map/all_to_all | solution.py:266
  143.1 0.7 shard_map.62
  (18 shorter events, 0.2 us)
Async XLA Ops:
  6.5 15.1 %copy-start.4 = (bf16[256,512]{1,0:T(8,128)(2,1)S(1)}, bf16[256,512]{1,0:T(8,128)(2,1)}, u32[]{:S(2)}) copy-start(bf16[256,512]{1,0:T(8,128)(2,1)} %param.8) | copy-start | bytes 786436
  6.5 26.4 %copy-start.2 = (bf16[64,64]{1,0:T(8,128)(2,1)S(1)}, bf16[64,64]{1,0:T(8,128)(2,1)}, u32[]{:S(2)}) copy-start(bf16[64,64]{1,0:T(8,128)(2,1)} %e_ref.1) | copy-start | bytes 24580
  6.5 40.4 %copy-start.1 = (bf16[4,512,512]{2,1,0:T(8,128)(2,1)S(1)}, bf16[4,512,512]{2,1,0:T(8,128)(2,1)}, u32[]{:S(2)}) copy-start(bf16[4,512,512]{2,1,0:T(8,128)(2,1)} %dy_ref.1) | copy-start | bytes 6291460
  9.7 22.6 %all-to-all-start = ((bf16[16,64,128]{2,1,0:T(8,128)(2,1)}), bf16[16,64,128]{2,1,0:T(8,128)(2,1)S(1)}, u32[]{:S(2)}, u32[]{:S(2)}) async-start(bf16[16,64,128]{2,1,0:T(8,128)(2,1)} %shard_map.55), calls=%async_computation | async-start | bytes 524288 | tf_op jit(solution)/shard_map/all_to_all | solution.py:231
  21.6 62.8 %all-gather.3.cloned.1.call-start = ((), (), s32[]{:S(2)}) async-start(), calls=%async_computation.5 | async-start | bytes 4456448 | tf_op jit(solution)/shard_map/all_gather | solution.py:233
  21.6 10.6 %collective-permute-start = (bf16[256,512]{1,0:T(8,128)(2,1)S(1)}, bf16[256,512]{1,0:T(8,128)(2,1)S(1)}, u32[]{:S(2)}, u32[]{:S(2)}) collective-permute-start(bf16[256,512]{1,0:T(8,128)(2,1)S(1)} %copy-done.4), channel_id=1, source_target_pairs={{0,0},{8,16},{16,8},{24,24},{1,1},{9,17},{17,9},{25,25},{2,2},{10,... | collective-permute-start | bytes 786440 | tf_op jit(solution)/shard_map/ppermute | solution.py:229
  32.2 0.7 copy-start.3
  33.9 13.0 %all-to-all-start.1 = ((bf16[16,64,128]{2,1,0:T(8,128)(2,1)}), bf16[16,64,128]{2,1,0:T(8,128)(2,1)S(1)}, u32[]{:S(2)}, u32[]{:S(2)}) async-start(bf16[16,64,128]{2,1,0:T(8,128)(2,1)} %shard_map.56), calls=%async_computation.1 | async-start | bytes 524288 | tf_op jit(solution)/shard_map/all_to_all | solution.py:234
  47.9 6.0 %collective-permute-start.1 = (bf16[256,256]{1,0:T(8,128)(2,1)S(1)}, bf16[256,256]{1,0:T(8,128)(2,1)S(1)}, u32[]{:S(2)}, u32[]{:S(2)}) collective-permute-start(bf16[256,256]{1,0:T(8,128)(2,1)S(1)} %get-tuple-element.13), channel_id=1, source_target_pairs={{0,0},{8,256},{256,8},{264,264},{1,1},{9,257},{257,9},{265,265},{2... | collective-permute-start | bytes 393224 | tf_op jit(solution)/shard_map/ppermute | solution.py:238
  48.6 8.0 %collective-permute-start.2 = (bf16[256,256]{1,0:T(8,128)(2,1)S(1)}, bf16[256,256]{1,0:T(8,128)(2,1)S(1)}, u32[]{:S(2)}, u32[]{:S(2)}) collective-permute-start(bf16[256,256]{1,0:T(8,128)(2,1)S(1)} %get-tuple-element.14), channel_id=1, source_target_pairs={{256,0},{0,8},{264,256},{8,264},{257,1},{1,9},{265,257},{9,265},{2... | collective-permute-start | bytes 393224 | tf_op jit(solution)/shard_map/ppermute | solution.py:237
  56.7 8.7 %collective-permute-start.3 = (bf16[2,256,256]{2,1,0:T(8,128)(2,1)S(1)}, bf16[2,256,256]{2,1,0:T(8,128)(2,1)S(1)}, u32[]{:S(2)}, u32[]{:S(2)}) collective-permute-start(bf16[2,256,256]{2,1,0:T(8,128)(2,1)S(1)} %pad_maximum_fusion.refs_0_), channel_id=1, source_target_pairs={{0,1},{1,2},{2,3},{3,4},{4,5},{5,6},{6,7},{7,0},{8,9},{9,10},{10,1... | collective-permute-start | bytes 786440 | tf_op jit(solution)/shard_map/ppermute | solution.py:217
  61.2 7.5 %collective-permute-start.7 = (bf16[2,256,256]{2,1,0:T(8,128)(2,1)S(1)}, bf16[2,256,256]{2,1,0:T(8,128)(2,1)S(1)}, u32[]{:S(2)}, u32[]{:S(2)}) collective-permute-start(bf16[2,256,256]{2,1,0:T(8,128)(2,1)S(1)} %pad_maximum_fusion.refs_0_), channel_id=1, source_target_pairs={{0,7},{1,0},{2,1},{3,2},{4,3},{5,4},{6,5},{7,6},{8,15},{9,8},{10,9... | collective-permute-start | bytes 786440 | tf_op jit(solution)/shard_map/ppermute | solution.py:217
  65.4 8.7 %collective-permute-start.4 = (bf16[2,256,256]{2,1,0:T(8,128)(2,1)S(1)}, bf16[2,256,256]{2,1,0:T(8,128)(2,1)S(1)}, u32[]{:S(2)}, u32[]{:S(2)}) collective-permute-start(bf16[2,256,256]{2,1,0:T(8,128)(2,1)S(1)} %collective-permute-done.3.refs_1_), channel_id=1, source_target_pairs={{0,1},{1,2},{2,3},{3,4},{4,5},{5,6},{6,7},{7,0},{8,9},{9,10},{10,1... | collective-permute-start | bytes 786440 | tf_op jit(solution)/shard_map/ppermute | solution.py:217
  68.7 7.5 %collective-permute-start.8 = (bf16[2,256,256]{2,1,0:T(8,128)(2,1)S(1)}, bf16[2,256,256]{2,1,0:T(8,128)(2,1)S(1)}, u32[]{:S(2)}, u32[]{:S(2)}) collective-permute-start(bf16[2,256,256]{2,1,0:T(8,128)(2,1)S(1)} %collective-permute-done.7.refs_2_), channel_id=1, source_target_pairs={{0,7},{1,0},{2,1},{3,2},{4,3},{5,4},{6,5},{7,6},{8,15},{9,8},{10,9... | collective-permute-start | bytes 786440 | tf_op jit(solution)/shard_map/ppermute | solution.py:217
  74.1 8.4 %collective-permute-start.5 = (bf16[2,256,256]{2,1,0:T(8,128)(2,1)S(1)}, bf16[2,256,256]{2,1,0:T(8,128)(2,1)S(1)}, u32[]{:S(2)}, u32[]{:S(2)}) collective-permute-start(bf16[2,256,256]{2,1,0:T(8,128)(2,1)S(1)} %collective-permute-done.4.refs_3_), channel_id=1, source_target_pairs={{0,1},{1,2},{2,3},{3,4},{4,5},{5,6},{6,7},{7,0},{8,9},{9,10},{10,1... | collective-permute-start | bytes 786440 | tf_op jit(solution)/shard_map/ppermute | solution.py:217
  76.2 8.1 %collective-permute-start.9 = (bf16[2,256,256]{2,1,0:T(8,128)(2,1)S(1)}, bf16[2,256,256]{2,1,0:T(8,128)(2,1)S(1)}, u32[]{:S(2)}, u32[]{:S(2)}) collective-permute-start(bf16[2,256,256]{2,1,0:T(8,128)(2,1)S(1)} %collective-permute-done.8.refs_4_), channel_id=1, source_target_pairs={{0,7},{1,0},{2,1},{3,2},{4,3},{5,4},{6,5},{7,6},{8,15},{9,8},{10,9... | collective-permute-start | bytes 786440 | tf_op jit(solution)/shard_map/ppermute | solution.py:217
  82.5 9.5 %collective-permute-start.6 = (bf16[2,256,256]{2,1,0:T(8,128)(2,1)S(1)}, bf16[2,256,256]{2,1,0:T(8,128)(2,1)S(1)}, u32[]{:S(2)}, u32[]{:S(2)}) collective-permute-start(bf16[2,256,256]{2,1,0:T(8,128)(2,1)S(1)} %collective-permute-done.5.refs_5_), channel_id=1, source_target_pairs={{0,1},{1,2},{2,3},{3,4},{4,5},{5,6},{6,7},{7,0},{8,9},{9,10},{10,1... | collective-permute-start | bytes 786440 | tf_op jit(solution)/shard_map/ppermute | solution.py:217
  84.4 2.2 %copy-start = (bf16[4096,512]{1,0:T(8,128)(2,1)S(1)}, bf16[4096,512]{1,0:T(8,128)(2,1)}, u32[]{:S(2)}) copy-start(bf16[4096,512]{1,0:T(8,128)(2,1)} %all-gather.3.cloned.1.call-done) | copy-start | bytes 12582916
Sparse Core Ops, SparseCore 0:
  33.1 44.1 all-gather.2

commit v5 on v4

--- a/solution.py
+++ b/solution.py
@@ -85,34 +85,31 @@
     )(parts, basis)
 
 
-def grad_kernel(ids_ref, rot_ref, dy_ref, keep_ref, send_ref):
+def grad_kernel(rot_ref, dy_ref, o_ref):
     count, rank = dy_ref.shape[0], rot_ref.shape[1]
     per = rot_ref.shape[0] // count
     half = dy_ref.shape[2] // 2
-    first = ids_ref[1] == 0
     for n in range(count):
         rot = jnp.concatenate([rot_ref[n * per + c] for c in range(per)], axis=1)
         grad = jnp.dot(rot, dy_ref[n], preferred_element_type=F32).astype(BF16)
-        low, high = grad[:, :half], grad[:, half:]
         rows = slice(n * rank, (n + 1) * rank)
-        keep_ref[rows, :] = jnp.where(first, low, high)
-        send_ref[rows, :] = jnp.where(first, high, low)
-
-
-def gradients(ids, rot, dy):
+        for h in range(2):
+            o_ref[h, rows, :] = grad[:, h * half : (h + 1) * half]
+
+
+def gradients(rot, dy):
     count, tokens, width = dy.shape
     rank = rot.shape[1]
-    out = jax.ShapeDtypeStruct((count * rank, width // 2), BF16)
     return pl.pallas_call(
         grad_kernel,
-        in_specs=[SCALARS, WHOLE, WHOLE],
-        out_specs=[WHOLE, WHOLE],
-        out_shape=[out, out],
+        in_specs=[WHOLE, WHOLE],
+        out_specs=WHOLE,
+        out_shape=jax.ShapeDtypeStruct((2, count * rank, width // 2), BF16),
         compiler_params=params(),
         cost_estimate=pl.CostEstimate(
             flops=2 * count * tokens * width * rank, bytes_accessed=3 << 20, transcendentals=0
         ),
-    )(ids, rot, dy)
+    )(rot, dy)
 
 
 def coef_parts(ids_ref, q_ref, pieces, offsets, dests):
@@ -123,7 +120,7 @@
         half = 1 - x_hi if other_hi else x_hi
         cols = pl.ds(pl.multiple_of(half * 256, 256), 256)
         for h in range(2):
-            rows = pl.ds(pl.multiple_of((1 - x_lo if h else x_lo) * 256, 256), 256)
+            rows = slice(256 * h, 256 * h + 256)
             total = None
             for piece, b in zip(pieces, blocks):
                 term = jnp.dot(piece[h], q_ref[b, j, :, cols], preferred_element_type=F32)
@@ -197,9 +194,7 @@
     total = p_ref[0].astype(F32)
     for i in range(1, p_ref.shape[0]):
         total = total + p_ref[i].astype(F32)
-    total = total * (1.0 / 128)
-    for i in range(o_ref.shape[0]):
-        o_ref[i] = total
+    o_ref[...] = total * (1.0 / 128)
 
 
 def join_kernel(p_ref, o_ref):
@@ -217,8 +212,7 @@
     return lax.ppermute(x, "z", [(i, (i + step) % 8) for i in range(8)])
 
 
-TURN = [(0, 0), (1, 2), (2, 1), (3, 3)]
-CROSS = [(2, 0), (0, 1), (3, 2), (1, 3)]
+TURN = [(4 * h + 2 * c + l, 4 * c + 2 * l + h) for h in range(2) for c in range(2) for l in range(2)]
 
 
 def shards(inputs, out_grads, down, out_basis, adapter_basis):
@@ -226,17 +220,15 @@
     x_hi, x_lo = lax.axis_index("x_hi"), lax.axis_index("x_lo")
     ids = jnp.stack([z, x_hi, x_lo]).astype(jnp.int32)
 
-    turned = lax.ppermute(out_basis, ("core", "x_lo"), TURN)
+    turned = lax.ppermute(out_basis, ("x_hi", "core", "x_lo"), TURN)
     parts = project(inputs, down)
     parts = lax.all_to_all(parts, EIGEN, 0, 0)
+    parts = rotate(parts, adapter_basis)
     parts, turned = lax.optimization_barrier((parts, turned))
     basis = lax.all_gather(turned, ("y", "core"), axis=0).reshape(8, 2, *out_basis.shape)
-    rot = lax.all_to_all(rotate(parts, adapter_basis), EIGEN, 0, 0)
-
-    keep, send = gradients(ids, rot, out_grads)
-    send = lax.ppermute(send, ("x_hi", "x_lo"), CROSS)
-    keep = lax.ppermute(keep, ("x_hi", "x_lo"), TURN)
-    piece = jnp.stack([keep, send])
+    rot = lax.all_to_all(parts, EIGEN, 0, 0)
+
+    piece = lax.all_to_all(gradients(rot, out_grads), "x_hi", 0, 0)
     pieces, offsets = [piece], [0]
     up = down_ = piece
     for s in range(1, 4):
@@ -260,10 +252,10 @@
         mean_kernel,
         in_specs=[WHOLE],
         out_specs=WHOLE,
-        out_shape=jax.ShapeDtypeStruct((4, 64, 256), F32),
+        out_shape=jax.ShapeDtypeStruct((64, 256), F32),
         compiler_params=params(),
     )(sums)
-    mean = lax.all_to_all(mean, ("x_hi", "core"), 0, 0)
+    mean = lax.all_gather(mean, ("x_hi", "core"), axis=0)
     return pl.pallas_call(
         join_kernel,
         in_specs=[WHOLE],

time: 151 us -> 149 us (0.987)
  blocking collectives: 49.4 us -> 71 us
  waiting for transfers between devices: 25.7 us -> 12.9 us
  starting transfers between devices: 48.8 us -> 38.7 us
    all_gather x0 -> x1, blocking collectives: none -> 19.1 us  [shards(): mean = lax.all_gather(mean, ('x_hi', 'core'), axis=0)]
    all_to_all x1 -> x0, waiting for transfers between devices: 7.71 us -> none  [shards(): rot = lax.all_to_all(rotate(parts, adapter_basis), EIGEN, 0, 0)]
    ppermute x3 -> x1, waiting for transfers between devices: 8.95 us -> 1.75 us  [shards(): turned = lax.ppermute(out_basis, ('x_hi', 'core', 'x_lo'), TURN)]
    all_to_all x1 -> x0, starting transfers between devices: 5.18 us -> none  [shards(): rot = lax.all_to_all(rotate(parts, adapter_basis), EIGEN, 0, 0)]
    ppermute x3 -> x1, starting transfers between devices: 10.3 us -> 5.2 us  [shards(): turned = lax.ppermute(out_basis, ('x_hi', 'core', 'x_lo'), TURN)]
    all_to_all x1, waiting for transfers between devices: 0.01 us -> 3.46 us  [shards(): parts = lax.all_to_all(parts, EIGEN, 0, 0)]
    all_to_all x1 -> x2, blocking collectives: 20.5 us -> 23.8 us  [the longest x1 14.7 us: shards(): rot = lax.all_to_all(parts, EIGEN, 0, 0)]
  transfers between devices with their start and end apart: 13 -> 10, of which waited for: 7 -> 6; matrix products, arithmetic and copies ran while one was open for 0% -> 0% of each run, Pallas kernels for 3% -> 2%
where the time goes in v5:
time: 149 us; the launch traced here: 148 us
  blocking collectives  71 us (48%)
  starting transfers between devices  38.7 us (26%)
  between operations  13.6 us (9%)
  waiting for transfers between devices  12.9 us (9%)
  Pallas kernels  8.77 us (6%)
  local copies, waits for them, and re-layouts  2.91 us (2%)
    ppermute x7, starting transfers between devices, shift(): return lax.ppermute(x, 'z', [(i, (i + step) % 8) for i in range(8)])  21.6 us
    all_gather x1, blocking collectives, shards(): mean = lax.all_gather(mean, ('x_hi', 'core'), axis=0)  19.1 us
    all_to_all x1, blocking collectives, shards(): sums = lax.all_to_all(sums, 'y', 0, 0)  15.9 us
    all_to_all x1, blocking collectives, shards(): rot = lax.all_to_all(parts, EIGEN, 0, 0)  14.7 us
    all_to_all x1, blocking collectives, shards(): away = lax.all_to_all(away, ('x_hi', 'x_lo'), 0, 0)  12.2 us
    all_to_all x1, starting transfers between devices, shards(): parts = lax.all_to_all(parts, EIGEN, 0, 0)  11.9 us
    all_to_all x1, blocking collectives, shards(): piece = lax.all_to_all(gradients(rot, out_grads), 'x_hi', 0, 0)  9.05 us
    ppermute x7, waiting for transfers between devices, shift(): return lax.ppermute(x, 'z', [(i, (i + step) % 8) for i in range(8)])  7.67 us
  transfers between devices with their start and end apart: 10, of which 6 were waited for; matrix products, arithmetic and copies ran while one was open for 0% of the time, Pallas kernels for 2%

profile of v5, /device:TPU:1, one launch (start us, length us, event | category | flops | bytes accessed | tf_op | source)
XLA Modules:
  0.0 147.9 jit_solution(6627163258829378033)
XLA Ops:
  6.5 3.1 %shard_map.55 = bf16[16,64,128]{2,1,0:T(8,128)(2,1)} custom-call(bf16[64,512]{1,0:T(8,128)(2,1)} %a_ref.1, bf16[4,512,512]{2,1,0:T(8,128)(2,1)} %x_ref.1), custom_call_target="tpu_custom_call" | custom-call | flops 134217728 | bytes 3145728 | tf_op jit(solution)/shard_map/pallas_call | solution.py:50
  9.7 11.9 %all-to-all-start = ((bf16[16,64,128]{2,1,0:T(8,128)(2,1)}), bf16[16,64,128]{2,1,0:T(8,128)(2,1)S(1)}, u32[]{:S(2)}, u32[]{:S(2)}) async-start(bf16[16,64,128]{2,1,0:T(8,128)(2,1)} %shard_map.55), calls=%async_computation | async-start | bytes 524288 | tf_op jit(solution)/shard_map/all_to_all | solution.py:225
  21.6 0.0 all-gather.4.cloned.1.call-start
  21.6 5.2 %collective-permute-start = (bf16[256,512]{1,0:T(8,128)(2,1)S(1)}, bf16[256,512]{1,0:T(8,128)(2,1)S(1)}, u32[]{:S(2)}, u32[]{:S(2)}) collective-permute-start(bf16[256,512]{1,0:T(8,128)(2,1)S(1)} %copy-done.4), channel_id=1, source_target_pairs={{0,0},{8,16},{16,256},{24,272},{256,8},{264,24},{272,264},{280,280... | collective-permute-start | bytes 786440 | tf_op jit(solution)/shard_map/ppermute | solution.py:223
  26.8 3.5 %all-to-all-done.p_ref = bf16[16,64,128]{2,1,0:T(8,128)(2,1)S(1)} async-done(((bf16[16,64,128]{2,1,0:T(8,128)(2,1)}), bf16[16,64,128]{2,1,0:T(8,128)(2,1)S(1)}, u32[]{:S(2)}, u32[]{:S(2)}) %all-to-all-start) | async-done | bytes 262176 | tf_op jit(solution)/shard_map/all_to_all | solution.py:225
  30.3 0.2 shard_map.56
  30.5 1.7 %collective-permute-done = bf16[256,512]{1,0:T(8,128)(2,1)S(1)} collective-permute-done((bf16[256,512]{1,0:T(8,128)(2,1)S(1)}, bf16[256,512]{1,0:T(8,128)(2,1)S(1)}, u32[]{:S(2)}, u32[]{:S(2)}) %collective-permute-start) | collective-permute-done | bytes 262176 | tf_op jit(solution)/shard_map/ppermute | solution.py:223
  32.3 0.7 copy-done.3
  33.0 0.0 all-gather.4.cloned.1.call-update
  33.0 14.7 %all_to_all.25.rot_ref = bf16[16,64,128]{2,1,0:T(8,128)(2,1)S(1)} all-to-all(bf16[16,64,128]{2,1,0:T(8,128)(2,1)S(1)} %shard_map.56), channel_id=1, replica_groups=mesh['x_hi'=2,'y'=8,'core'=2,'x_lo'=2,'z'=8] {'x_lo','z'}, dimensions={0} | all-to-all | bytes 524288 | tf_op jit(solution)/shard_map/all_to_all | solution.py:229
  47.7 0.5 shard_map.57
  48.2 9.1 %all_to_all.26.refs_0_ = bf16[2,256,256]{2,1,0:T(8,128)(2,1)S(1)} all-to-all(bf16[2,256,256]{2,1,0:T(8,128)(2,1)S(1)} %shard_map.57), channel_id=1, replica_groups=mesh['x_hi'=2,'y'=8,'core'=2,'x_lo'=2,'z'=8] {'x_hi'}, dimensions={0} | all-to-all | bytes 524288 | tf_op jit(solution)/shard_map/all_to_all | solution.py:231
  57.2 4.0 %collective-permute-start.1 = (bf16[2,256,256]{2,1,0:T(8,128)(2,1)S(1)}, bf16[2,256,256]{2,1,0:T(8,128)(2,1)S(1)}, u32[]{:S(2)}, u32[]{:S(2)}) collective-permute-start(bf16[2,256,256]{2,1,0:T(8,128)(2,1)S(1)} %all_to_all.26.refs_0_), channel_id=1, source_target_pairs={{0,1},{1,2},{2,3},{3,4},{4,5},{5,6},{6,7},{7,0},{8,9},{9,10},{10,1... | collective-permute-start | bytes 786440 | tf_op jit(solution)/shard_map/ppermute | solution.py:212
  61.3 2.5 %collective-permute-start.5 = (bf16[2,256,256]{2,1,0:T(8,128)(2,1)S(1)}, bf16[2,256,256]{2,1,0:T(8,128)(2,1)S(1)}, u32[]{:S(2)}, u32[]{:S(2)}) collective-permute-start(bf16[2,256,256]{2,1,0:T(8,128)(2,1)S(1)} %all_to_all.26.refs_0_), channel_id=1, source_target_pairs={{0,7},{1,0},{2,1},{3,2},{4,3},{5,4},{6,5},{7,6},{8,15},{9,8},{10,9... | collective-permute-start | bytes 786440 | tf_op jit(solution)/shard_map/ppermute | solution.py:212
  63.7 2.2 %collective-permute-done.1.refs_1_ = bf16[2,256,256]{2,1,0:T(8,128)(2,1)S(1)} collective-permute-done((bf16[2,256,256]{2,1,0:T(8,128)(2,1)S(1)}, bf16[2,256,256]{2,1,0:T(8,128)(2,1)S(1)}, u32[]{:S(2)}, u32[]{:S(2)}) %collective-permute-start.1) | collective-permute-done | bytes 262176 | tf_op jit(solution)/shard_map/ppermute | solution.py:212
  65.9 2.8 %collective-permute-start.2 = (bf16[2,256,256]{2,1,0:T(8,128)(2,1)S(1)}, bf16[2,256,256]{2,1,0:T(8,128)(2,1)S(1)}, u32[]{:S(2)}, u32[]{:S(2)}) collective-permute-start(bf16[2,256,256]{2,1,0:T(8,128)(2,1)S(1)} %collective-permute-done.1.refs_1_), channel_id=1, source_target_pairs={{0,1},{1,2},{2,3},{3,4},{4,5},{5,6},{6,7},{7,0},{8,9},{9,10},{10,1... | collective-permute-start | bytes 786440 | tf_op jit(solution)/shard_map/ppermute | solution.py:212
  68.8 3.7 %collective-permute-start.6 = (bf16[2,256,256]{2,1,0:T(8,128)(2,1)S(1)}, bf16[2,256,256]{2,1,0:T(8,128)(2,1)S(1)}, u32[]{:S(2)}, u32[]{:S(2)}) collective-permute-start(bf16[2,256,256]{2,1,0:T(8,128)(2,1)S(1)} %collective-permute-done.5.refs_2_), channel_id=1, source_target_pairs={{0,7},{1,0},{2,1},{3,2},{4,3},{5,4},{6,5},{7,6},{8,15},{9,8},{10,9... | collective-permute-start | bytes 786440 | tf_op jit(solution)/shard_map/ppermute | solution.py:212
  72.5 2.0 %collective-permute-done.2.refs_3_ = bf16[2,256,256]{2,1,0:T(8,128)(2,1)S(1)} collective-permute-done((bf16[2,256,256]{2,1,0:T(8,128)(2,1)S(1)}, bf16[2,256,256]{2,1,0:T(8,128)(2,1)S(1)}, u32[]{:S(2)}, u32[]{:S(2)}) %collective-permute-start.2) | collective-permute-done | bytes 262176 | tf_op jit(solution)/shard_map/ppermute | solution.py:212
  74.4 1.9 %collective-permute-start.3 = (bf16[2,256,256]{2,1,0:T(8,128)(2,1)S(1)}, bf16[2,256,256]{2,1,0:T(8,128)(2,1)S(1)}, u32[]{:S(2)}, u32[]{:S(2)}) collective-permute-start(bf16[2,256,256]{2,1,0:T(8,128)(2,1)S(1)} %collective-permute-done.2.refs_3_), channel_id=1, source_target_pairs={{0,1},{1,2},{2,3},{3,4},{4,5},{5,6},{6,7},{7,0},{8,9},{9,10},{10,1... | collective-permute-start | bytes 786440 | tf_op jit(solution)/shard_map/ppermute | solution.py:212
  76.4 4.8 %collective-permute-start.7 = (bf16[2,256,256]{2,1,0:T(8,128)(2,1)S(1)}, bf16[2,256,256]{2,1,0:T(8,128)(2,1)S(1)}, u32[]{:S(2)}, u32[]{:S(2)}) collective-permute-start(bf16[2,256,256]{2,1,0:T(8,128)(2,1)S(1)} %collective-permute-done.6.refs_4_), channel_id=1, source_target_pairs={{0,7},{1,0},{2,1},{3,2},{4,3},{5,4},{6,5},{7,6},{8,15},{9,8},{10,9... | collective-permute-start | bytes 786440 | tf_op jit(solution)/shard_map/ppermute | solution.py:212
  81.2 1.6 %collective-permute-done.3.refs_5_ = bf16[2,256,256]{2,1,0:T(8,128)(2,1)S(1)} collective-permute-done((bf16[2,256,256]{2,1,0:T(8,128)(2,1)S(1)}, bf16[2,256,256]{2,1,0:T(8,128)(2,1)S(1)}, u32[]{:S(2)}, u32[]{:S(2)}) %collective-permute-start.3) | collective-permute-done | bytes 262176 | tf_op jit(solution)/shard_map/ppermute | solution.py:212
  82.7 1.9 %collective-permute-start.4 = (bf16[2,256,256]{2,1,0:T(8,128)(2,1)S(1)}, bf16[2,256,256]{2,1,0:T(8,128)(2,1)S(1)}, u32[]{:S(2)}, u32[]{:S(2)}) collective-permute-start(bf16[2,256,256]{2,1,0:T(8,128)(2,1)S(1)} %collective-permute-done.3.refs_5_), channel_id=1, source_target_pairs={{0,1},{1,2},{2,3},{3,4},{4,5},{5,6},{6,7},{7,0},{8,9},{9,10},{10,1... | collective-permute-start | bytes 786440 | tf_op jit(solution)/shard_map/ppermute | solution.py:212
  84.7 0.1 pad_add_fusion.ids_ref
  84.7 2.2 %copy-done = bf16[4096,512]{1,0:T(8,128)(2,1)S(1)} copy-done((bf16[4096,512]{1,0:T(8,128)(2,1)S(1)}, bf16[4096,512]{1,0:T(8,128)(2,1)}, u32[]{:S(2)}) %copy-start) | copy-done | bytes 4194328
  86.9 2.6 %shard_map.58.sum_ref = f32[4,512,256]{2,1,0:T(8,128)S(1)} custom-call(s32[3]{0:T(128)S(1)} %pad_add_fusion.ids_ref, bf16[8,2,256,512]{3,2,1,0:T(8,128)(2,1)S(1)} %bitcast.5, bf16[2,256,256]{2,1,0:T(8,128)(2,1)S(1)} %all_to_all.26.refs_0_, bf16[2,256,256]{2,1,0:T(8,128)(2,1)S(1)} %collective-permute-done.1.refs_1_, ...), custom_call_target="tpu_custom_call" | custom-call | flops 2147483648 | bytes 8388608 | tf_op jit(solution)/shard_map/pallas_call | solution.py:152
  89.5 1.9 %collective-permute-done.4.piece_ref = bf16[2,256,256]{2,1,0:T(8,128)(2,1)S(1)} collective-permute-done((bf16[2,256,256]{2,1,0:T(8,128)(2,1)S(1)}, bf16[2,256,256]{2,1,0:T(8,128)(2,1)S(1)}, u32[]{:S(2)}, u32[]{:S(2)}) %collective-permute-start.4) | collective-permute-done | bytes 262176 | tf_op jit(solution)/shard_map/ppermute | solution.py:212
  91.4 1.0 shard_map.59
  92.4 12.2 %all_to_all.27.p_ref = bf16[4,512,256]{2,1,0:T(8,128)(2,1)S(1)} all-to-all(bf16[4,512,256]{2,1,0:T(8,128)(2,1)S(1)} %get-tuple-element.12), channel_id=1, replica_groups=mesh['x_hi'=2,'y'=8,'core'=2,'x_lo'=2,'z'=8] {'x_hi','x_lo'}, dimensions={0} | all-to-all | bytes 2097152 | tf_op jit(solution)/shard_map/all_to_all | solution.py:242
  104.6 0.7 shard_map.60
  105.3 15.9 %all_to_all.28.p_ref = bf16[8,64,256]{2,1,0:T(8,128)(2,1)S(1)} all-to-all(bf16[8,64,256]{2,1,0:T(8,128)(2,1)S(1)} %shard_map.60), channel_id=1, replica_groups=mesh['x_hi'=2,'y'=8,'core'=2,'x_lo'=2,'z'=8] {'y'}, dimensions={0} | all-to-all | bytes 524288 | tf_op jit(solution)/shard_map/all_to_all | solution.py:250
  121.3 19.1 %all-gather.1 = f32[256,256]{1,0:T(8,128)S(1)} all-gather(f32[64,256]{1,0:T(8,128)S(1)} %shard_map.61), channel_id=3, replica_groups=mesh['x_hi'=2,'y'=8,'core'=2,'x_lo'=2,'z'=8] {'x_hi','core'}, dimensions={0}, use_global_device_ids=true | all-gather | bytes 327680 | tf_op jit(solution)/shard_map/all_gather | solution.py:258
  140.4 0.7 shard_map.62
  (13 shorter events, 0.1 us)
Async XLA Ops:
  6.5 15.1 %copy-start.4 = (bf16[256,512]{1,0:T(8,128)(2,1)S(1)}, bf16[256,512]{1,0:T(8,128)(2,1)}, u32[]{:S(2)}) copy-start(bf16[256,512]{1,0:T(8,128)(2,1)} %param.8) | copy-start | bytes 786436
  6.5 23.8 %copy-start.2 = (bf16[64,64]{1,0:T(8,128)(2,1)S(1)}, bf16[64,64]{1,0:T(8,128)(2,1)}, u32[]{:S(2)}) copy-start(bf16[64,64]{1,0:T(8,128)(2,1)} %e_ref.1) | copy-start | bytes 24580
  6.5 41.2 %copy-start.1 = (bf16[4,512,512]{2,1,0:T(8,128)(2,1)S(1)}, bf16[4,512,512]{2,1,0:T(8,128)(2,1)}, u32[]{:S(2)}) copy-start(bf16[4,512,512]{2,1,0:T(8,128)(2,1)} %dy_ref.1) | copy-start | bytes 6291460
  9.7 20.6 %all-to-all-start = ((bf16[16,64,128]{2,1,0:T(8,128)(2,1)}), bf16[16,64,128]{2,1,0:T(8,128)(2,1)S(1)}, u32[]{:S(2)}, u32[]{:S(2)}) async-start(bf16[16,64,128]{2,1,0:T(8,128)(2,1)} %shard_map.55), calls=%async_computation | async-start | bytes 524288 | tf_op jit(solution)/shard_map/all_to_all | solution.py:225
  21.6 63.2 %all-gather.4.cloned.1.call-start = ((), (), s32[]{:S(2)}) async-start(), calls=%async_computation.5 | async-start | bytes 4456448 | tf_op jit(solution)/shard_map/all_gather | solution.py:228
  21.6 10.6 %collective-permute-start = (bf16[256,512]{1,0:T(8,128)(2,1)S(1)}, bf16[256,512]{1,0:T(8,128)(2,1)S(1)}, u32[]{:S(2)}, u32[]{:S(2)}) collective-permute-start(bf16[256,512]{1,0:T(8,128)(2,1)S(1)} %copy-done.4), channel_id=1, source_target_pairs={{0,0},{8,16},{16,256},{24,272},{256,8},{264,24},{272,264},{280,280... | collective-permute-start | bytes 786440 | tf_op jit(solution)/shard_map/ppermute | solution.py:223
  32.3 0.7 copy-start.3
  57.2 8.7 %collective-permute-start.1 = (bf16[2,256,256]{2,1,0:T(8,128)(2,1)S(1)}, bf16[2,256,256]{2,1,0:T(8,128)(2,1)S(1)}, u32[]{:S(2)}, u32[]{:S(2)}) collective-permute-start(bf16[2,256,256]{2,1,0:T(8,128)(2,1)S(1)} %all_to_all.26.refs_0_), channel_id=1, source_target_pairs={{0,1},{1,2},{2,3},{3,4},{4,5},{5,6},{6,7},{7,0},{8,9},{9,10},{10,1... | collective-permute-start | bytes 786440 | tf_op jit(solution)/shard_map/ppermute | solution.py:212
  61.3 7.5 %collective-permute-start.5 = (bf16[2,256,256]{2,1,0:T(8,128)(2,1)S(1)}, bf16[2,256,256]{2,1,0:T(8,128)(2,1)S(1)}, u32[]{:S(2)}, u32[]{:S(2)}) collective-permute-start(bf16[2,256,256]{2,1,0:T(8,128)(2,1)S(1)} %all_to_all.26.refs_0_), channel_id=1, source_target_pairs={{0,7},{1,0},{2,1},{3,2},{4,3},{5,4},{6,5},{7,6},{8,15},{9,8},{10,9... | collective-permute-start | bytes 786440 | tf_op jit(solution)/shard_map/ppermute | solution.py:212
  65.9 8.5 %collective-permute-start.2 = (bf16[2,256,256]{2,1,0:T(8,128)(2,1)S(1)}, bf16[2,256,256]{2,1,0:T(8,128)(2,1)S(1)}, u32[]{:S(2)}, u32[]{:S(2)}) collective-permute-start(bf16[2,256,256]{2,1,0:T(8,128)(2,1)S(1)} %collective-permute-done.1.refs_1_), channel_id=1, source_target_pairs={{0,1},{1,2},{2,3},{3,4},{4,5},{5,6},{6,7},{7,0},{8,9},{9,10},{10,1... | collective-permute-start | bytes 786440 | tf_op jit(solution)/shard_map/ppermute | solution.py:212
  68.8 7.6 %collective-permute-start.6 = (bf16[2,256,256]{2,1,0:T(8,128)(2,1)S(1)}, bf16[2,256,256]{2,1,0:T(8,128)(2,1)S(1)}, u32[]{:S(2)}, u32[]{:S(2)}) collective-permute-start(bf16[2,256,256]{2,1,0:T(8,128)(2,1)S(1)} %collective-permute-done.5.refs_2_), channel_id=1, source_target_pairs={{0,7},{1,0},{2,1},{3,2},{4,3},{5,4},{6,5},{7,6},{8,15},{9,8},{10,9... | collective-permute-start | bytes 786440 | tf_op jit(solution)/shard_map/ppermute | solution.py:212
  74.4 8.3 %collective-permute-start.3 = (bf16[2,256,256]{2,1,0:T(8,128)(2,1)S(1)}, bf16[2,256,256]{2,1,0:T(8,128)(2,1)S(1)}, u32[]{:S(2)}, u32[]{:S(2)}) collective-permute-start(bf16[2,256,256]{2,1,0:T(8,128)(2,1)S(1)} %collective-permute-done.2.refs_3_), channel_id=1, source_target_pairs={{0,1},{1,2},{2,3},{3,4},{4,5},{5,6},{6,7},{7,0},{8,9},{9,10},{10,1... | collective-permute-start | bytes 786440 | tf_op jit(solution)/shard_map/ppermute | solution.py:212
  76.4 8.4 %collective-permute-start.7 = (bf16[2,256,256]{2,1,0:T(8,128)(2,1)S(1)}, bf16[2,256,256]{2,1,0:T(8,128)(2,1)S(1)}, u32[]{:S(2)}, u32[]{:S(2)}) collective-permute-start(bf16[2,256,256]{2,1,0:T(8,128)(2,1)S(1)} %collective-permute-done.6.refs_4_), channel_id=1, source_target_pairs={{0,7},{1,0},{2,1},{3,2},{4,3},{5,4},{6,5},{7,6},{8,15},{9,8},{10,9... | collective-permute-start | bytes 786440 | tf_op jit(solution)/shard_map/ppermute | solution.py:212
  82.7 8.7 %collective-permute-start.4 = (bf16[2,256,256]{2,1,0:T(8,128)(2,1)S(1)}, bf16[2,256,256]{2,1,0:T(8,128)(2,1)S(1)}, u32[]{:S(2)}, u32[]{:S(2)}) collective-permute-start(bf16[2,256,256]{2,1,0:T(8,128)(2,1)S(1)} %collective-permute-done.3.refs_5_), channel_id=1, source_target_pairs={{0,1},{1,2},{2,3},{3,4},{4,5},{5,6},{6,7},{7,0},{8,9},{9,10},{10,1... | collective-permute-start | bytes 786440 | tf_op jit(solution)/shard_map/ppermute | solution.py:212
  84.7 2.2 %copy-start = (bf16[4096,512]{1,0:T(8,128)(2,1)S(1)}, bf16[4096,512]{1,0:T(8,128)(2,1)}, u32[]{:S(2)}) copy-start(bf16[4096,512]{1,0:T(8,128)(2,1)} %all-gather.4.cloned.1.call-done) | copy-start | bytes 12582916
Sparse Core Ops, SparseCore 0:
  33.1 45.6 all-gather.3

commit v6 on v5

--- a/solution.py
+++ b/solution.py
@@ -197,10 +197,14 @@
     o_ref[...] = total * (1.0 / 128)
 
 
+def add_kernel(p_ref, o_ref):
+    o_ref[...] = p_ref[0] + p_ref[1]
+
+
 def join_kernel(p_ref, o_ref):
     half = p_ref.shape[2]
     for h in range(2):
-        o_ref[:, h * half : (h + 1) * half] = p_ref[2 * h] + p_ref[2 * h + 1]
+        o_ref[:, h * half : (h + 1) * half] = p_ref[h]
 
 
 def swap(x, axis, stride=1):
@@ -255,7 +259,14 @@
         out_shape=jax.ShapeDtypeStruct((64, 256), F32),
         compiler_params=params(),
     )(sums)
-    mean = lax.all_gather(mean, ("x_hi", "core"), axis=0)
+    mean = pl.pallas_call(
+        add_kernel,
+        in_specs=[WHOLE],
+        out_specs=WHOLE,
+        out_shape=jax.ShapeDtypeStruct((64, 256), F32),
+        compiler_params=params(),
+    )(lax.all_gather(mean, "core", axis=0))
+    mean = lax.all_gather(mean, "x_hi", axis=0)
     return pl.pallas_call(
         join_kernel,
         in_specs=[WHOLE],

time: 149 us -> 148 us (level)
    all_gather x1 -> x2, blocking collectives: 19.1 us -> 18.9 us  [the longest x1 13.6 us: shards(): lax.all_gather(mean, 'core', axis=0)]
where the time goes in v6:
time: 148 us
  blocking collectives  70.7 us (48%)
  starting transfers between devices  38.7 us (26%)
  between operations  13.6 us (9%)
  waiting for transfers between devices  12.9 us (9%)
  Pallas kernels  8.78 us (6%)
  local copies, waits for them, and re-layouts  2.91 us (2%)
    ppermute x7, starting transfers between devices, shift(): return lax.ppermute(x, 'z', [(i, (i + step) % 8) for i in range(8)])  21.6 us
    all_to_all x1, blocking collectives, shards(): sums = lax.all_to_all(sums, 'y', 0, 0)  15.9 us
    all_to_all x1, blocking collectives, shards(): rot = lax.all_to_all(parts, EIGEN, 0, 0)  14.7 us
    all_gather x1, blocking collectives, shards(): lax.all_gather(mean, 'core', axis=0)  13.6 us
    all_to_all x1, blocking collectives, shards(): away = lax.all_to_all(away, ('x_hi', 'x_lo'), 0, 0)  12.2 us
    all_to_all x1, starting transfers between devices, shards(): parts = lax.all_to_all(parts, EIGEN, 0, 0)  11.9 us
    all_to_all x1, blocking collectives, shards(): piece = lax.all_to_all(gradients(rot, out_grads), 'x_hi', 0, 0)  9.05 us
    ppermute x7, waiting for transfers between devices, shift(): return lax.ppermute(x, 'z', [(i, (i + step) % 8) for i in range(8)])  7.67 us
  transfers between devices with their start and end apart: 10, of which 6 were waited for; matrix products, arithmetic and copies ran while one was open for 0% of the time, Pallas kernels for 2%

profile of v6, /device:TPU:1, one launch (start us, length us, event | category | flops | bytes accessed | tf_op | source)
XLA Modules:
  0.0 147.7 jit_solution(8526198460713462590)
XLA Ops:
  6.5 3.1 %shard_map.55 = bf16[16,64,128]{2,1,0:T(8,128)(2,1)} custom-call(bf16[64,512]{1,0:T(8,128)(2,1)} %a_ref.1, bf16[4,512,512]{2,1,0:T(8,128)(2,1)} %x_ref.1), custom_call_target="tpu_custom_call" | custom-call | flops 134217728 | bytes 3145728 | tf_op jit(solution)/shard_map/pallas_call | solution.py:50
  9.7 11.9 %all-to-all-start = ((bf16[16,64,128]{2,1,0:T(8,128)(2,1)}), bf16[16,64,128]{2,1,0:T(8,128)(2,1)S(1)}, u32[]{:S(2)}, u32[]{:S(2)}) async-start(bf16[16,64,128]{2,1,0:T(8,128)(2,1)} %shard_map.55), calls=%async_computation | async-start | bytes 524288 | tf_op jit(solution)/shard_map/all_to_all | solution.py:229
  21.6 0.0 all-gather.5.cloned.1.call-start
  21.6 5.2 %collective-permute-start = (bf16[256,512]{1,0:T(8,128)(2,1)S(1)}, bf16[256,512]{1,0:T(8,128)(2,1)S(1)}, u32[]{:S(2)}, u32[]{:S(2)}) collective-permute-start(bf16[256,512]{1,0:T(8,128)(2,1)S(1)} %copy-done.4), channel_id=1, source_target_pairs={{0,0},{8,16},{16,256},{24,272},{256,8},{264,24},{272,264},{280,280... | collective-permute-start | bytes 786440 | tf_op jit(solution)/shard_map/ppermute | solution.py:227
  26.8 3.5 %all-to-all-done.p_ref = bf16[16,64,128]{2,1,0:T(8,128)(2,1)S(1)} async-done(((bf16[16,64,128]{2,1,0:T(8,128)(2,1)}), bf16[16,64,128]{2,1,0:T(8,128)(2,1)S(1)}, u32[]{:S(2)}, u32[]{:S(2)}) %all-to-all-start) | async-done | bytes 262176 | tf_op jit(solution)/shard_map/all_to_all | solution.py:229
  30.3 0.2 shard_map.56
  30.5 1.7 %collective-permute-done = bf16[256,512]{1,0:T(8,128)(2,1)S(1)} collective-permute-done((bf16[256,512]{1,0:T(8,128)(2,1)S(1)}, bf16[256,512]{1,0:T(8,128)(2,1)S(1)}, u32[]{:S(2)}, u32[]{:S(2)}) %collective-permute-start) | collective-permute-done | bytes 262176 | tf_op jit(solution)/shard_map/ppermute | solution.py:227
  32.3 0.7 copy-done.3
  33.0 14.7 %all_to_all.25.rot_ref = bf16[16,64,128]{2,1,0:T(8,128)(2,1)S(1)} all-to-all(bf16[16,64,128]{2,1,0:T(8,128)(2,1)S(1)} %shard_map.56), channel_id=1, replica_groups=mesh['x_hi'=2,'y'=8,'core'=2,'x_lo'=2,'z'=8] {'x_lo','z'}, dimensions={0} | all-to-all | bytes 524288 | tf_op jit(solution)/shard_map/all_to_all | solution.py:233
  47.7 0.5 shard_map.57
  48.2 9.1 %all_to_all.26.refs_0_ = bf16[2,256,256]{2,1,0:T(8,128)(2,1)S(1)} all-to-all(bf16[2,256,256]{2,1,0:T(8,128)(2,1)S(1)} %shard_map.57), channel_id=1, replica_groups=mesh['x_hi'=2,'y'=8,'core'=2,'x_lo'=2,'z'=8] {'x_hi'}, dimensions={0} | all-to-all | bytes 524288 | tf_op jit(solution)/shard_map/all_to_all | solution.py:235
  57.2 4.0 %collective-permute-start.1 = (bf16[2,256,256]{2,1,0:T(8,128)(2,1)S(1)}, bf16[2,256,256]{2,1,0:T(8,128)(2,1)S(1)}, u32[]{:S(2)}, u32[]{:S(2)}) collective-permute-start(bf16[2,256,256]{2,1,0:T(8,128)(2,1)S(1)} %all_to_all.26.refs_0_), channel_id=1, source_target_pairs={{0,1},{1,2},{2,3},{3,4},{4,5},{5,6},{6,7},{7,0},{8,9},{9,10},{10,1... | collective-permute-start | bytes 786440 | tf_op jit(solution)/shard_map/ppermute | solution.py:216
  61.3 2.5 %collective-permute-start.5 = (bf16[2,256,256]{2,1,0:T(8,128)(2,1)S(1)}, bf16[2,256,256]{2,1,0:T(8,128)(2,1)S(1)}, u32[]{:S(2)}, u32[]{:S(2)}) collective-permute-start(bf16[2,256,256]{2,1,0:T(8,128)(2,1)S(1)} %all_to_all.26.refs_0_), channel_id=1, source_target_pairs={{0,7},{1,0},{2,1},{3,2},{4,3},{5,4},{6,5},{7,6},{8,15},{9,8},{10,9... | collective-permute-start | bytes 786440 | tf_op jit(solution)/shard_map/ppermute | solution.py:216
  63.7 2.2 %collective-permute-done.1.refs_1_ = bf16[2,256,256]{2,1,0:T(8,128)(2,1)S(1)} collective-permute-done((bf16[2,256,256]{2,1,0:T(8,128)(2,1)S(1)}, bf16[2,256,256]{2,1,0:T(8,128)(2,1)S(1)}, u32[]{:S(2)}, u32[]{:S(2)}) %collective-permute-start.1) | collective-permute-done | bytes 262176 | tf_op jit(solution)/shard_map/ppermute | solution.py:216
  65.9 2.8 %collective-permute-start.2 = (bf16[2,256,256]{2,1,0:T(8,128)(2,1)S(1)}, bf16[2,256,256]{2,1,0:T(8,128)(2,1)S(1)}, u32[]{:S(2)}, u32[]{:S(2)}) collective-permute-start(bf16[2,256,256]{2,1,0:T(8,128)(2,1)S(1)} %collective-permute-done.1.refs_1_), channel_id=1, source_target_pairs={{0,1},{1,2},{2,3},{3,4},{4,5},{5,6},{6,7},{7,0},{8,9},{9,10},{10,1... | collective-permute-start | bytes 786440 | tf_op jit(solution)/shard_map/ppermute | solution.py:216
  68.8 3.7 %collective-permute-start.6 = (bf16[2,256,256]{2,1,0:T(8,128)(2,1)S(1)}, bf16[2,256,256]{2,1,0:T(8,128)(2,1)S(1)}, u32[]{:S(2)}, u32[]{:S(2)}) collective-permute-start(bf16[2,256,256]{2,1,0:T(8,128)(2,1)S(1)} %collective-permute-done.5.refs_2_), channel_id=1, source_target_pairs={{0,7},{1,0},{2,1},{3,2},{4,3},{5,4},{6,5},{7,6},{8,15},{9,8},{10,9... | collective-permute-start | bytes 786440 | tf_op jit(solution)/shard_map/ppermute | solution.py:216
  72.5 2.0 %collective-permute-done.2.refs_3_ = bf16[2,256,256]{2,1,0:T(8,128)(2,1)S(1)} collective-permute-done((bf16[2,256,256]{2,1,0:T(8,128)(2,1)S(1)}, bf16[2,256,256]{2,1,0:T(8,128)(2,1)S(1)}, u32[]{:S(2)}, u32[]{:S(2)}) %collective-permute-start.2) | collective-permute-done | bytes 262176 | tf_op jit(solution)/shard_map/ppermute | solution.py:216
  74.4 1.9 %collective-permute-start.3 = (bf16[2,256,256]{2,1,0:T(8,128)(2,1)S(1)}, bf16[2,256,256]{2,1,0:T(8,128)(2,1)S(1)}, u32[]{:S(2)}, u32[]{:S(2)}) collective-permute-start(bf16[2,256,256]{2,1,0:T(8,128)(2,1)S(1)} %collective-permute-done.2.refs_3_), channel_id=1, source_target_pairs={{0,1},{1,2},{2,3},{3,4},{4,5},{5,6},{6,7},{7,0},{8,9},{9,10},{10,1... | collective-permute-start | bytes 786440 | tf_op jit(solution)/shard_map/ppermute | solution.py:216
  76.4 4.8 %collective-permute-start.7 = (bf16[2,256,256]{2,1,0:T(8,128)(2,1)S(1)}, bf16[2,256,256]{2,1,0:T(8,128)(2,1)S(1)}, u32[]{:S(2)}, u32[]{:S(2)}) collective-permute-start(bf16[2,256,256]{2,1,0:T(8,128)(2,1)S(1)} %collective-permute-done.6.refs_4_), channel_id=1, source_target_pairs={{0,7},{1,0},{2,1},{3,2},{4,3},{5,4},{6,5},{7,6},{8,15},{9,8},{10,9... | collective-permute-start | bytes 786440 | tf_op jit(solution)/shard_map/ppermute | solution.py:216
  81.2 1.6 %collective-permute-done.3.refs_5_ = bf16[2,256,256]{2,1,0:T(8,128)(2,1)S(1)} collective-permute-done((bf16[2,256,256]{2,1,0:T(8,128)(2,1)S(1)}, bf16[2,256,256]{2,1,0:T(8,128)(2,1)S(1)}, u32[]{:S(2)}, u32[]{:S(2)}) %collective-permute-start.3) | collective-permute-done | bytes 262176 | tf_op jit(solution)/shard_map/ppermute | solution.py:216
  82.7 1.9 %collective-permute-start.4 = (bf16[2,256,256]{2,1,0:T(8,128)(2,1)S(1)}, bf16[2,256,256]{2,1,0:T(8,128)(2,1)S(1)}, u32[]{:S(2)}, u32[]{:S(2)}) collective-permute-start(bf16[2,256,256]{2,1,0:T(8,128)(2,1)S(1)} %collective-permute-done.3.refs_5_), channel_id=1, source_target_pairs={{0,1},{1,2},{2,3},{3,4},{4,5},{5,6},{6,7},{7,0},{8,9},{9,10},{10,1... | collective-permute-start | bytes 786440 | tf_op jit(solution)/shard_map/ppermute | solution.py:216
  84.7 0.1 pad_add_fusion.ids_ref
  84.7 2.2 %copy-done = bf16[4096,512]{1,0:T(8,128)(2,1)S(1)} copy-done((bf16[4096,512]{1,0:T(8,128)(2,1)S(1)}, bf16[4096,512]{1,0:T(8,128)(2,1)}, u32[]{:S(2)}) %copy-start) | copy-done | bytes 4194328
  86.9 2.6 %shard_map.58.sum_ref = f32[4,512,256]{2,1,0:T(8,128)S(1)} custom-call(s32[3]{0:T(128)S(1)} %pad_add_fusion.ids_ref, bf16[8,2,256,512]{3,2,1,0:T(8,128)(2,1)S(1)} %bitcast.6, bf16[2,256,256]{2,1,0:T(8,128)(2,1)S(1)} %all_to_all.26.refs_0_, bf16[2,256,256]{2,1,0:T(8,128)(2,1)S(1)} %collective-permute-done.1.refs_1_, ...), custom_call_target="tpu_custom_call" | custom-call | flops 2147483648 | bytes 8388608 | tf_op jit(solution)/shard_map/pallas_call | solution.py:152
  89.5 1.9 %collective-permute-done.4.piece_ref = bf16[2,256,256]{2,1,0:T(8,128)(2,1)S(1)} collective-permute-done((bf16[2,256,256]{2,1,0:T(8,128)(2,1)S(1)}, bf16[2,256,256]{2,1,0:T(8,128)(2,1)S(1)}, u32[]{:S(2)}, u32[]{:S(2)}) %collective-permute-start.4) | collective-permute-done | bytes 262176 | tf_op jit(solution)/shard_map/ppermute | solution.py:216
  91.4 1.0 shard_map.59
  92.4 12.2 %all_to_all.27.p_ref = bf16[4,512,256]{2,1,0:T(8,128)(2,1)S(1)} all-to-all(bf16[4,512,256]{2,1,0:T(8,128)(2,1)S(1)} %get-tuple-element.12), channel_id=1, replica_groups=mesh['x_hi'=2,'y'=8,'core'=2,'x_lo'=2,'z'=8] {'x_hi','x_lo'}, dimensions={0} | all-to-all | bytes 2097152 | tf_op jit(solution)/shard_map/all_to_all | solution.py:246
  104.6 0.7 shard_map.60
  105.3 15.9 %all_to_all.28.p_ref = bf16[8,64,256]{2,1,0:T(8,128)(2,1)S(1)} all-to-all(bf16[8,64,256]{2,1,0:T(8,128)(2,1)S(1)} %shard_map.60), channel_id=1, replica_groups=mesh['x_hi'=2,'y'=8,'core'=2,'x_lo'=2,'z'=8] {'y'}, dimensions={0} | all-to-all | bytes 524288 | tf_op jit(solution)/shard_map/all_to_all | solution.py:254
  121.3 13.6 %all-gather.1 = f32[128,256]{1,0:T(8,128)S(1)} all-gather(f32[64,256]{1,0:T(8,128)S(1)} %shard_map.61), channel_id=3, replica_groups=mesh['x_hi'=2,'y'=8,'core'=2,'x_lo'=2,'z'=8] {'core'}, dimensions={0}, use_global_device_ids=true | all-gather | bytes 196608 | tf_op jit(solution)/shard_map/all_gather | solution.py:268
  134.9 5.3 %all-gather.2 = f32[128,256]{1,0:T(8,128)S(1)} all-gather(f32[64,256]{1,0:T(8,128)S(1)} %shard_map.62), channel_id=4, replica_groups=mesh['x_hi'=2,'y'=8,'core'=2,'x_lo'=2,'z'=8] {'x_hi'}, dimensions={0}, use_global_device_ids=true | all-gather | bytes 196608 | tf_op jit(solution)/shard_map/all_gather | solution.py:269
  140.2 0.7 shard_map.63
  (15 shorter events, 0.1 us)
Async XLA Ops:
  6.5 15.1 %copy-start.4 = (bf16[256,512]{1,0:T(8,128)(2,1)S(1)}, bf16[256,512]{1,0:T(8,128)(2,1)}, u32[]{:S(2)}) copy-start(bf16[256,512]{1,0:T(8,128)(2,1)} %param.8) | copy-start | bytes 786436
  6.5 23.8 %copy-start.2 = (bf16[64,64]{1,0:T(8,128)(2,1)S(1)}, bf16[64,64]{1,0:T(8,128)(2,1)}, u32[]{:S(2)}) copy-start(bf16[64,64]{1,0:T(8,128)(2,1)} %e_ref.1) | copy-start | bytes 24580
  6.5 41.2 %copy-start.1 = (bf16[4,512,512]{2,1,0:T(8,128)(2,1)S(1)}, bf16[4,512,512]{2,1,0:T(8,128)(2,1)}, u32[]{:S(2)}) copy-start(bf16[4,512,512]{2,1,0:T(8,128)(2,1)} %dy_ref.1) | copy-start | bytes 6291460
  9.7 20.6 %all-to-all-start = ((bf16[16,64,128]{2,1,0:T(8,128)(2,1)}), bf16[16,64,128]{2,1,0:T(8,128)(2,1)S(1)}, u32[]{:S(2)}, u32[]{:S(2)}) async-start(bf16[16,64,128]{2,1,0:T(8,128)(2,1)} %shard_map.55), calls=%async_computation | async-start | bytes 524288 | tf_op jit(solution)/shard_map/all_to_all | solution.py:229
  21.6 63.2 %all-gather.5.cloned.1.call-start = ((), (), s32[]{:S(2)}) async-start(), calls=%async_computation.5 | async-start | bytes 4456448 | tf_op jit(solution)/shard_map/all_gather | solution.py:232
  21.6 10.6 %collective-permute-start = (bf16[256,512]{1,0:T(8,128)(2,1)S(1)}, bf16[256,512]{1,0:T(8,128)(2,1)S(1)}, u32[]{:S(2)}, u32[]{:S(2)}) collective-permute-start(bf16[256,512]{1,0:T(8,128)(2,1)S(1)} %copy-done.4), channel_id=1, source_target_pairs={{0,0},{8,16},{16,256},{24,272},{256,8},{264,24},{272,264},{280,280... | collective-permute-start | bytes 786440 | tf_op jit(solution)/shard_map/ppermute | solution.py:227
  32.3 0.7 copy-start.3
  57.2 8.7 %collective-permute-start.1 = (bf16[2,256,256]{2,1,0:T(8,128)(2,1)S(1)}, bf16[2,256,256]{2,1,0:T(8,128)(2,1)S(1)}, u32[]{:S(2)}, u32[]{:S(2)}) collective-permute-start(bf16[2,256,256]{2,1,0:T(8,128)(2,1)S(1)} %all_to_all.26.refs_0_), channel_id=1, source_target_pairs={{0,1},{1,2},{2,3},{3,4},{4,5},{5,6},{6,7},{7,0},{8,9},{9,10},{10,1... | collective-permute-start | bytes 786440 | tf_op jit(solution)/shard_map/ppermute | solution.py:216
  61.3 7.5 %collective-permute-start.5 = (bf16[2,256,256]{2,1,0:T(8,128)(2,1)S(1)}, bf16[2,256,256]{2,1,0:T(8,128)(2,1)S(1)}, u32[]{:S(2)}, u32[]{:S(2)}) collective-permute-start(bf16[2,256,256]{2,1,0:T(8,128)(2,1)S(1)} %all_to_all.26.refs_0_), channel_id=1, source_target_pairs={{0,7},{1,0},{2,1},{3,2},{4,3},{5,4},{6,5},{7,6},{8,15},{9,8},{10,9... | collective-permute-start | bytes 786440 | tf_op jit(solution)/shard_map/ppermute | solution.py:216
  65.9 8.5 %collective-permute-start.2 = (bf16[2,256,256]{2,1,0:T(8,128)(2,1)S(1)}, bf16[2,256,256]{2,1,0:T(8,128)(2,1)S(1)}, u32[]{:S(2)}, u32[]{:S(2)}) collective-permute-start(bf16[2,256,256]{2,1,0:T(8,128)(2,1)S(1)} %collective-permute-done.1.refs_1_), channel_id=1, source_target_pairs={{0,1},{1,2},{2,3},{3,4},{4,5},{5,6},{6,7},{7,0},{8,9},{9,10},{10,1... | collective-permute-start | bytes 786440 | tf_op jit(solution)/shard_map/ppermute | solution.py:216
  68.8 7.6 %collective-permute-start.6 = (bf16[2,256,256]{2,1,0:T(8,128)(2,1)S(1)}, bf16[2,256,256]{2,1,0:T(8,128)(2,1)S(1)}, u32[]{:S(2)}, u32[]{:S(2)}) collective-permute-start(bf16[2,256,256]{2,1,0:T(8,128)(2,1)S(1)} %collective-permute-done.5.refs_2_), channel_id=1, source_target_pairs={{0,7},{1,0},{2,1},{3,2},{4,3},{5,4},{6,5},{7,6},{8,15},{9,8},{10,9... | collective-permute-start | bytes 786440 | tf_op jit(solution)/shard_map/ppermute | solution.py:216
  74.4 8.3 %collective-permute-start.3 = (bf16[2,256,256]{2,1,0:T(8,128)(2,1)S(1)}, bf16[2,256,256]{2,1,0:T(8,128)(2,1)S(1)}, u32[]{:S(2)}, u32[]{:S(2)}) collective-permute-start(bf16[2,256,256]{2,1,0:T(8,128)(2,1)S(1)} %collective-permute-done.2.refs_3_), channel_id=1, source_target_pairs={{0,1},{1,2},{2,3},{3,4},{4,5},{5,6},{6,7},{7,0},{8,9},{9,10},{10,1... | collective-permute-start | bytes 786440 | tf_op jit(solution)/shard_map/ppermute | solution.py:216
  76.4 8.4 %collective-permute-start.7 = (bf16[2,256,256]{2,1,0:T(8,128)(2,1)S(1)}, bf16[2,256,256]{2,1,0:T(8,128)(2,1)S(1)}, u32[]{:S(2)}, u32[]{:S(2)}) collective-permute-start(bf16[2,256,256]{2,1,0:T(8,128)(2,1)S(1)} %collective-permute-done.6.refs_4_), channel_id=1, source_target_pairs={{0,7},{1,0},{2,1},{3,2},{4,3},{5,4},{6,5},{7,6},{8,15},{9,8},{10,9... | collective-permute-start | bytes 786440 | tf_op jit(solution)/shard_map/ppermute | solution.py:216
  82.7 8.7 %collective-permute-start.4 = (bf16[2,256,256]{2,1,0:T(8,128)(2,1)S(1)}, bf16[2,256,256]{2,1,0:T(8,128)(2,1)S(1)}, u32[]{:S(2)}, u32[]{:S(2)}) collective-permute-start(bf16[2,256,256]{2,1,0:T(8,128)(2,1)S(1)} %collective-permute-done.3.refs_5_), channel_id=1, source_target_pairs={{0,1},{1,2},{2,3},{3,4},{4,5},{5,6},{6,7},{7,0},{8,9},{9,10},{10,1... | collective-permute-start | bytes 786440 | tf_op jit(solution)/shard_map/ppermute | solution.py:216
  84.7 2.2 %copy-start = (bf16[4096,512]{1,0:T(8,128)(2,1)S(1)}, bf16[4096,512]{1,0:T(8,128)(2,1)}, u32[]{:S(2)}) copy-start(bf16[4096,512]{1,0:T(8,128)(2,1)} %all-gather.5.cloned.1.call-done) | copy-start | bytes 12582916
Sparse Core Ops, SparseCore 0:
  33.1 45.6 all-gather.4

commit v7 on v6

--- a/solution.py
+++ b/solution.py
@@ -144,7 +144,7 @@
         if i == 3:
             keep_ref[rows, :] = total
         hi, lo = DESTS[i]
-        slot = (1 - ids_ref[1] if hi else ids_ref[1]) * 2 + (1 - ids_ref[2] if lo else ids_ref[2])
+        slot = (1 - ids_ref[2] if lo else ids_ref[2]) * 2 + (1 - ids_ref[1] if hi else ids_ref[1])
         away_ref[slot, rows, :] = total.astype(BF16)
 
 
@@ -175,8 +175,8 @@
 
 def square_kernel(ids_ref, keep_ref, p_ref, o_ref):
     x_hi, x_lo = ids_ref[1], ids_ref[2]
-    far, beside = 2 * (1 - x_hi) + x_lo, 2 * x_hi + 1 - x_lo
-    across = 2 * (1 - x_hi) + 1 - x_lo
+    far, beside = 2 * x_lo + 1 - x_hi, 2 * (1 - x_lo) + x_hi
+    across = 2 * (1 - x_lo) + 1 - x_hi
     coef = keep_ref[...]
     for slot in (far, beside, across):
         coef = coef + p_ref[slot].astype(F32)
@@ -243,7 +243,7 @@
 
     sums = early(ids, basis, pieces, offsets)
     away, keep = late(ids, basis, last, 4, sums)
-    away = lax.all_to_all(away, ("x_hi", "x_lo"), 0, 0)
+    away = lax.all_to_all(away, ("x_lo", "x_hi"), 0, 0)
     sums = pl.pallas_call(
         square_kernel,
         in_specs=[SCALARS] + [WHOLE] * 2,

time: 148 us -> 148 us (level)
  no operation moved by 1% of the time
where the time goes in v7:
time: 148 us; the launch traced here: 147 us
  blocking collectives  70.4 us (48%)
  starting transfers between devices  38.7 us (26%)
  between operations  13.6 us (9%)
  waiting for transfers between devices  12.9 us (9%)
  Pallas kernels  8.78 us (6%)
  local copies, waits for them, and re-layouts  2.91 us (2%)
    ppermute x7, starting transfers between devices, shift(): return lax.ppermute(x, 'z', [(i, (i + step) % 8) for i in range(8)])  21.6 us
    all_to_all x1, blocking collectives, shards(): sums = lax.all_to_all(sums, 'y', 0, 0)  15.9 us
    all_to_all x1, blocking collectives, shards(): rot = lax.all_to_all(parts, EIGEN, 0, 0)  14.7 us
    all_gather x1, blocking collectives, shards(): lax.all_gather(mean, 'core', axis=0)  13.6 us
    all_to_all x1, starting transfers between devices, shards(): parts = lax.all_to_all(parts, EIGEN, 0, 0)  11.9 us
    all_to_all x1, blocking collectives, shards(): away = lax.all_to_all(away, ('x_lo', 'x_hi'), 0, 0)  11.9 us
    all_to_all x1, blocking collectives, shards(): piece = lax.all_to_all(gradients(rot, out_grads), 'x_hi', 0, 0)  9.05 us
    ppermute x7, waiting for transfers between devices, shift(): return lax.ppermute(x, 'z', [(i, (i + step) % 8) for i in range(8)])  7.67 us
  transfers between devices with their start and end apart: 10, of which 6 were waited for; matrix products, arithmetic and copies ran while one was open for 0% of the time, Pallas kernels for 2%

profile of v7, /device:TPU:1, one launch (start us, length us, event | category | flops | bytes accessed | tf_op | source)
XLA Modules:
  0.0 147.4 jit_solution(16148343659878375279)
XLA Ops:
  6.5 3.1 %shard_map.55 = bf16[16,64,128]{2,1,0:T(8,128)(2,1)} custom-call(bf16[64,512]{1,0:T(8,128)(2,1)} %a_ref.1, bf16[4,512,512]{2,1,0:T(8,128)(2,1)} %x_ref.1), custom_call_target="tpu_custom_call" | custom-call | flops 134217728 | bytes 3145728 | tf_op jit(solution)/shard_map/pallas_call | solution.py:50
  9.7 11.9 %all-to-all-start = ((bf16[16,64,128]{2,1,0:T(8,128)(2,1)}), bf16[16,64,128]{2,1,0:T(8,128)(2,1)S(1)}, u32[]{:S(2)}, u32[]{:S(2)}) async-start(bf16[16,64,128]{2,1,0:T(8,128)(2,1)} %shard_map.55), calls=%async_computation | async-start | bytes 524288 | tf_op jit(solution)/shard_map/all_to_all | solution.py:229
  21.6 0.0 all-gather.5.cloned.1.call-start
  21.6 5.2 %collective-permute-start = (bf16[256,512]{1,0:T(8,128)(2,1)S(1)}, bf16[256,512]{1,0:T(8,128)(2,1)S(1)}, u32[]{:S(2)}, u32[]{:S(2)}) collective-permute-start(bf16[256,512]{1,0:T(8,128)(2,1)S(1)} %copy-done.4), channel_id=1, source_target_pairs={{0,0},{8,16},{16,256},{24,272},{256,8},{264,24},{272,264},{280,280... | collective-permute-start | bytes 786440 | tf_op jit(solution)/shard_map/ppermute | solution.py:227
  26.8 3.5 %all-to-all-done.p_ref = bf16[16,64,128]{2,1,0:T(8,128)(2,1)S(1)} async-done(((bf16[16,64,128]{2,1,0:T(8,128)(2,1)}), bf16[16,64,128]{2,1,0:T(8,128)(2,1)S(1)}, u32[]{:S(2)}, u32[]{:S(2)}) %all-to-all-start) | async-done | bytes 262176 | tf_op jit(solution)/shard_map/all_to_all | solution.py:229
  30.3 0.2 shard_map.56
  30.5 1.7 %collective-permute-done = bf16[256,512]{1,0:T(8,128)(2,1)S(1)} collective-permute-done((bf16[256,512]{1,0:T(8,128)(2,1)S(1)}, bf16[256,512]{1,0:T(8,128)(2,1)S(1)}, u32[]{:S(2)}, u32[]{:S(2)}) %collective-permute-start) | collective-permute-done | bytes 262176 | tf_op jit(solution)/shard_map/ppermute | solution.py:227
  32.3 0.7 copy-done.3
  33.0 14.7 %all_to_all.25.rot_ref = bf16[16,64,128]{2,1,0:T(8,128)(2,1)S(1)} all-to-all(bf16[16,64,128]{2,1,0:T(8,128)(2,1)S(1)} %shard_map.56), channel_id=1, replica_groups=mesh['x_hi'=2,'y'=8,'core'=2,'x_lo'=2,'z'=8] {'x_lo','z'}, dimensions={0} | all-to-all | bytes 524288 | tf_op jit(solution)/shard_map/all_to_all | solution.py:233
  47.7 0.5 shard_map.57
  48.2 9.1 %all_to_all.26.refs_0_ = bf16[2,256,256]{2,1,0:T(8,128)(2,1)S(1)} all-to-all(bf16[2,256,256]{2,1,0:T(8,128)(2,1)S(1)} %shard_map.57), channel_id=1, replica_groups=mesh['x_hi'=2,'y'=8,'core'=2,'x_lo'=2,'z'=8] {'x_hi'}, dimensions={0} | all-to-all | bytes 524288 | tf_op jit(solution)/shard_map/all_to_all | solution.py:235
  57.2 4.0 %collective-permute-start.1 = (bf16[2,256,256]{2,1,0:T(8,128)(2,1)S(1)}, bf16[2,256,256]{2,1,0:T(8,128)(2,1)S(1)}, u32[]{:S(2)}, u32[]{:S(2)}) collective-permute-start(bf16[2,256,256]{2,1,0:T(8,128)(2,1)S(1)} %all_to_all.26.refs_0_), channel_id=1, source_target_pairs={{0,1},{1,2},{2,3},{3,4},{4,5},{5,6},{6,7},{7,0},{8,9},{9,10},{10,1... | collective-permute-start | bytes 786440 | tf_op jit(solution)/shard_map/ppermute | solution.py:216
  61.3 2.5 %collective-permute-start.5 = (bf16[2,256,256]{2,1,0:T(8,128)(2,1)S(1)}, bf16[2,256,256]{2,1,0:T(8,128)(2,1)S(1)}, u32[]{:S(2)}, u32[]{:S(2)}) collective-permute-start(bf16[2,256,256]{2,1,0:T(8,128)(2,1)S(1)} %all_to_all.26.refs_0_), channel_id=1, source_target_pairs={{0,7},{1,0},{2,1},{3,2},{4,3},{5,4},{6,5},{7,6},{8,15},{9,8},{10,9... | collective-permute-start | bytes 786440 | tf_op jit(solution)/shard_map/ppermute | solution.py:216
  63.7 2.2 %collective-permute-done.1.refs_1_ = bf16[2,256,256]{2,1,0:T(8,128)(2,1)S(1)} collective-permute-done((bf16[2,256,256]{2,1,0:T(8,128)(2,1)S(1)}, bf16[2,256,256]{2,1,0:T(8,128)(2,1)S(1)}, u32[]{:S(2)}, u32[]{:S(2)}) %collective-permute-start.1) | collective-permute-done | bytes 262176 | tf_op jit(solution)/shard_map/ppermute | solution.py:216
  65.9 2.8 %collective-permute-start.2 = (bf16[2,256,256]{2,1,0:T(8,128)(2,1)S(1)}, bf16[2,256,256]{2,1,0:T(8,128)(2,1)S(1)}, u32[]{:S(2)}, u32[]{:S(2)}) collective-permute-start(bf16[2,256,256]{2,1,0:T(8,128)(2,1)S(1)} %collective-permute-done.1.refs_1_), channel_id=1, source_target_pairs={{0,1},{1,2},{2,3},{3,4},{4,5},{5,6},{6,7},{7,0},{8,9},{9,10},{10,1... | collective-permute-start | bytes 786440 | tf_op jit(solution)/shard_map/ppermute | solution.py:216
  68.8 3.7 %collective-permute-start.6 = (bf16[2,256,256]{2,1,0:T(8,128)(2,1)S(1)}, bf16[2,256,256]{2,1,0:T(8,128)(2,1)S(1)}, u32[]{:S(2)}, u32[]{:S(2)}) collective-permute-start(bf16[2,256,256]{2,1,0:T(8,128)(2,1)S(1)} %collective-permute-done.5.refs_2_), channel_id=1, source_target_pairs={{0,7},{1,0},{2,1},{3,2},{4,3},{5,4},{6,5},{7,6},{8,15},{9,8},{10,9... | collective-permute-start | bytes 786440 | tf_op jit(solution)/shard_map/ppermute | solution.py:216
  72.5 2.0 %collective-permute-done.2.refs_3_ = bf16[2,256,256]{2,1,0:T(8,128)(2,1)S(1)} collective-permute-done((bf16[2,256,256]{2,1,0:T(8,128)(2,1)S(1)}, bf16[2,256,256]{2,1,0:T(8,128)(2,1)S(1)}, u32[]{:S(2)}, u32[]{:S(2)}) %collective-permute-start.2) | collective-permute-done | bytes 262176 | tf_op jit(solution)/shard_map/ppermute | solution.py:216
  74.4 1.9 %collective-permute-start.3 = (bf16[2,256,256]{2,1,0:T(8,128)(2,1)S(1)}, bf16[2,256,256]{2,1,0:T(8,128)(2,1)S(1)}, u32[]{:S(2)}, u32[]{:S(2)}) collective-permute-start(bf16[2,256,256]{2,1,0:T(8,128)(2,1)S(1)} %collective-permute-done.2.refs_3_), channel_id=1, source_target_pairs={{0,1},{1,2},{2,3},{3,4},{4,5},{5,6},{6,7},{7,0},{8,9},{9,10},{10,1... | collective-permute-start | bytes 786440 | tf_op jit(solution)/shard_map/ppermute | solution.py:216
  76.4 4.8 %collective-permute-start.7 = (bf16[2,256,256]{2,1,0:T(8,128)(2,1)S(1)}, bf16[2,256,256]{2,1,0:T(8,128)(2,1)S(1)}, u32[]{:S(2)}, u32[]{:S(2)}) collective-permute-start(bf16[2,256,256]{2,1,0:T(8,128)(2,1)S(1)} %collective-permute-done.6.refs_4_), channel_id=1, source_target_pairs={{0,7},{1,0},{2,1},{3,2},{4,3},{5,4},{6,5},{7,6},{8,15},{9,8},{10,9... | collective-permute-start | bytes 786440 | tf_op jit(solution)/shard_map/ppermute | solution.py:216
  81.2 1.6 %collective-permute-done.3.refs_5_ = bf16[2,256,256]{2,1,0:T(8,128)(2,1)S(1)} collective-permute-done((bf16[2,256,256]{2,1,0:T(8,128)(2,1)S(1)}, bf16[2,256,256]{2,1,0:T(8,128)(2,1)S(1)}, u32[]{:S(2)}, u32[]{:S(2)}) %collective-permute-start.3) | collective-permute-done | bytes 262176 | tf_op jit(solution)/shard_map/ppermute | solution.py:216
  82.7 1.9 %collective-permute-start.4 = (bf16[2,256,256]{2,1,0:T(8,128)(2,1)S(1)}, bf16[2,256,256]{2,1,0:T(8,128)(2,1)S(1)}, u32[]{:S(2)}, u32[]{:S(2)}) collective-permute-start(bf16[2,256,256]{2,1,0:T(8,128)(2,1)S(1)} %collective-permute-done.3.refs_5_), channel_id=1, source_target_pairs={{0,1},{1,2},{2,3},{3,4},{4,5},{5,6},{6,7},{7,0},{8,9},{9,10},{10,1... | collective-permute-start | bytes 786440 | tf_op jit(solution)/shard_map/ppermute | solution.py:216
  84.7 0.1 pad_add_fusion.ids_ref
  84.7 2.2 %copy-done = bf16[4096,512]{1,0:T(8,128)(2,1)S(1)} copy-done((bf16[4096,512]{1,0:T(8,128)(2,1)S(1)}, bf16[4096,512]{1,0:T(8,128)(2,1)}, u32[]{:S(2)}) %copy-start) | copy-done | bytes 4194328
  86.9 2.6 %shard_map.58.sum_ref = f32[4,512,256]{2,1,0:T(8,128)S(1)} custom-call(s32[3]{0:T(128)S(1)} %pad_add_fusion.ids_ref, bf16[8,2,256,512]{3,2,1,0:T(8,128)(2,1)S(1)} %bitcast.6, bf16[2,256,256]{2,1,0:T(8,128)(2,1)S(1)} %all_to_all.26.refs_0_, bf16[2,256,256]{2,1,0:T(8,128)(2,1)S(1)} %collective-permute-done.1.refs_1_, ...), custom_call_target="tpu_custom_call" | custom-call | flops 2147483648 | bytes 8388608 | tf_op jit(solution)/shard_map/pallas_call | solution.py:152
  89.5 1.9 %collective-permute-done.4.piece_ref = bf16[2,256,256]{2,1,0:T(8,128)(2,1)S(1)} collective-permute-done((bf16[2,256,256]{2,1,0:T(8,128)(2,1)S(1)}, bf16[2,256,256]{2,1,0:T(8,128)(2,1)S(1)}, u32[]{:S(2)}, u32[]{:S(2)}) %collective-permute-start.4) | collective-permute-done | bytes 262176 | tf_op jit(solution)/shard_map/ppermute | solution.py:216
  91.4 1.0 shard_map.59
  92.4 11.9 %all_to_all.27.p_ref = bf16[4,512,256]{2,1,0:T(8,128)(2,1)S(1)} all-to-all(bf16[4,512,256]{2,1,0:T(8,128)(2,1)S(1)} %get-tuple-element.12), channel_id=1, replica_groups=mesh['x_hi'=2,'y'=8,'core'=2,'x_lo'=2,'z'=8] {'x_lo','x_hi'}, dimensions={0} | all-to-all | bytes 2097152 | tf_op jit(solution)/shard_map/all_to_all | solution.py:246
  104.3 0.7 shard_map.60
  105.0 15.9 %all_to_all.28.p_ref = bf16[8,64,256]{2,1,0:T(8,128)(2,1)S(1)} all-to-all(bf16[8,64,256]{2,1,0:T(8,128)(2,1)S(1)} %shard_map.60), channel_id=1, replica_groups=mesh['x_hi'=2,'y'=8,'core'=2,'x_lo'=2,'z'=8] {'y'}, dimensions={0} | all-to-all | bytes 524288 | tf_op jit(solution)/shard_map/all_to_all | solution.py:254
  121.0 13.6 %all-gather.1 = f32[128,256]{1,0:T(8,128)S(1)} all-gather(f32[64,256]{1,0:T(8,128)S(1)} %shard_map.61), channel_id=3, replica_groups=mesh['x_hi'=2,'y'=8,'core'=2,'x_lo'=2,'z'=8] {'core'}, dimensions={0}, use_global_device_ids=true | all-gather | bytes 196608 | tf_op jit(solution)/shard_map/all_gather | solution.py:268
  134.6 5.3 %all-gather.2 = f32[128,256]{1,0:T(8,128)S(1)} all-gather(f32[64,256]{1,0:T(8,128)S(1)} %shard_map.62), channel_id=4, replica_groups=mesh['x_hi'=2,'y'=8,'core'=2,'x_lo'=2,'z'=8] {'x_hi'}, dimensions={0}, use_global_device_ids=true | all-gather | bytes 196608 | tf_op jit(solution)/shard_map/all_gather | solution.py:269
  139.9 0.7 shard_map.63
  (15 shorter events, 0.1 us)
Async XLA Ops:
  6.5 15.1 %copy-start.4 = (bf16[256,512]{1,0:T(8,128)(2,1)S(1)}, bf16[256,512]{1,0:T(8,128)(2,1)}, u32[]{:S(2)}) copy-start(bf16[256,512]{1,0:T(8,128)(2,1)} %param.8) | copy-start | bytes 786436
  6.5 23.8 %copy-start.2 = (bf16[64,64]{1,0:T(8,128)(2,1)S(1)}, bf16[64,64]{1,0:T(8,128)(2,1)}, u32[]{:S(2)}) copy-start(bf16[64,64]{1,0:T(8,128)(2,1)} %e_ref.1) | copy-start | bytes 24580
  6.5 41.2 %copy-start.1 = (bf16[4,512,512]{2,1,0:T(8,128)(2,1)S(1)}, bf16[4,512,512]{2,1,0:T(8,128)(2,1)}, u32[]{:S(2)}) copy-start(bf16[4,512,512]{2,1,0:T(8,128)(2,1)} %dy_ref.1) | copy-start | bytes 6291460
  9.7 20.6 %all-to-all-start = ((bf16[16,64,128]{2,1,0:T(8,128)(2,1)}), bf16[16,64,128]{2,1,0:T(8,128)(2,1)S(1)}, u32[]{:S(2)}, u32[]{:S(2)}) async-start(bf16[16,64,128]{2,1,0:T(8,128)(2,1)} %shard_map.55), calls=%async_computation | async-start | bytes 524288 | tf_op jit(solution)/shard_map/all_to_all | solution.py:229
  21.6 63.2 %all-gather.5.cloned.1.call-start = ((), (), s32[]{:S(2)}) async-start(), calls=%async_computation.5 | async-start | bytes 4456448 | tf_op jit(solution)/shard_map/all_gather | solution.py:232
  21.6 10.6 %collective-permute-start = (bf16[256,512]{1,0:T(8,128)(2,1)S(1)}, bf16[256,512]{1,0:T(8,128)(2,1)S(1)}, u32[]{:S(2)}, u32[]{:S(2)}) collective-permute-start(bf16[256,512]{1,0:T(8,128)(2,1)S(1)} %copy-done.4), channel_id=1, source_target_pairs={{0,0},{8,16},{16,256},{24,272},{256,8},{264,24},{272,264},{280,280... | collective-permute-start | bytes 786440 | tf_op jit(solution)/shard_map/ppermute | solution.py:227
  32.3 0.7 copy-start.3
  57.2 8.7 %collective-permute-start.1 = (bf16[2,256,256]{2,1,0:T(8,128)(2,1)S(1)}, bf16[2,256,256]{2,1,0:T(8,128)(2,1)S(1)}, u32[]{:S(2)}, u32[]{:S(2)}) collective-permute-start(bf16[2,256,256]{2,1,0:T(8,128)(2,1)S(1)} %all_to_all.26.refs_0_), channel_id=1, source_target_pairs={{0,1},{1,2},{2,3},{3,4},{4,5},{5,6},{6,7},{7,0},{8,9},{9,10},{10,1... | collective-permute-start | bytes 786440 | tf_op jit(solution)/shard_map/ppermute | solution.py:216
  61.3 7.5 %collective-permute-start.5 = (bf16[2,256,256]{2,1,0:T(8,128)(2,1)S(1)}, bf16[2,256,256]{2,1,0:T(8,128)(2,1)S(1)}, u32[]{:S(2)}, u32[]{:S(2)}) collective-permute-start(bf16[2,256,256]{2,1,0:T(8,128)(2,1)S(1)} %all_to_all.26.refs_0_), channel_id=1, source_target_pairs={{0,7},{1,0},{2,1},{3,2},{4,3},{5,4},{6,5},{7,6},{8,15},{9,8},{10,9... | collective-permute-start | bytes 786440 | tf_op jit(solution)/shard_map/ppermute | solution.py:216
  65.9 8.5 %collective-permute-start.2 = (bf16[2,256,256]{2,1,0:T(8,128)(2,1)S(1)}, bf16[2,256,256]{2,1,0:T(8,128)(2,1)S(1)}, u32[]{:S(2)}, u32[]{:S(2)}) collective-permute-start(bf16[2,256,256]{2,1,0:T(8,128)(2,1)S(1)} %collective-permute-done.1.refs_1_), channel_id=1, source_target_pairs={{0,1},{1,2},{2,3},{3,4},{4,5},{5,6},{6,7},{7,0},{8,9},{9,10},{10,1... | collective-permute-start | bytes 786440 | tf_op jit(solution)/shard_map/ppermute | solution.py:216
  68.8 7.6 %collective-permute-start.6 = (bf16[2,256,256]{2,1,0:T(8,128)(2,1)S(1)}, bf16[2,256,256]{2,1,0:T(8,128)(2,1)S(1)}, u32[]{:S(2)}, u32[]{:S(2)}) collective-permute-start(bf16[2,256,256]{2,1,0:T(8,128)(2,1)S(1)} %collective-permute-done.5.refs_2_), channel_id=1, source_target_pairs={{0,7},{1,0},{2,1},{3,2},{4,3},{5,4},{6,5},{7,6},{8,15},{9,8},{10,9... | collective-permute-start | bytes 786440 | tf_op jit(solution)/shard_map/ppermute | solution.py:216
  74.4 8.3 %collective-permute-start.3 = (bf16[2,256,256]{2,1,0:T(8,128)(2,1)S(1)}, bf16[2,256,256]{2,1,0:T(8,128)(2,1)S(1)}, u32[]{:S(2)}, u32[]{:S(2)}) collective-permute-start(bf16[2,256,256]{2,1,0:T(8,128)(2,1)S(1)} %collective-permute-done.2.refs_3_), channel_id=1, source_target_pairs={{0,1},{1,2},{2,3},{3,4},{4,5},{5,6},{6,7},{7,0},{8,9},{9,10},{10,1... | collective-permute-start | bytes 786440 | tf_op jit(solution)/shard_map/ppermute | solution.py:216
  76.4 8.4 %collective-permute-start.7 = (bf16[2,256,256]{2,1,0:T(8,128)(2,1)S(1)}, bf16[2,256,256]{2,1,0:T(8,128)(2,1)S(1)}, u32[]{:S(2)}, u32[]{:S(2)}) collective-permute-start(bf16[2,256,256]{2,1,0:T(8,128)(2,1)S(1)} %collective-permute-done.6.refs_4_), channel_id=1, source_target_pairs={{0,7},{1,0},{2,1},{3,2},{4,3},{5,4},{6,5},{7,6},{8,15},{9,8},{10,9... | collective-permute-start | bytes 786440 | tf_op jit(solution)/shard_map/ppermute | solution.py:216
  82.7 8.7 %collective-permute-start.4 = (bf16[2,256,256]{2,1,0:T(8,128)(2,1)S(1)}, bf16[2,256,256]{2,1,0:T(8,128)(2,1)S(1)}, u32[]{:S(2)}, u32[]{:S(2)}) collective-permute-start(bf16[2,256,256]{2,1,0:T(8,128)(2,1)S(1)} %collective-permute-done.3.refs_5_), channel_id=1, source_target_pairs={{0,1},{1,2},{2,3},{3,4},{4,5},{5,6},{6,7},{7,0},{8,9},{9,10},{10,1... | collective-permute-start | bytes 786440 | tf_op jit(solution)/shard_map/ppermute | solution.py:216
  84.7 2.2 %copy-start = (bf16[4096,512]{1,0:T(8,128)(2,1)S(1)}, bf16[4096,512]{1,0:T(8,128)(2,1)}, u32[]{:S(2)}) copy-start(bf16[4096,512]{1,0:T(8,128)(2,1)} %all-gather.5.cloned.1.call-done) | copy-start | bytes 12582916
Sparse Core Ops, SparseCore 0:
  33.1 45.6 all-gather.4

commit v8 on v6

--- a/solution.py
+++ b/solution.py
@@ -227,10 +227,9 @@
     turned = lax.ppermute(out_basis, ("x_hi", "core", "x_lo"), TURN)
     parts = project(inputs, down)
     parts = lax.all_to_all(parts, EIGEN, 0, 0)
-    parts = rotate(parts, adapter_basis)
     parts, turned = lax.optimization_barrier((parts, turned))
     basis = lax.all_gather(turned, ("y", "core"), axis=0).reshape(8, 2, *out_basis.shape)
-    rot = lax.all_to_all(parts, EIGEN, 0, 0)
+    rot = lax.all_to_all(rotate(parts, adapter_basis), EIGEN, 0, 0)
 
     piece = lax.all_to_all(gradients(rot, out_grads), "x_hi", 0, 0)
     pieces, offsets = [piece], [0]

time: 148 us -> 148 us (level)
    ppermute x1, waiting for transfers between devices: 1.75 us -> 5.41 us  [shards(): turned = lax.ppermute(out_basis, ('x_hi', 'core', 'x_lo'), TURN)]
    all_to_all x1, waiting for transfers between devices: 3.46 us -> 0.01 us  [shards(): parts = lax.all_to_all(parts, EIGEN, 0, 0)]
  transfers between devices with their start and end apart: 10 -> 10, of which waited for: 6 -> 5; matrix products, arithmetic and copies ran while one was open for 0% -> 0% of each run, Pallas kernels for 2% -> 2%
where the time goes in v8:
time: 148 us
  blocking collectives  70.7 us (48%)
  starting transfers between devices  38.6 us (26%)
  between operations  13.6 us (9%)
  waiting for transfers between devices  13.2 us (9%)
  Pallas kernels  8.78 us (6%)
  local copies, waits for them, and re-layouts  2.9 us (2%)
    ppermute x7, starting transfers between devices, shift(): return lax.ppermute(x, 'z', [(i, (i + step) % 8) for i in range(8)])  21.5 us
    all_to_all x1, blocking collectives, shards(): sums = lax.all_to_all(sums, 'y', 0, 0)  15.9 us
    all_to_all x1, blocking collectives, shards(): rot = lax.all_to_all(rotate(parts, adapter_basis), EIGEN, 0, 0)  14.7 us
    all_gather x1, blocking collectives, shards(): lax.all_gather(mean, 'core', axis=0)  13.6 us
    all_to_all x1, blocking collectives, shards(): away = lax.all_to_all(away, ('x_hi', 'x_lo'), 0, 0)  12.2 us
    all_to_all x1, starting transfers between devices, shards(): parts = lax.all_to_all(parts, EIGEN, 0, 0)  11.9 us
    all_to_all x1, blocking collectives, shards(): piece = lax.all_to_all(gradients(rot, out_grads), 'x_hi', 0, 0)  9.05 us
    ppermute x7, waiting for transfers between devices, shift(): return lax.ppermute(x, 'z', [(i, (i + step) % 8) for i in range(8)])  7.79 us
  transfers between devices with their start and end apart: 10, of which 5 were waited for; matrix products, arithmetic and copies ran while one was open for 0% of the time, Pallas kernels for 2%

profile of v8, /device:TPU:1, one launch (start us, length us, event | category | flops | bytes accessed | tf_op | source)
XLA Modules:
  0.0 147.9 jit_solution(10868523702546569832)
XLA Ops:
  6.5 3.1 %shard_map.55 = bf16[16,64,128]{2,1,0:T(8,128)(2,1)} custom-call(bf16[64,512]{1,0:T(8,128)(2,1)} %a_ref.1, bf16[4,512,512]{2,1,0:T(8,128)(2,1)} %x_ref.1), custom_call_target="tpu_custom_call" | custom-call | flops 134217728 | bytes 3145728 | tf_op jit(solution)/shard_map/pallas_call | solution.py:50
  9.7 11.9 %all-to-all-start = ((bf16[16,64,128]{2,1,0:T(8,128)(2,1)}), bf16[16,64,128]{2,1,0:T(8,128)(2,1)S(1)}, u32[]{:S(2)}, u32[]{:S(2)}) async-start(bf16[16,64,128]{2,1,0:T(8,128)(2,1)} %shard_map.55), calls=%async_computation | async-start | bytes 524288 | tf_op jit(solution)/shard_map/all_to_all | solution.py:229
  21.6 0.0 all-gather.5.cloned.1.call-start
  21.6 5.2 %collective-permute-start = (bf16[256,512]{1,0:T(8,128)(2,1)S(1)}, bf16[256,512]{1,0:T(8,128)(2,1)S(1)}, u32[]{:S(2)}, u32[]{:S(2)}) collective-permute-start(bf16[256,512]{1,0:T(8,128)(2,1)S(1)} %copy-done.4), channel_id=1, source_target_pairs={{0,0},{8,16},{16,256},{24,272},{256,8},{264,24},{272,264},{280,280... | collective-permute-start | bytes 786440 | tf_op jit(solution)/shard_map/ppermute | solution.py:227
  26.8 5.4 %collective-permute-done = bf16[256,512]{1,0:T(8,128)(2,1)S(1)} collective-permute-done((bf16[256,512]{1,0:T(8,128)(2,1)S(1)}, bf16[256,512]{1,0:T(8,128)(2,1)S(1)}, u32[]{:S(2)}, u32[]{:S(2)}) %collective-permute-start) | collective-permute-done | bytes 262176 | tf_op jit(solution)/shard_map/ppermute | solution.py:227
  32.3 0.7 copy-done.3
  33.0 0.2 shard_map.56
  33.2 14.7 %all_to_all.25.rot_ref = bf16[16,64,128]{2,1,0:T(8,128)(2,1)S(1)} all-to-all(bf16[16,64,128]{2,1,0:T(8,128)(2,1)S(1)} %shard_map.56), channel_id=1, replica_groups=mesh['x_hi'=2,'y'=8,'core'=2,'x_lo'=2,'z'=8] {'x_lo','z'}, dimensions={0} | all-to-all | bytes 524288 | tf_op jit(solution)/shard_map/all_to_all | solution.py:232
  47.9 0.5 shard_map.57
  48.4 9.1 %all_to_all.26.refs_0_ = bf16[2,256,256]{2,1,0:T(8,128)(2,1)S(1)} all-to-all(bf16[2,256,256]{2,1,0:T(8,128)(2,1)S(1)} %shard_map.57), channel_id=1, replica_groups=mesh['x_hi'=2,'y'=8,'core'=2,'x_lo'=2,'z'=8] {'x_hi'}, dimensions={0} | all-to-all | bytes 524288 | tf_op jit(solution)/shard_map/all_to_all | solution.py:234
  57.4 4.0 %collective-permute-start.1 = (bf16[2,256,256]{2,1,0:T(8,128)(2,1)S(1)}, bf16[2,256,256]{2,1,0:T(8,128)(2,1)S(1)}, u32[]{:S(2)}, u32[]{:S(2)}) collective-permute-start(bf16[2,256,256]{2,1,0:T(8,128)(2,1)S(1)} %all_to_all.26.refs_0_), channel_id=1, source_target_pairs={{0,1},{1,2},{2,3},{3,4},{4,5},{5,6},{6,7},{7,0},{8,9},{9,10},{10,1... | collective-permute-start | bytes 786440 | tf_op jit(solution)/shard_map/ppermute | solution.py:216
  61.5 2.5 %collective-permute-start.5 = (bf16[2,256,256]{2,1,0:T(8,128)(2,1)S(1)}, bf16[2,256,256]{2,1,0:T(8,128)(2,1)S(1)}, u32[]{:S(2)}, u32[]{:S(2)}) collective-permute-start(bf16[2,256,256]{2,1,0:T(8,128)(2,1)S(1)} %all_to_all.26.refs_0_), channel_id=1, source_target_pairs={{0,7},{1,0},{2,1},{3,2},{4,3},{5,4},{6,5},{7,6},{8,15},{9,8},{10,9... | collective-permute-start | bytes 786440 | tf_op jit(solution)/shard_map/ppermute | solution.py:216
  63.9 2.2 %collective-permute-done.1.refs_1_ = bf16[2,256,256]{2,1,0:T(8,128)(2,1)S(1)} collective-permute-done((bf16[2,256,256]{2,1,0:T(8,128)(2,1)S(1)}, bf16[2,256,256]{2,1,0:T(8,128)(2,1)S(1)}, u32[]{:S(2)}, u32[]{:S(2)}) %collective-permute-start.1) | collective-permute-done | bytes 262176 | tf_op jit(solution)/shard_map/ppermute | solution.py:216
  66.2 2.8 %collective-permute-start.2 = (bf16[2,256,256]{2,1,0:T(8,128)(2,1)S(1)}, bf16[2,256,256]{2,1,0:T(8,128)(2,1)S(1)}, u32[]{:S(2)}, u32[]{:S(2)}) collective-permute-start(bf16[2,256,256]{2,1,0:T(8,128)(2,1)S(1)} %collective-permute-done.1.refs_1_), channel_id=1, source_target_pairs={{0,1},{1,2},{2,3},{3,4},{4,5},{5,6},{6,7},{7,0},{8,9},{9,10},{10,1... | collective-permute-start | bytes 786440 | tf_op jit(solution)/shard_map/ppermute | solution.py:216
  69.0 3.7 %collective-permute-start.6 = (bf16[2,256,256]{2,1,0:T(8,128)(2,1)S(1)}, bf16[2,256,256]{2,1,0:T(8,128)(2,1)S(1)}, u32[]{:S(2)}, u32[]{:S(2)}) collective-permute-start(bf16[2,256,256]{2,1,0:T(8,128)(2,1)S(1)} %collective-permute-done.5.refs_2_), channel_id=1, source_target_pairs={{0,7},{1,0},{2,1},{3,2},{4,3},{5,4},{6,5},{7,6},{8,15},{9,8},{10,9... | collective-permute-start | bytes 786440 | tf_op jit(solution)/shard_map/ppermute | solution.py:216
  72.7 1.8 %collective-permute-done.2.refs_3_ = bf16[2,256,256]{2,1,0:T(8,128)(2,1)S(1)} collective-permute-done((bf16[2,256,256]{2,1,0:T(8,128)(2,1)S(1)}, bf16[2,256,256]{2,1,0:T(8,128)(2,1)S(1)}, u32[]{:S(2)}, u32[]{:S(2)}) %collective-permute-start.2) | collective-permute-done | bytes 262176 | tf_op jit(solution)/shard_map/ppermute | solution.py:216
  74.5 2.0 %collective-permute-start.3 = (bf16[2,256,256]{2,1,0:T(8,128)(2,1)S(1)}, bf16[2,256,256]{2,1,0:T(8,128)(2,1)S(1)}, u32[]{:S(2)}, u32[]{:S(2)}) collective-permute-start(bf16[2,256,256]{2,1,0:T(8,128)(2,1)S(1)} %collective-permute-done.2.refs_3_), channel_id=1, source_target_pairs={{0,1},{1,2},{2,3},{3,4},{4,5},{5,6},{6,7},{7,0},{8,9},{9,10},{10,1... | collective-permute-start | bytes 786440 | tf_op jit(solution)/shard_map/ppermute | solution.py:216
  76.5 0.0 collective-permute-done.6.refs_4_
  76.5 4.6 %collective-permute-start.7 = (bf16[2,256,256]{2,1,0:T(8,128)(2,1)S(1)}, bf16[2,256,256]{2,1,0:T(8,128)(2,1)S(1)}, u32[]{:S(2)}, u32[]{:S(2)}) collective-permute-start(bf16[2,256,256]{2,1,0:T(8,128)(2,1)S(1)} %collective-permute-done.6.refs_4_), channel_id=1, source_target_pairs={{0,7},{1,0},{2,1},{3,2},{4,3},{5,4},{6,5},{7,6},{8,15},{9,8},{10,9... | collective-permute-start | bytes 786440 | tf_op jit(solution)/shard_map/ppermute | solution.py:216
  81.1 1.7 %collective-permute-done.3.refs_5_ = bf16[2,256,256]{2,1,0:T(8,128)(2,1)S(1)} collective-permute-done((bf16[2,256,256]{2,1,0:T(8,128)(2,1)S(1)}, bf16[2,256,256]{2,1,0:T(8,128)(2,1)S(1)}, u32[]{:S(2)}, u32[]{:S(2)}) %collective-permute-start.3) | collective-permute-done | bytes 262176 | tf_op jit(solution)/shard_map/ppermute | solution.py:216
  82.8 1.9 %collective-permute-start.4 = (bf16[2,256,256]{2,1,0:T(8,128)(2,1)S(1)}, bf16[2,256,256]{2,1,0:T(8,128)(2,1)S(1)}, u32[]{:S(2)}, u32[]{:S(2)}) collective-permute-start(bf16[2,256,256]{2,1,0:T(8,128)(2,1)S(1)} %collective-permute-done.3.refs_5_), channel_id=1, source_target_pairs={{0,1},{1,2},{2,3},{3,4},{4,5},{5,6},{6,7},{7,0},{8,9},{9,10},{10,1... | collective-permute-start | bytes 786440 | tf_op jit(solution)/shard_map/ppermute | solution.py:216
  84.7 0.1 pad_add_fusion.ids_ref
  84.8 2.2 %copy-done = bf16[4096,512]{1,0:T(8,128)(2,1)S(1)} copy-done((bf16[4096,512]{1,0:T(8,128)(2,1)S(1)}, bf16[4096,512]{1,0:T(8,128)(2,1)}, u32[]{:S(2)}) %copy-start) | copy-done | bytes 4194328
  87.0 2.6 %shard_map.58.sum_ref = f32[4,512,256]{2,1,0:T(8,128)S(1)} custom-call(s32[3]{0:T(128)S(1)} %pad_add_fusion.ids_ref, bf16[8,2,256,512]{3,2,1,0:T(8,128)(2,1)S(1)} %bitcast.6, bf16[2,256,256]{2,1,0:T(8,128)(2,1)S(1)} %all_to_all.26.refs_0_, bf16[2,256,256]{2,1,0:T(8,128)(2,1)S(1)} %collective-permute-done.1.refs_1_, ...), custom_call_target="tpu_custom_call" | custom-call | flops 2147483648 | bytes 8388608 | tf_op jit(solution)/shard_map/pallas_call | solution.py:152
  89.6 2.0 %collective-permute-done.4.piece_ref = bf16[2,256,256]{2,1,0:T(8,128)(2,1)S(1)} collective-permute-done((bf16[2,256,256]{2,1,0:T(8,128)(2,1)S(1)}, bf16[2,256,256]{2,1,0:T(8,128)(2,1)S(1)}, u32[]{:S(2)}, u32[]{:S(2)}) %collective-permute-start.4) | collective-permute-done | bytes 262176 | tf_op jit(solution)/shard_map/ppermute | solution.py:216
  91.6 1.0 shard_map.59
  92.6 12.2 %all_to_all.27.p_ref = bf16[4,512,256]{2,1,0:T(8,128)(2,1)S(1)} all-to-all(bf16[4,512,256]{2,1,0:T(8,128)(2,1)S(1)} %get-tuple-element.12), channel_id=1, replica_groups=mesh['x_hi'=2,'y'=8,'core'=2,'x_lo'=2,'z'=8] {'x_hi','x_lo'}, dimensions={0} | all-to-all | bytes 2097152 | tf_op jit(solution)/shard_map/all_to_all | solution.py:245
  104.8 0.7 shard_map.60
  105.5 15.9 %all_to_all.28.p_ref = bf16[8,64,256]{2,1,0:T(8,128)(2,1)S(1)} all-to-all(bf16[8,64,256]{2,1,0:T(8,128)(2,1)S(1)} %shard_map.60), channel_id=1, replica_groups=mesh['x_hi'=2,'y'=8,'core'=2,'x_lo'=2,'z'=8] {'y'}, dimensions={0} | all-to-all | bytes 524288 | tf_op jit(solution)/shard_map/all_to_all | solution.py:253
  121.5 13.6 %all-gather.1 = f32[128,256]{1,0:T(8,128)S(1)} all-gather(f32[64,256]{1,0:T(8,128)S(1)} %shard_map.61), channel_id=3, replica_groups=mesh['x_hi'=2,'y'=8,'core'=2,'x_lo'=2,'z'=8] {'core'}, dimensions={0}, use_global_device_ids=true | all-gather | bytes 196608 | tf_op jit(solution)/shard_map/all_gather | solution.py:267
  135.1 5.3 %all-gather.2 = f32[128,256]{1,0:T(8,128)S(1)} all-gather(f32[64,256]{1,0:T(8,128)S(1)} %shard_map.62), channel_id=4, replica_groups=mesh['x_hi'=2,'y'=8,'core'=2,'x_lo'=2,'z'=8] {'x_hi'}, dimensions={0}, use_global_device_ids=true | all-gather | bytes 196608 | tf_op jit(solution)/shard_map/all_gather | solution.py:268
  140.4 0.7 shard_map.63
  (15 shorter events, 0.1 us)
Async XLA Ops:
  6.5 15.1 %copy-start.4 = (bf16[256,512]{1,0:T(8,128)(2,1)S(1)}, bf16[256,512]{1,0:T(8,128)(2,1)}, u32[]{:S(2)}) copy-start(bf16[256,512]{1,0:T(8,128)(2,1)} %param.8) | copy-start | bytes 786436
  6.5 26.5 %copy-start.2 = (bf16[64,64]{1,0:T(8,128)(2,1)S(1)}, bf16[64,64]{1,0:T(8,128)(2,1)}, u32[]{:S(2)}) copy-start(bf16[64,64]{1,0:T(8,128)(2,1)} %e_ref.1) | copy-start | bytes 24580
  6.5 41.4 %copy-start.1 = (bf16[4,512,512]{2,1,0:T(8,128)(2,1)S(1)}, bf16[4,512,512]{2,1,0:T(8,128)(2,1)}, u32[]{:S(2)}) copy-start(bf16[4,512,512]{2,1,0:T(8,128)(2,1)} %dy_ref.1) | copy-start | bytes 6291460
  9.7 22.6 %all-to-all-start = ((bf16[16,64,128]{2,1,0:T(8,128)(2,1)}), bf16[16,64,128]{2,1,0:T(8,128)(2,1)S(1)}, u32[]{:S(2)}, u32[]{:S(2)}) async-start(bf16[16,64,128]{2,1,0:T(8,128)(2,1)} %shard_map.55), calls=%async_computation | async-start | bytes 524288 | tf_op jit(solution)/shard_map/all_to_all | solution.py:229
  21.6 63.2 %all-gather.5.cloned.1.call-start = ((), (), s32[]{:S(2)}) async-start(), calls=%async_computation.5 | async-start | bytes 4456448 | tf_op jit(solution)/shard_map/all_gather | solution.py:231
  21.6 10.6 %collective-permute-start = (bf16[256,512]{1,0:T(8,128)(2,1)S(1)}, bf16[256,512]{1,0:T(8,128)(2,1)S(1)}, u32[]{:S(2)}, u32[]{:S(2)}) collective-permute-start(bf16[256,512]{1,0:T(8,128)(2,1)S(1)} %copy-done.4), channel_id=1, source_target_pairs={{0,0},{8,16},{16,256},{24,272},{256,8},{264,24},{272,264},{280,280... | collective-permute-start | bytes 786440 | tf_op jit(solution)/shard_map/ppermute | solution.py:227
  32.3 0.7 copy-start.3
  57.4 8.7 %collective-permute-start.1 = (bf16[2,256,256]{2,1,0:T(8,128)(2,1)S(1)}, bf16[2,256,256]{2,1,0:T(8,128)(2,1)S(1)}, u32[]{:S(2)}, u32[]{:S(2)}) collective-permute-start(bf16[2,256,256]{2,1,0:T(8,128)(2,1)S(1)} %all_to_all.26.refs_0_), channel_id=1, source_target_pairs={{0,1},{1,2},{2,3},{3,4},{4,5},{5,6},{6,7},{7,0},{8,9},{9,10},{10,1... | collective-permute-start | bytes 786440 | tf_op jit(solution)/shard_map/ppermute | solution.py:216
  61.5 7.5 %collective-permute-start.5 = (bf16[2,256,256]{2,1,0:T(8,128)(2,1)S(1)}, bf16[2,256,256]{2,1,0:T(8,128)(2,1)S(1)}, u32[]{:S(2)}, u32[]{:S(2)}) collective-permute-start(bf16[2,256,256]{2,1,0:T(8,128)(2,1)S(1)} %all_to_all.26.refs_0_), channel_id=1, source_target_pairs={{0,7},{1,0},{2,1},{3,2},{4,3},{5,4},{6,5},{7,6},{8,15},{9,8},{10,9... | collective-permute-start | bytes 786440 | tf_op jit(solution)/shard_map/ppermute | solution.py:216
  66.2 8.3 %collective-permute-start.2 = (bf16[2,256,256]{2,1,0:T(8,128)(2,1)S(1)}, bf16[2,256,256]{2,1,0:T(8,128)(2,1)S(1)}, u32[]{:S(2)}, u32[]{:S(2)}) collective-permute-start(bf16[2,256,256]{2,1,0:T(8,128)(2,1)S(1)} %collective-permute-done.1.refs_1_), channel_id=1, source_target_pairs={{0,1},{1,2},{2,3},{3,4},{4,5},{5,6},{6,7},{7,0},{8,9},{9,10},{10,1... | collective-permute-start | bytes 786440 | tf_op jit(solution)/shard_map/ppermute | solution.py:216
  69.0 7.5 %collective-permute-start.6 = (bf16[2,256,256]{2,1,0:T(8,128)(2,1)S(1)}, bf16[2,256,256]{2,1,0:T(8,128)(2,1)S(1)}, u32[]{:S(2)}, u32[]{:S(2)}) collective-permute-start(bf16[2,256,256]{2,1,0:T(8,128)(2,1)S(1)} %collective-permute-done.5.refs_2_), channel_id=1, source_target_pairs={{0,7},{1,0},{2,1},{3,2},{4,3},{5,4},{6,5},{7,6},{8,15},{9,8},{10,9... | collective-permute-start | bytes 786440 | tf_op jit(solution)/shard_map/ppermute | solution.py:216
  74.5 8.3 %collective-permute-start.3 = (bf16[2,256,256]{2,1,0:T(8,128)(2,1)S(1)}, bf16[2,256,256]{2,1,0:T(8,128)(2,1)S(1)}, u32[]{:S(2)}, u32[]{:S(2)}) collective-permute-start(bf16[2,256,256]{2,1,0:T(8,128)(2,1)S(1)} %collective-permute-done.2.refs_3_), channel_id=1, source_target_pairs={{0,1},{1,2},{2,3},{3,4},{4,5},{5,6},{6,7},{7,0},{8,9},{9,10},{10,1... | collective-permute-start | bytes 786440 | tf_op jit(solution)/shard_map/ppermute | solution.py:216
  76.5 8.3 %collective-permute-start.7 = (bf16[2,256,256]{2,1,0:T(8,128)(2,1)S(1)}, bf16[2,256,256]{2,1,0:T(8,128)(2,1)S(1)}, u32[]{:S(2)}, u32[]{:S(2)}) collective-permute-start(bf16[2,256,256]{2,1,0:T(8,128)(2,1)S(1)} %collective-permute-done.6.refs_4_), channel_id=1, source_target_pairs={{0,7},{1,0},{2,1},{3,2},{4,3},{5,4},{6,5},{7,6},{8,15},{9,8},{10,9... | collective-permute-start | bytes 786440 | tf_op jit(solution)/shard_map/ppermute | solution.py:216
  82.8 8.8 %collective-permute-start.4 = (bf16[2,256,256]{2,1,0:T(8,128)(2,1)S(1)}, bf16[2,256,256]{2,1,0:T(8,128)(2,1)S(1)}, u32[]{:S(2)}, u32[]{:S(2)}) collective-permute-start(bf16[2,256,256]{2,1,0:T(8,128)(2,1)S(1)} %collective-permute-done.3.refs_5_), channel_id=1, source_target_pairs={{0,1},{1,2},{2,3},{3,4},{4,5},{5,6},{6,7},{7,0},{8,9},{9,10},{10,1... | collective-permute-start | bytes 786440 | tf_op jit(solution)/shard_map/ppermute | solution.py:216
  84.8 2.2 %copy-start = (bf16[4096,512]{1,0:T(8,128)(2,1)S(1)}, bf16[4096,512]{1,0:T(8,128)(2,1)}, u32[]{:S(2)}) copy-start(bf16[4096,512]{1,0:T(8,128)(2,1)} %all-gather.5.cloned.1.call-done) | copy-start | bytes 12582916
Sparse Core Ops, SparseCore 0:
  33.1 45.5 all-gather.4
